TPU v7x, 32 devices: a whole 2x2x4 slice. The times are simulated.
32 devices in a mesh: img: 16 (over z, x, core), band: 2 (over y).
Axes of the slice: x: 2, y: 2, z: 4, core: 2. Of those that a mesh axis runs over, the one named last changes fastest.
Arguments:
- tokens: bfloat16 [128, 32, 32, 384], P('img', 'band'), may hold values from -6 to 6
- cotangent: bfloat16 [128, 32, 32, 384], P('img', 'band'), may hold values from -6 to 6
- valid_mask: int32 [128, 32, 32], P('img'), may hold values from 0 to 1, as said below
- timesteps: int32 [128], P('img'), may hold values from 0 to 999
- index_table: int32 [567], replicated, may hold values from 0 to 566, each once
- first_gain: float32 [2, 384], replicated, may hold values from 0.5 to 1.5
- first_shift: float32 [2, 384], replicated, may hold values from -1.25 to 1.25
- attend_weight: bfloat16 [2, 384, 1152], replicated, may hold values from -0.3125 to 0.3125
- time_weight: bfloat16 [2, 384, 768], replicated, may hold values from -0.078125 to 0.078125
- offset_bias: float32 [2, 6, 567], replicated, may hold values from -6 to 6
- output_weight: bfloat16 [2, 384, 384], replicated, may hold values from -1.75 to 1.75
- output_bias: float32 [2, 384], replicated, may hold values from -1.75 to 1.75
- second_gain: float32 [2, 384], replicated, may hold values from 0.5 to 1.5
- second_shift: float32 [2, 384], replicated, may hold values from -1.25 to 1.25
- expand_weight: bfloat16 [2, 384, 1536], replicated, may hold values from -0.3125 to 0.3125
- expand_bias: float32 [2, 1536], replicated, may hold values from -3 to 3
- reduce_weight: bfloat16 [2, 1536, 384], replicated, may hold values from -0.15625 to 0.15625
- reduce_bias: float32 [2, 384], replicated, may hold values from -1.75 to 1.75
Outputs:
- output: bfloat16 [128, 32, 32, 384], P('img', 'band')
- input_grad: bfloat16 [128, 32, 32, 384], P('img', 'band')
- grad_first_gain: float32 [2, 384], replicated
- grad_first_shift: float32 [2, 384], replicated
- grad_attend_weight: float32 [2, 384, 1152], replicated
- grad_time_weight: float32 [2, 384, 768], replicated
- grad_offset_bias: float32 [2, 6, 567], replicated
- grad_output_weight: float32 [2, 384, 384], replicated
- grad_output_bias: float32 [2, 384], replicated
- grad_second_gain: float32 [2, 384], replicated
- grad_second_shift: float32 [2, 384], replicated
- grad_expand_weight: float32 [2, 384, 1536], replicated
- grad_expand_bias: float32 [2, 1536], replicated
- grad_reduce_weight: float32 [2, 1536, 384], replicated
- grad_reduce_bias: float32 [2, 384], replicated
Inputs may be any that keep to these rules, and one draw needn't show every extreme that they name: `valid_mask`: an image's valid patches are its first h rows and first w columns, h and w at least a quarter of 32 and 32; among the 8 images of each index of img, one has all 32 rows valid.
All inputs are finite; a program needn't handle non-finite values.
Results may differ from a plain program's by a relative error of at most 0.015.
Values may be sent and summed in bfloat16 or wider, within the bound.
A program may use at most 640 MiB of HBM per device.

v0:
```python
import math

import jax
import jax.numpy as jnp
from jax import lax
from jax.sharding import PartitionSpec as P

WIN = 4


EXACT = lax.Precision.HIGHEST
NEG_FILL = -1000000000.0
EPSILON = 1e-06


def padded(block, sides, width):
    for axis, dim in sides:
        count = lax.axis_size(axis)
        forward = [(i, i + 1) for i in range(count - 1)]
        backward = [(target, source) for source, target in forward]
        low = lax.ppermute(
            lax.slice_in_dim(block, block.shape[dim] - width, None, axis=dim), axis, forward
        )
        high = lax.ppermute(lax.slice_in_dim(block, 0, width, axis=dim), axis, backward)
        block = jnp.concatenate([low, block, high], axis=dim)
    return block


def shifted(shard, axis, by):
    count = lax.axis_size(axis)
    pairs = [(i, i + by) for i in range(count) if 0 <= i + by < count]
    return lax.ppermute(shard, axis, pairs)


def time_embedding(timesteps, width):
    half_width = width // 2
    frequency = jnp.exp(
        jnp.arange(half_width, dtype=jnp.int32).astype(jnp.float32)
        * (-math.log(10000.0) / half_width)
    )
    angles = timesteps.astype(jnp.float32)[:, None] * frequency[None, :]
    return jnp.concatenate([jnp.sin(angles), jnp.cos(angles)], axis=-1)


def normalize(values):
    mean_value = jnp.mean(values, axis=-1, keepdims=True)
    centered = values - mean_value
    inverse = lax.rsqrt(jnp.mean(centered * centered, axis=-1, keepdims=True) + EPSILON)
    return (centered * inverse, inverse)


def normalize_back(grad_normed, scaled, inverse, gain):
    grad_scaled = grad_normed * gain
    return inverse * (
        grad_scaled
        - jnp.mean(grad_scaled, axis=-1, keepdims=True)
        - scaled * jnp.mean(grad_scaled * scaled, axis=-1, keepdims=True)
    )


def smooth_gate(values):
    return jax.nn.gelu(values, approximate=True)


def column_table(grid_cols):
    col_diff = (
        jnp.arange(grid_cols, dtype=jnp.int32)[None, :]
        - jnp.arange(grid_cols, dtype=jnp.int32)[:, None]
        + grid_cols
        - 1
    )
    return (
        col_diff[:, :, None] == jnp.arange(2 * grid_cols - 1, dtype=jnp.int32)[None, None, :]
    ).astype(jnp.float32)


def position_bias(table, index_table, col_pick, band_rows, key_rows):
    entries = index_table.shape[0]
    span = 2 * WIN + 1
    select = (index_table[:, None] == jnp.arange(entries, dtype=jnp.int32)[None, :]).astype(
        jnp.float32
    )
    per_offset = jnp.dot(table, select.T, precision=EXACT)
    per_offset = per_offset.reshape(table.shape[0], span, col_pick.shape[2])
    column_mixed = jnp.einsum("hab,ctb->hcat", per_offset, col_pick, precision=EXACT)
    placed = [
        jnp.pad(column_mixed, ((0, 0), (0, 0), (row, key_rows - row - span), (0, 0)))
        for row in range(band_rows)
    ]
    expanded = jnp.stack(placed, axis=1)
    grid_cols = col_pick.shape[0]
    return expanded.reshape(table.shape[0], band_rows * grid_cols, key_rows * grid_cols)


def body(
    tokens,
    cotangent,
    valid_mask,
    timesteps,
    index_table,
    first_gain,
    first_shift,
    attend_weight,
    time_weight,
    offset_bias,
    output_weight,
    output_bias,
    second_gain,
    second_shift,
    expand_weight,
    expand_bias,
    reduce_weight,
    reduce_bias,
):
    image_count, band_rows, grid_cols, model_width = tokens.shape
    head_count = offset_bias.shape[1]
    head_size = model_width // head_count
    score_scale = head_size ** (-0.5)
    layer_count = attend_weight.shape[0]
    key_rows = band_rows + 2 * WIN
    query_count = band_rows * grid_cols
    key_count = key_rows * grid_cols
    row_start = lax.axis_index("band") * band_rows
    query_row = row_start + jnp.arange(band_rows, dtype=jnp.int32)
    key_row = row_start - WIN + jnp.arange(key_rows, dtype=jnp.int32)
    in_window = jnp.abs(key_row[None, :] - query_row[:, None]) <= WIN
    same_row = key_row[None, :] == query_row[:, None]
    col_index = jnp.arange(grid_cols, dtype=jnp.int32)
    same_col = col_index[:, None] == col_index[None, :]
    padded_valid = jnp.pad(valid_mask, ((0, 0), (WIN, WIN), (0, 0)))
    key_valid = lax.dynamic_slice_in_dim(padded_valid, row_start, key_rows, 1) == 1
    allowed = in_window[None, :, None, :, None] & (
        key_valid[:, None, None, :, :]
        | same_row[None, :, None, :, None] & same_col[None, None, :, None, :]
    )
    allowed = allowed.reshape(image_count, 1, query_count, key_count)
    col_pick = column_table(grid_cols)

    def make_bias(table):
        return position_bias(table, index_table, col_pick, band_rows, key_rows)

    biases = [make_bias(offset_bias[layer_index]) for layer_index in range(layer_count)]
    time_low = time_embedding(timesteps, model_width).astype(jnp.bfloat16)
    time_wide = time_low.astype(jnp.float32)

    def forward_layer(residual, layer_index):
        scaled_one, inverse_one = normalize(residual)
        normed_one = (scaled_one * first_gain[layer_index] + first_shift[layer_index]).astype(
            jnp.bfloat16
        )
        time_proj = jnp.dot(time_low, time_weight[layer_index], preferred_element_type=jnp.float32)
        time_value = jnp.pad(time_proj[:, model_width:], ((0, 0), (model_width, 0)))[
            :, None, None, :
        ]
        weights_now = attend_weight[layer_index]
        queries = (
            jnp.dot(normed_one, weights_now[:, :model_width], preferred_element_type=jnp.float32)
            + time_proj[:, None, :model_width]
        ).astype(jnp.bfloat16)
        grid_normed = normed_one.reshape(image_count, band_rows, grid_cols, model_width)
        pairs = (
            jnp.dot(grid_normed, weights_now[:, model_width:], preferred_element_type=jnp.float32)
            + time_value
        )
        padded_pairs = padded(pairs.astype(jnp.bfloat16), (("band", 1),), WIN)
        query_heads = queries.reshape(image_count, query_count, head_count, head_size)
        key_heads = padded_pairs[..., :model_width].reshape(
            image_count, key_count, head_count, head_size
        )
        value_heads = padded_pairs[..., model_width:].reshape(
            image_count, key_count, head_count, head_size
        )
        scores = (
            jnp.einsum(
                "bnhe,bkhe->bhnk", query_heads, key_heads, preferred_element_type=jnp.float32
            )
            * score_scale
            + biases[layer_index][None]
        )
        scores = jnp.where(allowed, scores, NEG_FILL)
        row_max = jnp.max(scores, axis=-1, keepdims=True)
        exp_terms = jnp.exp(scores - row_max)
        attention = exp_terms / jnp.sum(exp_terms, axis=-1, keepdims=True)
        attention_low = attention.astype(jnp.bfloat16)
        attended = jnp.einsum(
            "bhnk,bkhe->bnhe", attention_low, value_heads, preferred_element_type=jnp.float32
        )
        attended = attended.astype(jnp.bfloat16).reshape(image_count, query_count, model_width)
        branch = (
            jnp.dot(attended, output_weight[layer_index], preferred_element_type=jnp.float32)
            + output_bias[layer_index]
        )
        middle = residual + branch
        scaled_two, inverse_two = normalize(middle)
        normed_two = (scaled_two * second_gain[layer_index] + second_shift[layer_index]).astype(
            jnp.bfloat16
        )
        hidden = (
            jnp.dot(normed_two, expand_weight[layer_index], preferred_element_type=jnp.float32)
            + expand_bias[layer_index]
        )
        active = smooth_gate(hidden).astype(jnp.bfloat16)
        result = middle + (
            jnp.dot(active, reduce_weight[layer_index], preferred_element_type=jnp.float32)
            + reduce_bias[layer_index]
        )
        kept = (
            scaled_one,
            inverse_one,
            normed_one,
            query_heads,
            key_heads,
            value_heads,
            attention,
            attention_low,
            attended,
            scaled_two,
            inverse_two,
            normed_two,
            hidden,
            active,
        )
        return (result, kept)

    residual = tokens.reshape(image_count, query_count, model_width).astype(jnp.float32)
    layer_inputs = []
    for layer_index in range(layer_count):
        layer_inputs.append(residual)
        residual, unused = forward_layer(residual, layer_index)
    output = residual.astype(jnp.bfloat16).reshape(tokens.shape)
    grad_residual = cotangent.reshape(image_count, query_count, model_width).astype(jnp.float32)
    per_layer = [None] * layer_count
    for layer_index in reversed(range(layer_count)):
        backward_residual = layer_inputs[layer_index]
        backward_unused, backward_kept = forward_layer(backward_residual, layer_index)
        (
            backward_scaled_one,
            backward_inverse_one,
            backward_normed_one,
            backward_query_heads,
            backward_key_heads,
            backward_value_heads,
            backward_attention,
            backward_attention_low,
            backward_attended,
            backward_scaled_two,
            backward_inverse_two,
            backward_normed_two,
            backward_hidden,
            backward_active,
        ) = backward_kept
        grad_low = grad_residual.astype(jnp.bfloat16)
        grad_reduce_bias = jnp.sum(grad_low, axis=(0, 1), dtype=jnp.float32)
        grad_reduce = jnp.einsum(
            "bnf,bnd->fd", backward_active, grad_low, preferred_element_type=jnp.float32
        )
        grad_active = jnp.einsum(
            "bnd,fd->bnf", grad_low, reduce_weight[layer_index], preferred_element_type=jnp.float32
        )
        grad_hidden = jax.vjp(smooth_gate, backward_hidden)[1](grad_active)[0].astype(jnp.bfloat16)
        grad_expand_bias = jnp.sum(grad_hidden, axis=(0, 1), dtype=jnp.float32)
        grad_expand = jnp.einsum(
            "bnd,bnf->df", backward_normed_two, grad_hidden, preferred_element_type=jnp.float32
        )
        grad_normed_two = jnp.einsum(
            "bnf,df->bnd",
            grad_hidden,
            expand_weight[layer_index],
            preferred_element_type=jnp.float32,
        )
        grad_second_gain = jnp.sum(grad_normed_two * backward_scaled_two, axis=(0, 1))
        grad_second_shift = jnp.sum(grad_normed_two, axis=(0, 1))
        grad_middle = grad_residual + normalize_back(
            grad_normed_two, backward_scaled_two, backward_inverse_two, second_gain[layer_index]
        )
        grad_branch = grad_middle.astype(jnp.bfloat16)
        grad_output_bias = jnp.sum(grad_branch, axis=(0, 1), dtype=jnp.float32)
        grad_output = jnp.einsum(
            "bnd,bne->de", backward_attended, grad_branch, preferred_element_type=jnp.float32
        )
        grad_attended = jnp.einsum(
            "bne,de->bnd",
            grad_branch,
            output_weight[layer_index],
            preferred_element_type=jnp.float32,
        )
        grad_attended = grad_attended.astype(jnp.bfloat16).reshape(
            image_count, query_count, head_count, head_size
        )
        grad_attention = jnp.einsum(
            "bnhe,bkhe->bhnk",
            grad_attended,
            backward_value_heads,
            preferred_element_type=jnp.float32,
        )
        row_dot = jnp.sum(backward_attention * grad_attention, axis=-1, keepdims=True)
        grad_scores = (backward_attention * (grad_attention - row_dot)).astype(jnp.bfloat16)
        unused_bias, bias_pull = jax.vjp(make_bias, offset_bias[layer_index])
        grad_offset = bias_pull(jnp.sum(grad_scores, axis=0, dtype=jnp.float32))[0]
        grad_queries = (
            (
                jnp.einsum(
                    "bhnk,bkhe->bnhe",
                    grad_scores,
                    backward_key_heads,
                    preferred_element_type=jnp.float32,
                )
                * score_scale
            )
            .astype(jnp.bfloat16)
            .reshape(image_count, query_count, model_width)
        )
        grad_keys = (
            jnp.einsum(
                "bhnk,bnhe->bkhe",
                grad_scores,
                backward_query_heads,
                preferred_element_type=jnp.float32,
            )
            * score_scale
        )
        grad_values = jnp.einsum(
            "bhnk,bnhe->bkhe",
            backward_attention_low,
            grad_attended,
            preferred_element_type=jnp.float32,
        )
        grad_pairs = jnp.concatenate(
            [
                grad_keys.reshape(image_count, key_rows, grid_cols, model_width),
                grad_values.reshape(image_count, key_rows, grid_cols, model_width),
            ],
            axis=-1,
        )
        upper_part = grad_pairs[:, :WIN]
        lower_part = grad_pairs[:, WIN + band_rows :]
        from_below = shifted(upper_part.astype(jnp.bfloat16), "band", -1).astype(upper_part.dtype)
        from_above = shifted(lower_part.astype(jnp.bfloat16), "band", 1).astype(lower_part.dtype)
        own_rows = grad_pairs[:, WIN : WIN + band_rows]
        own_rows = own_rows + jnp.pad(from_above, ((0, 0), (0, band_rows - WIN), (0, 0), (0, 0)))
        own_rows = own_rows + jnp.pad(from_below, ((0, 0), (band_rows - WIN, 0), (0, 0), (0, 0)))
        pairs_low = own_rows.astype(jnp.bfloat16).reshape(image_count, query_count, 2 * model_width)
        grad_time_proj = jnp.concatenate(
            [
                jnp.sum(grad_queries, axis=1, dtype=jnp.float32),
                jnp.sum(pairs_low[..., model_width:], axis=1, dtype=jnp.float32),
            ],
            axis=-1,
        )
        grad_time = jnp.sum(time_wide[:, :, None] * grad_time_proj[:, None, :], axis=0)
        combined = jnp.concatenate([grad_queries, pairs_low], axis=-1)
        grad_attend = jnp.einsum(
            "bnd,bne->de", backward_normed_one, combined, preferred_element_type=jnp.float32
        )
        grad_normed_one = jnp.einsum(
            "bne,de->bnd", combined, attend_weight[layer_index], preferred_element_type=jnp.float32
        )
        grad_first_gain = jnp.sum(grad_normed_one * backward_scaled_one, axis=(0, 1))
        grad_first_shift = jnp.sum(grad_normed_one, axis=(0, 1))
        grad_input = grad_middle + normalize_back(
            grad_normed_one, backward_scaled_one, backward_inverse_one, first_gain[layer_index]
        )
        grad_residual, per_layer[layer_index] = (
            grad_input,
            (
                grad_first_gain,
                grad_first_shift,
                grad_attend,
                grad_time,
                grad_offset,
                grad_output,
                grad_output_bias,
                grad_second_gain,
                grad_second_shift,
                grad_expand,
                grad_expand_bias,
                grad_reduce,
                grad_reduce_bias,
            ),
        )
    input_grad = grad_residual.astype(jnp.bfloat16).reshape(tokens.shape)
    stacked = tuple(
        (
            jnp.stack([per_layer[layer_index][member] for layer_index in range(layer_count)])
            for member in range(13)
        )
    )
    summed = tuple(lax.psum(stacked, ("img", "band")))
    return (output, input_grad) + summed


def solution(mesh):
    placed = (
        P("img", "band", None, None),
        P("img", "band", None, None),
        P("img", None, None),
        P("img"),
        P(),
        P(),
        P(),
        P(),
        P(),
        P(),
        P(),
        P(),
        P(),
        P(),
        P(),
        P(),
        P(),
        P(),
    )
    return jax.shard_map(
        body,
        mesh=mesh,
        in_specs=placed,
        out_specs=(
            P("img", "band", None, None),
            P("img", "band", None, None),
            P(),
            P(),
            P(),
            P(),
            P(),
            P(),
            P(),
            P(),
            P(),
            P(),
            P(),
            P(),
            P(),
        ),
        check_vma=False,
    )
```

profile of v0, /device:TPU:0, one launch (start us, length us, event | category | flops | bytes accessed | tf_op | source)
XLA Modules:
  0.0 1701.6 jit_solution(9021139611309728021)
XLA Ops:
  85.1 28.4 %reshape.471 = f32[6,512,768]{2,0,1:T(8,128)} reshape(f32[6,16,32,24,32]{4,3,0,2,1:T(8,128)} %bitcast_dynamic-update-slice_fusion.16) | data formatting | bytes 18874368 | tf_op jit(solution)/shard_map/add | solution.py:174
  213.0 40.6 %fusion.185 = (f32[8,6,512]{2,1,0:T(8,128)S(1)}, f32[8,6,512,768]{3,2,1,0:T(8,128)}) fusion(f32[6,512,768]{2,1,0:T(8,128)} %copy.192, pred[8,512,768]{2,1,0:T(8,128)(4,1)S(1)} %copy-done.15, bf16[8,512,6,64]{1,3,2,0:T(8,128)(2,1)} %bitcast.503, bf16[8,768,6,64]{1,3,2,0:T(8,128)(2,1)} %copy.118), kind=kOutput, calls=%fused_computation.412 | convolution fusion | flops 2510291712 | bytes 96043008 | tf_op jit(solution)/shard_map/sub | solution.py:182
  253.6 27.4 %fusion.78 = bf16[8,6,64,512]{3,2,1,0:T(8,128)(2,1)S(1)} fusion(bf16[8,768,6,64]{1,3,2,0:T(8,128)(2,1)} %copy.121, f32[8,6,512,768]{3,2,1,0:T(8,128)} %get-tuple-element.172, f32[8,6,512]{2,1,0:T(8,128)S(1)} %get-tuple-element.171), kind=kOutput, calls=%fused_computation.218 | convolution fusion | flops 2455240704 | bytes 83460096 | tf_op jit(solution)/shard_map/bhnk,bkhe->bnhe/dot_general | solution.py:185
  342.9 28.4 %reshape.473 = f32[6,512,768]{2,0,1:T(8,128)} reshape(f32[6,16,32,24,32]{4,3,0,2,1:T(8,128)} %bitcast_dynamic-update-slice_fusion) | data formatting | bytes 18874368 | tf_op jit(solution)/shard_map/add | solution.py:174
  452.2 42.3 %fusion.188 = (f32[8,6,512]{2,1,0:T(8,128)S(1)}, f32[8,6,512,768]{3,2,1,0:T(8,128)}) fusion(f32[6,512,768]{2,1,0:T(8,128)} %copy.194, pred[8,512,768]{2,1,0:T(8,128)(4,1)} %or_and_fusion, bf16[8,512,6,64]{1,3,2,0:T(8,128)(2,1)} %bitcast.505, bf16[8,768,6,64]{1,3,2,0:T(8,128)(2,1)} %copy.124), kind=kOutput, calls=%fused_computation.415 | convolution fusion | flops 2510291712 | bytes 96043008 | tf_op jit(solution)/shard_map/sub | solution.py:182
  494.5 27.6 %fusion.81 = bf16[8,6,64,512]{3,2,1,0:T(8,128)(2,1)S(1)} fusion(bf16[8,768,6,64]{1,3,2,0:T(8,128)(2,1)} %copy.127, f32[8,6,512,768]{3,2,1,0:T(8,128)} %get-tuple-element.180, f32[8,6,512]{2,1,0:T(8,128)S(1)} %get-tuple-element.179), kind=kOutput, calls=%fused_computation.219 | convolution fusion | flops 2455240704 | bytes 83460096 | tf_op jit(solution)/shard_map/bhnk,bkhe->bnhe/dot_general | solution.py:185
  544.7 24.9 %convert_reduce_fusion.2 = (f32[1536]{0:T(1024)}, bf16[8,512,1536]{2,1,0:T(8,128)(2,1)}) fusion(f32[8,512,1536]{2,1,0:T(8,128)} %get-tuple-element.184, f32[1536]{0:T(1024)S(1)} %copy-done.104, bf16[8,512,384]{2,1,0:T(8,128)(2,1)S(1)} %bitcast.487, bf16[2,1536,384]{2,1,0:T(8,128)(2,1)S(1)} %copy-done.136), kind=kOutput, calls=%fused_computation.42 | convolution fusion | flops 4976540160 | bytes 42088448 | tf_op jit(solution)/shard_map/bnd,fd->bnf/dot_general | solution.py:257
  589.7 28.9 %fusion.68 = f32[8,768,6,64]{1,3,2,0:T(8,128)} fusion(bf16[8,512,6,64]{1,3,2,0:T(8,128)(2,1)S(1)} %bitcast.518, f32[8,6,512,768]{3,2,1,0:T(8,128)} %get-tuple-element.180, f32[8,6,512]{2,1,0:T(8,128)S(1)} %get-tuple-element.179), kind=kOutput, calls=%fused_computation.141 | convolution fusion | flops 2453667840 | bytes 88178688 | tf_op jit(solution)/shard_map/bhnk,bnhe->bkhe/dot_general | solution.py:322
  618.7 50.0 %multiply_reduce_fusion.1 = (f32[8,6,512]{2,1,0:T(8,128)S(1)}, f32[8,6,512,768]{3,2,1,0:T(8,128)}) fusion(f32[8,6,512,768]{3,2,1,0:T(8,128)} %get-tuple-element.180, f32[8,6,512]{2,1,0:T(8,128)S(1)} %get-tuple-element.179, bf16[8,512,6,64]{1,3,2,0:T(8,128)(2,1)S(1)} %bitcast.519, bf16[8,768,6,64]{1,3,2,0:T(8,128)(2,1)} %copy.127), kind=kOutput, calls=%fused_computation.7 | convolution fusion | flops 2472517632 | bytes 159055872 | tf_op jit(solution)/shard_map/bnhe,bkhe->bhnk/dot_general | solution.py:290
  668.7 66.0 %convert_reduce_fusion = (f32[6,512,768]{2,1,0:T(8,128)}, bf16[8,6,512,768]{3,2,1,0:T(8,128)(2,1)}) fusion(f32[8,6,512,768]{3,2,1,0:T(8,128)} %get-tuple-element.187, f32[8,6,512]{2,1,0:T(8,128)S(1)} %get-tuple-element.186, f32[8,6,512,768]{3,2,1,0:T(8,128)} %get-tuple-element.180, f32[8,6,512]{2,1,0:T(8,128)S(1)} %get-tuple-element.179), kind=kLoop, calls=%fused_computation.2 | loop fusion | flops 110886912 | bytes 198377472 | tf_op jit(solution)/shard_map/reduce_sum | solution.py:299
  734.6 19.8 %convert_reduce_fusion.10 = (f32[8,6,64]{2,1,0:T(8,128)S(1)}, bf16[8,6,64,512]{3,2,1,0:T(8,128)(2,1)}) fusion(bf16[8,768,6,64]{1,3,2,0:T(8,128)(2,1)} %copy.124, bf16[8,6,512,768]{3,2,1,0:T(8,128)(2,1)} %get-tuple-element.114), kind=kOutput, calls=%fused_computation.103 | convolution fusion | flops 2422207488 | bytes 45625344 | tf_op jit(solution)/shard_map/bhnk,bkhe->bnhe/dot_general | solution.py:302
  754.4 20.1 %multiply_bitcast_fusion.1 = f32[8,768,6,64]{1,3,2,0:T(8,128)} fusion(bf16[8,512,6,64]{1,3,2,0:T(8,128)(2,1)} %bitcast.506, bf16[8,6,512,768]{3,2,1,0:T(8,128)(2,1)} %get-tuple-element.114), kind=kOutput, calls=%fused_computation.70 | convolution fusion | flops 2418278400 | bytes 50331648 | tf_op jit(solution)/shard_map/bhnk,bnhe->bkhe/dot_general | solution.py:314
  785.4 16.6 copy.132
  802.0 19.6 %reshape.432 = f32[8,24,32,384]{3,2,1,0:T(8,128)} reshape(f32[8,768,6,64]{3,2,1,0:T(8,128)} %copy.132) | data formatting | bytes 18874368 | tf_op jit(solution)/shard_map/reshape | solution.py:331
  825.1 16.6 copy.131
  841.6 19.4 %reshape.431 = f32[8,24,32,384]{3,2,1,0:T(8,128)} reshape(f32[8,768,6,64]{3,2,1,0:T(8,128)} %copy.131) | data formatting | bytes 18874368 | tf_op jit(solution)/shard_map/reshape | solution.py:330
  887.8 24.0 %reshape.442 = f32[6,16,32,24,32]{4,3,2,1,0:T(8,128)} reshape(f32[6,512,768]{2,1,0:T(8,128)} %get-tuple-element.113) | data formatting | bytes 18874368 | tf_op jit(solution)/shard_map/transpose(jvp())/reshape | solution.py:92
  911.8 23.6 %slice_bitcast_fusion.15 = (f32[6,32,24,32]{3,2,1,0:T(8,128)S(1)}, f32[6,32,24,32]{3,2,1,0:T(8,128)S(1)}, f32[6,32,24,32]{3,2,1,0:T(8,128)}, f32[6,32,24,32]{3,2...) fusion(f32[6,16,32,24,32]{4,3,2,1,0:T(8,128)} %reshape.442), kind=kLoop, calls=%fused_computation.168 | loop fusion | bytes 18874368 | tf_op jit(solution)/shard_map/transpose(jvp())/unstack | solution.py:90
  1005.3 27.4 %convert_reduce_fusion.3 = (f32[1536]{0:T(1024)}, bf16[8,512,1536]{2,1,0:T(8,128)(2,1)}) fusion(f32[8,512,1536]{2,1,0:T(8,128)} %get-tuple-element.176, f32[1536]{0:T(1024)S(1)} %copy-done.103, bf16[2,1536,384]{2,1,0:T(8,128)(2,1)S(1)} %copy-done.137, f32[8,512,384]{2,1,0:T(8,128)} %copy-done.17), kind=kOutput, calls=%fused_computation.43 | convolution fusion | flops 4978113024 | bytes 45234176 | tf_op jit(solution)/shard_map/bnd,fd->bnf/dot_general | solution.py:257
  1068.3 29.3 %fusion.65 = f32[8,768,6,64]{1,3,2,0:T(8,128)} fusion(bf16[8,512,6,64]{1,3,2,0:T(8,128)(2,1)S(1)} %bitcast.521, f32[8,6,512,768]{3,2,1,0:T(8,128)} %get-tuple-element.172, f32[8,6,512]{2,1,0:T(8,128)S(1)} %copy-done.51), kind=kOutput, calls=%fused_computation.140 | convolution fusion | flops 2453667840 | bytes 88178688 | tf_op jit(solution)/shard_map/bhnk,bnhe->bkhe/dot_general | solution.py:322
  1097.5 50.0 %multiply_reduce_fusion = (f32[8,6,512]{2,1,0:T(8,128)S(1)}, f32[8,6,512,768]{3,2,1,0:T(8,128)}) fusion(f32[8,6,512,768]{3,2,1,0:T(8,128)} %get-tuple-element.172, f32[8,6,512]{2,1,0:T(8,128)S(1)} %copy-done.51, bf16[8,512,6,64]{1,3,2,0:T(8,128)(2,1)S(1)} %bitcast.522, bf16[8,768,6,64]{1,3,2,0:T(8,128)(2,1)} %copy.121), kind=kOutput, calls=%fused_computation.5 | convolution fusion | flops 2472517632 | bytes 159055872 | tf_op jit(solution)/shard_map/bnhe,bkhe->bhnk/dot_general | solution.py:290
  1147.6 66.1 %convert_reduce_fusion.1 = (f32[6,512,768]{2,1,0:T(8,128)}, bf16[8,6,512,768]{3,2,1,0:T(8,128)(2,1)}) fusion(f32[8,6,512,768]{3,2,1,0:T(8,128)} %get-tuple-element.191, f32[8,6,512]{2,1,0:T(8,128)S(1)} %get-tuple-element.190, f32[8,6,512,768]{3,2,1,0:T(8,128)} %get-tuple-element.172, f32[8,6,512]{2,1,0:T(8,128)S(1)} %copy-done.51), kind=kLoop, calls=%fused_computation.3 | loop fusion | flops 110886912 | bytes 198377472 | tf_op jit(solution)/shard_map/reduce_sum | solution.py:299
  1213.7 18.2 %convert_reduce_fusion.12 = (f32[8,6,64]{2,1,0:T(8,128)S(1)}, bf16[8,6,64,512]{3,2,1,0:T(8,128)(2,1)S(1)}) fusion(bf16[8,768,6,64]{1,3,2,0:T(8,128)(2,1)} %copy.118, bf16[8,6,512,768]{3,2,1,0:T(8,128)(2,1)} %get-tuple-element.112), kind=kOutput, calls=%fused_computation.105 | convolution fusion | flops 2422207488 | bytes 45625344 | tf_op jit(solution)/shard_map/bhnk,bkhe->bnhe/dot_general | solution.py:302
  1231.8 19.8 %multiply_bitcast_fusion = f32[8,768,6,64]{1,3,2,0:T(8,128)} fusion(bf16[8,512,6,64]{1,3,2,0:T(8,128)(2,1)} %bitcast.504, bf16[8,6,512,768]{3,2,1,0:T(8,128)(2,1)} %get-tuple-element.112), kind=kOutput, calls=%fused_computation.69 | convolution fusion | flops 2418278400 | bytes 50331648 | tf_op jit(solution)/shard_map/bhnk,bnhe->bkhe/dot_general | solution.py:314
  1251.6 16.6 copy.137
  1268.2 19.5 %reshape.437 = f32[8,24,32,384]{3,2,1,0:T(8,128)} reshape(f32[8,768,6,64]{3,2,1,0:T(8,128)} %copy.137) | data formatting | bytes 18874368 | tf_op jit(solution)/shard_map/reshape | solution.py:331
  1290.5 16.7 copy.136
  1307.3 19.4 %reshape.436 = f32[8,24,32,384]{3,2,1,0:T(8,128)} reshape(f32[8,768,6,64]{3,2,1,0:T(8,128)} %copy.136) | data formatting | bytes 18874368 | tf_op jit(solution)/shard_map/reshape | solution.py:330
  1415.9 23.8 %reshape.440 = f32[6,16,32,24,32]{4,3,2,1,0:T(8,128)} reshape(f32[6,512,768]{2,1,0:T(8,128)} %get-tuple-element.111) | data formatting | bytes 18874368 | tf_op jit(solution)/shard_map/transpose(jvp())/reshape | solution.py:92
  1439.7 25.5 %slice_bitcast_fusion.31 = (f32[6,32,24,32]{3,2,1,0:T(8,128)S(1)}, f32[6,32,24,32]{3,2,1,0:T(8,128)}, f32[6,32,24,32]{3,2,1,0:T(8,128)}, f32[6,32,24,32]{3,2,1,0...) fusion(f32[6,16,32,24,32]{4,3,2,1,0:T(8,128)} %reshape.440), kind=kLoop, calls=%fused_computation.184 | loop fusion | bytes 18874368 | tf_op jit(solution)/shard_map/transpose(jvp())/unstack | solution.py:90
  1489.4 42.4 %all-reduce.39 = (f32[2,384]{1,0:T(2,128)}, f32[2,384]{1,0:T(2,128)}, f32[2,6,567]{2,1,0:T(8,128)S(1)}, f32[2,384]{1,0:T(2,128)}, f32[2,384]{1,0:T(2,128)}, /*in...) all-reduce(f32[2,384]{1,0:T(2,128)S(1)} %pad_maximum_fusion.22, ...), channel_id=1, replica_groups=mesh['img'=16,'band'=2] {'img','band'}, use_global_device_ids=true, to_apply=%region_24.25 | all-reduce | flops 14484 | bytes 115872 | tf_op jit(solution)/shard_map/psum | solution.py:388
  1540.1 142.0 %all-reduce.43.cloned.1.call-done = (f32[2,384,1152]{2,1,0:T(8,128)}, f32[2,384,768]{2,1,0:T(8,128)}, f32[2,384,384]{2,1,0:T(8,128)}, f32[2,384,1536]{2,1,0:T(8,128)}, f32[2,1536,384]{2,1,0:T(8,128)}) async-done(((f32[2,384,1152]{2,1,0:T(8,128)}, f32[2,384,768]{2,1,0:T(8,128)}, f32[2,384,384]{2,1,0:T(8,128)}, f32[2,384,1536]{2,1,0:T(8,128)}, f32[2,1536,384]{2,1,0:T(8,128)}), (f32[2,384,1152]{2,1,0:T(8,128)}, ...) | async-done | bytes 16515088 | tf_op jit(solution)/shard_map/psum | solution.py:388
  (535 shorter events, 644.2 us)
Async XLA Ops:
  7.2 1674.9 %all-reduce.43.cloned.1.call-start = ((), (), s32[]{:S(2)}) async-start(), calls=%async_computation | async-start | bytes 33030144 | tf_op jit(solution)/shard_map/psum | solution.py:388
  8.2 25.5 %copy-start.74 = (bf16[8,192]{1,0:T(8,128)(2,1)}, bf16[8,192]{1,0:T(8,128)(2,1)S(1)}, u32[]{:S(2)}) copy-start(bf16[8,192]{1,0:T(8,128)(2,1)S(1)} %get-tuple-element.167) | copy-start | bytes 9220
  8.2 25.5 %copy-start.76 = (bf16[8,192]{1,0:T(8,128)(2,1)}, bf16[8,192]{1,0:T(8,128)(2,1)S(1)}, u32[]{:S(2)}) copy-start(bf16[8,192]{1,0:T(8,128)(2,1)S(1)} %get-tuple-element.168) | copy-start | bytes 9220
  26.2 121.7 %collective-permute-start = (bf16[8,4,32,768]{3,2,1,0:T(8,128)(2,1)}, bf16[8,4,32,768]{3,2,1,0:T(8,128)(2,1)}, u32[]{:S(2)}, u32[]{:S(2)}) collective-permute-start(bf16[8,4,32,768]{3,2,1,0:T(8,128)(2,1)} %get-tuple-element.157), channel_id=1, source_target_pairs={{0,1},{2,3},{4,5},{6,7},{8,9},{10,11},{12,13},{14,15},{16,17},{18,... | collective-permute-start | bytes 4718600 | tf_op jit(solution)/shard_map/ppermute | solution.py:21
  32.4 115.5 %collective-permute-start.1 = (bf16[8,4,32,768]{3,2,1,0:T(8,128)(2,1)}, bf16[8,4,32,768]{3,2,1,0:T(8,128)(2,1)}, u32[]{:S(2)}, u32[]{:S(2)}) collective-permute-start(bf16[8,4,32,768]{3,2,1,0:T(8,128)(2,1)} %get-tuple-element.158), channel_id=1, source_target_pairs={{1,0},{3,2},{5,4},{7,6},{9,8},{11,10},{13,12},{15,14},{17,16},{19,... | collective-permute-start | bytes 4718600 | tf_op jit(solution)/shard_map/ppermute | solution.py:24
  34.1 93.7 %copy-start.56 = (f32[8,512]{1,0:T(8,128)}, f32[8,512]{1,0:T(8,128)S(1)}, u32[]{:S(2)}) copy-start(f32[8,512]{1,0:T(8,128)S(1)} %div.84) | copy-start | bytes 49156
  43.1 83.9 %copy-start = (f32[6,32,9,32]{3,2,0,1:T(8,128)}, f32[6,32,9,32]{3,2,0,1:T(8,128)S(1)}, u32[]{:S(2)}) copy-start(f32[6,32,9,32]{3,2,0,1:T(8,128)S(1)} %convolution_bitcast_fusion.4) | copy-start | bytes 663556
  253.6 27.4 %copy-start.50 = (f32[8,6,512]{2,1,0:T(8,128)}, f32[8,6,512]{2,1,0:T(8,128)S(1)}, u32[]{:S(2)}) copy-start(f32[8,6,512]{2,1,0:T(8,128)S(1)} %get-tuple-element.171) | copy-start | bytes 294916
  253.6 27.4 %copy-start.8 = (bf16[8,16,32,384]{3,2,1,0:T(8,128)(2,1)S(1)}, bf16[8,16,32,384]{3,2,1,0:T(8,128)(2,1)}, u32[]{:S(2)}) copy-start(bf16[8,16,32,384]{3,2,1,0:T(8,128)(2,1)} %param.18) | copy-start | bytes 9437188
  253.6 27.5 %copy-start.41 = (bf16[2,384,384]{2,1,0:T(8,128)(2,1)S(1)}, bf16[2,384,384]{2,1,0:T(8,128)(2,1)}, u32[]{:S(2)}) copy-start(bf16[2,384,384]{2,1,0:T(8,128)(2,1)} %param.28) | copy-start | bytes 1769476
  253.6 27.5 %copy-start.125 = (f32[384]{0:T(512)S(1)}, f32[384]{0:T(512)}, u32[]{:S(2)}) copy-start(f32[384]{0:T(512)} %get-tuple-element.91) | copy-start | bytes 4612
  316.6 66.7 %copy-start.31 = (bf16[8,512,384]{2,1,0:T(8,128)(2,1)}, bf16[8,512,384]{2,1,0:T(8,128)(2,1)S(1)}, u32[]{:S(2)}) copy-start(bf16[8,512,384]{2,1,0:T(8,128)(2,1)S(1)} %add_convert_fusion.5) | copy-start | bytes 9437188
  322.4 65.1 %collective-permute-start.2 = (bf16[8,4,32,768]{3,2,1,0:T(8,128)(2,1)}, bf16[8,4,32,768]{3,2,1,0:T(8,128)(2,1)}, u32[]{:S(2)}, u32[]{:S(2)}) collective-permute-start(bf16[8,4,32,768]{3,2,1,0:T(8,128)(2,1)} %get-tuple-element.155), channel_id=1, source_target_pairs={{0,1},{2,3},{4,5},{6,7},{8,9},{10,11},{12,13},{14,15},{16,17},{18,... | collective-permute-start | bytes 4718600 | tf_op jit(solution)/shard_map/ppermute | solution.py:21
  329.2 58.2 %collective-permute-start.3 = (bf16[8,4,32,768]{3,2,1,0:T(8,128)(2,1)}, bf16[8,4,32,768]{3,2,1,0:T(8,128)(2,1)}, u32[]{:S(2)}, u32[]{:S(2)}) collective-permute-start(bf16[8,4,32,768]{3,2,1,0:T(8,128)(2,1)} %get-tuple-element.156), channel_id=1, source_target_pairs={{1,0},{3,2},{5,4},{7,6},{9,8},{11,10},{13,12},{15,14},{17,16},{19,... | collective-permute-start | bytes 4718600 | tf_op jit(solution)/shard_map/ppermute | solution.py:24
  452.2 69.9 %slice-start.2 = ((s8[6291456]{0:T(1024)(128)(4,1)}), s8[2097152]{0:T(1024)(128)(4,1)S(1)}, s32[]{:S(2)}) async-start(s8[6291456]{0:T(1024)(128)(4,1)} %bitcast.483), calls=%async_computation.3 | async-start | bytes 4194304
  494.5 27.6 %slice-start.3 = ((s8[6291456]{0:T(1024)(128)(4,1)}), s8[4194304]{0:T(1024)(128)(4,1)S(1)}, s32[]{:S(2)}) async-start(s8[6291456]{0:T(1024)(128)(4,1)} %bitcast.483), calls=%async_computation.4 | async-start | bytes 8388608
  494.5 27.6 %copy-start.42 = (bf16[2,384,384]{2,1,0:T(8,128)(2,1)S(1)}, bf16[2,384,384]{2,1,0:T(8,128)(2,1)}, u32[]{:S(2)}) copy-start(bf16[2,384,384]{2,1,0:T(8,128)(2,1)} %param.28) | copy-start | bytes 1769476
  494.5 27.6 %copy-start.97 = (f32[384]{0:T(512)S(1)}, f32[384]{0:T(512)}, u32[]{:S(2)}) copy-start(f32[384]{0:T(512)} %get-tuple-element.90) | copy-start | bytes 4612
  524.9 56.3 %copy-start.2 = (f32[8,512,384]{2,1,0:T(8,128)}, f32[8,512,384]{2,1,0:T(8,128)S(1)}, u32[]{:S(2)}) copy-start(f32[8,512,384]{2,1,0:T(8,128)S(1)} %get-tuple-element.182) | copy-start | bytes 18874372
  524.9 56.2 %copy-start.54 = (f32[8,512]{1,0:T(8,128)}, f32[8,512]{1,0:T(8,128)S(1)}, u32[]{:S(2)}) copy-start(f32[8,512]{1,0:T(8,128)S(1)} %broadcast_multiply_fusion.9) | copy-start | bytes 49156
  526.3 54.8 %copy-start.67 = (f32[8,512]{1,0:T(8,128)}, f32[8,512]{1,0:T(8,128)S(1)}, u32[]{:S(2)}) copy-start(f32[8,512]{1,0:T(8,128)S(1)} %add_rsqrt_fusion.1) | copy-start | bytes 49156
  879.6 80.1 %collective-permute-start.4 = (bf16[8,4,32,768]{3,2,1,0:T(8,128)(2,1)}, bf16[8,4,32,768]{3,2,1,0:T(8,128)(2,1)}, u32[]{:S(2)}, u32[]{:S(2)}) collective-permute-start(bf16[8,4,32,768]{3,2,1,0:T(8,128)(2,1)} %get-tuple-element.149), channel_id=1, source_target_pairs={{0,1},{2,3},{4,5},{6,7},{8,9},{10,11},{12,13},{14,15},{16,17},{18,... | collective-permute-start | bytes 4718600 | tf_op jit(solution)/shard_map/ppermute | solution.py:32
  886.5 73.2 %collective-permute-start.5 = (bf16[8,4,32,768]{3,2,1,0:T(8,128)(2,1)}, bf16[8,4,32,768]{3,2,1,0:T(8,128)(2,1)}, u32[]{:S(2)}, u32[]{:S(2)}) collective-permute-start(bf16[8,4,32,768]{3,2,1,0:T(8,128)(2,1)} %get-tuple-element.150), channel_id=1, source_target_pairs={{1,0},{3,2},{5,4},{7,6},{9,8},{11,10},{13,12},{15,14},{17,16},{19,... | collective-permute-start | bytes 4718600 | tf_op jit(solution)/shard_map/ppermute | solution.py:32
  992.1 40.5 %slice-start.8 = ((s8[6291456]{0:T(1024)(128)(4,1)}), s8[4194304]{0:T(1024)(128)(4,1)S(1)}, s32[]{:S(2)}) async-start(s8[6291456]{0:T(1024)(128)(4,1)} %bitcast.491), calls=%async_computation.9 | async-start | bytes 8388608
  1005.2 27.4 %slice-start.9 = ((s8[6291456]{0:T(1024)(128)(4,1)}), s8[2097152]{0:T(1024)(128)(4,1)S(1)}, s32[]{:S(2)}) async-start(s8[6291456]{0:T(1024)(128)(4,1)} %bitcast.491), calls=%async_computation.10 | async-start | bytes 4194304
  1005.2 27.4 %copy-start.66 = (f32[8,512]{1,0:T(8,128)S(1)}, f32[8,512]{1,0:T(8,128)}, u32[]{:S(2)}) copy-start(f32[8,512]{1,0:T(8,128)} %copy-done.65) | copy-start | bytes 49156
  1005.2 27.4 %copy-start.79 = (f32[8,512]{1,0:T(8,128)S(1)}, f32[8,512]{1,0:T(8,128)}, u32[]{:S(2)}) copy-start(f32[8,512]{1,0:T(8,128)} %copy-done.78) | copy-start | bytes 49156
  1005.2 27.4 %copy-start.109 = (f32[384]{0:T(512)S(1)}, f32[384]{0:T(512)}, u32[]{:S(2)}) copy-start(f32[384]{0:T(512)} %get-tuple-element.203) | copy-start | bytes 4612
  1005.2 27.4 %copy-start.121 = (f32[384]{0:T(512)S(1)}, f32[384]{0:T(512)}, u32[]{:S(2)}) copy-start(f32[384]{0:T(512)} %get-tuple-element.83) | copy-start | bytes 4612
  1340.3 38.2 %collective-permute-start.6 = (bf16[8,4,32,768]{3,2,1,0:T(8,128)(2,1)}, bf16[8,4,32,768]{3,2,1,0:T(8,128)(2,1)}, u32[]{:S(2)}, u32[]{:S(2)}) collective-permute-start(bf16[8,4,32,768]{3,2,1,0:T(8,128)(2,1)} %get-tuple-element.147), channel_id=1, source_target_pairs={{0,1},{2,3},{4,5},{6,7},{8,9},{10,11},{12,13},{14,15},{16,17},{18,... | collective-permute-start | bytes 4718600 | tf_op jit(solution)/shard_map/ppermute | solution.py:32
  1347.4 36.4 %collective-permute-start.7 = (bf16[8,4,32,768]{3,2,1,0:T(8,128)(2,1)}, bf16[8,4,32,768]{3,2,1,0:T(8,128)(2,1)}, u32[]{:S(2)}, u32[]{:S(2)}) collective-permute-start(bf16[8,4,32,768]{3,2,1,0:T(8,128)(2,1)} %get-tuple-element.148), channel_id=1, source_target_pairs={{1,0},{3,2},{5,4},{7,6},{9,8},{11,10},{13,12},{15,14},{17,16},{19,... | collective-permute-start | bytes 4718600 | tf_op jit(solution)/shard_map/ppermute | solution.py:32
  1439.7 25.5 %copy-start.62 = (s32[32,32]{1,0:T(8,128)S(1)}, s32[32,32]{1,0:T(8,128)}, u32[]{:S(2)}) copy-start(s32[32,32]{1,0:T(8,128)} %copy-done.60) | copy-start | bytes 12292
  (134 other events, 1202.9 us)
Sparse Core Ops, SparseCore 0:
  1402.0 280.1 all-reduce.42
where the time goes:
time: 1720 us; the launch traced here: 1700 us
  matrix products  654 us (38%)
  local copies, waits for them, and re-layouts  578 us (34%)
  other arithmetic  217 us (13%)
  waiting for transfers between devices  161 us (9%)
  blocking collectives  42.4 us (2%)
  starting transfers between devices  32.2 us (2%)
    psum x1, waiting for transfers between devices, body(): summed = tuple(lax.psum(stacked, ('img', 'band')))  142 us
    reduce_sum x2, other arithmetic, body(): grad_offset = bias_pull(jnp.sum(grad_scores, axis=0, dtype=jnp.float32))[0]  132 us
    dot_general x2, matrix products, body(): jnp.einsum('bnhe,bkhe->bhnk', grad_attended, backward_value_heads, prefer...  100 us
    unnamed x352, local copies, waits for them, and re-layouts  89.3 us
    sub x2, matrix products, forward_layer(): exp_terms = jnp.exp(scores - row_max)  82.9 us
    add x4, local copies, waits for them, and re-layouts, forward_layer(): jnp.einsum('bnhe,bkhe->bhnk', query_heads, key_heads, preferred_element_t...  79.3 us
    dot_general x2, matrix products, body(): jnp.einsum('bhnk,bnhe->bkhe', backward_attention_low, grad_attended, pref...  58.2 us
    reshape x4, local copies, waits for them, and re-layouts, forward_layer(): padded_pairs[..., model_width:]  55.1 us
  transfers between devices with their start and end apart: 9, of which 3 were waited for; matrix products, arithmetic and copies ran while one was open for 20% of the time, Pallas kernels for 0%

commit v1 on v0

v1 whole, which is shorter than its diff:
```python
import functools
import math

import jax
import jax.numpy as jnp
from jax import lax
from jax.experimental import pallas as pl
from jax.experimental.pallas import tpu as pltpu
from jax.sharding import PartitionSpec as P

WIN = 4
CHUNK = 256
QBLOCK = 128
KWIN = 384
HALO = 128

EXACT = lax.Precision.HIGHEST
NEG_FILL = -1000000000.0
EPSILON = 1e-06
GELU_A = math.sqrt(2.0 / math.pi)
GELU_B = 0.044715 * GELU_A
VMEM_BYTES = 58 * 1024 * 1024

F32 = jnp.float32
BF16 = jnp.bfloat16


def dot(a, b):
    return jnp.dot(a, b, preferred_element_type=F32)


def dot_nt(a, b):
    return lax.dot_general(a, b, (((1,), (1,)), ((), ())), preferred_element_type=F32)


def norm_stats(v):
    mean = jnp.mean(v, axis=-1, keepdims=True)
    centered = v - mean
    inverse = lax.rsqrt(jnp.mean(centered * centered, axis=-1, keepdims=True) + EPSILON)
    return centered * inverse, inverse


def norm_back(gy, xh, inverse, gain):
    gs = gy * gain
    return inverse * (
        gs - jnp.mean(gs, axis=-1, keepdims=True) - xh * jnp.mean(gs * xh, axis=-1, keepdims=True)
    )


def row_sums(v):
    rows, cols = v.shape
    return jnp.sum(v.reshape(rows // 8, 8, cols), axis=0)


def split_heads(block):
    lane = lax.broadcasted_iota(jnp.int32, block.shape, 1)
    zero = jnp.zeros_like(block)
    first = lane < block.shape[1] // 2
    return jnp.concatenate(
        [jnp.where(first, block, zero), jnp.where(first, zero, block)], axis=0
    )


def join_heads(product):
    half = product.shape[0] // 2
    width = product.shape[1] // 2
    return jnp.concatenate([product[:half, :width], product[half:, width:]], axis=0).T


def forward_kernel(
    pairs,
    x_new,
    x_old,
    tproj,
    mask,
    bias,
    gain1,
    shift1,
    wqkv,
    wo,
    bo,
    gain2,
    shift2,
    w1,
    b1,
    w2,
    b2,
    qkv_out,
    p_out,
    o_out,
    mid_out,
    act_out,
    slope_out,
    x_out,
    q_ring,
    k_ring,
    vt_ring,
    o_ring,
):
    step = pl.program_id(0)
    width = x_new.shape[1]

    @pl.when(step == 0)
    def _():
        q_ring[...] = jnp.zeros_like(q_ring)
        k_ring[...] = jnp.zeros_like(k_ring)
        vt_ring[...] = jnp.zeros_like(vt_ring)
        o_ring[...] = jnp.zeros_like(o_ring)

    attended = o_ring[...]
    mid = x_old[...].astype(F32) + (dot(attended, wo[...]) + bo[...])
    mid_out[...] = mid
    xh2, _ = norm_stats(mid)
    c = (xh2 * gain2[...] + shift2[...]).astype(BF16)
    u = dot(c, w1[...]) + b1[...]
    u2 = u * u
    t = jnp.tanh(u * (GELU_A + GELU_B * u2))
    h = 0.5 + 0.5 * t
    e = u * h
    act = e.astype(BF16)
    act_out[...] = act
    slope_out[...] = (h + (e * (1.0 - t)) * (GELU_A + (3.0 * GELU_B) * u2)).astype(BF16)
    x_out[...] = (mid + (dot(act, w2[...]) + b2[...])).astype(x_out.dtype)

    queries = q_ring[...]
    xh1, _ = norm_stats(x_new[...].astype(F32))
    a = (xh1 * gain1[...] + shift1[...]).astype(BF16)
    qkv = (dot(a, wqkv[...]) + tproj[0]).astype(BF16)
    qkv_out[...] = qkv
    q_ring[...] = qkv[:, :width] * jnp.asarray(0.125, BF16)
    k_ring[:HALO, :] = k_ring[CHUNK : CHUNK + HALO, :]
    k_ring[HALO : HALO + CHUNK, :] = k_ring[HALO + CHUNK :, :]
    k_ring[HALO + CHUNK :, :] = qkv[:, width : 2 * width]
    vt_ring[:, :HALO] = vt_ring[:, CHUNK : CHUNK + HALO]
    vt_ring[:, HALO : HALO + CHUNK] = vt_ring[:, HALO + CHUNK :]
    vt_ring[:, HALO + CHUNK :] = qkv[:, 2 * width :].T

    key_index = lax.broadcasted_iota(jnp.int32, (KWIN, QBLOCK), 0)
    query_index = lax.broadcasted_iota(jnp.int32, (KWIN, QBLOCK), 1)
    diagonal = key_index == query_index + HALO
    for blk in range(CHUNK // QBLOCK):
        low = blk * QBLOCK
        row = mask[0, :, low : low + KWIN]
        column = jnp.broadcast_to(row, (QBLOCK, KWIN)).T
        extra = jnp.where(diagonal, 0.0, column)
        extra = jnp.concatenate([extra, extra], axis=1)
        for pair in range(pairs):
            feat = slice(pair * 128, (pair + 1) * 128)
            split_q = split_heads(queries[low : low + QBLOCK, feat])
            s = dot_nt(k_ring[low : low + KWIN, feat], split_q) + bias[pair] + extra
            top = jnp.max(s, axis=0, keepdims=True)
            ex = jnp.exp(s - top)
            total = jnp.sum(ex, axis=0, keepdims=True)
            p = (ex * (1.0 / total)).astype(BF16)
            p_out[blk, pair] = p
            o = join_heads(dot(vt_ring[feat, low : low + KWIN], p)).astype(BF16)
            o_ring[low : low + QBLOCK, feat] = o
            o_out[low : low + QBLOCK, feat] = o


def const_spec(shape):
    zeros = (0,) * len(shape)
    return pl.BlockSpec(shape, lambda g: zeros, pipeline_mode=pl.Buffered(1))


def forward_layer(x, x_lead, chunks, chunks_per_image, tproj, mask, bias, weights, out_dtype):
    width = x.shape[1]
    hidden = weights[7].shape[1]
    pairs = width // 128
    steps = chunks + 2

    def at(lead, least=0):
        def index(g):
            return jnp.clip(g - lead, least, chunks - 1)

        return index

    new_at, attn_at, old_at = at(0), at(1), at(2)
    row = pl.BlockSpec((CHUNK, width), lambda g: (g, 0))
    wide = pl.BlockSpec((CHUNK, hidden), lambda g: (g, 0))
    rows = steps * CHUNK
    gain1, shift1, wqkv, wo, bo, gain2, shift2, w1, b1, w2, b2 = weights
    consts = [gain1, shift1, wqkv, wo, bo, gain2, shift2, w1, b1, w2, b2]
    return pl.pallas_call(
        functools.partial(forward_kernel, pairs),
        grid=(steps,),
        in_specs=[
            pl.BlockSpec((CHUNK, width), lambda g: (new_at(g) + x_lead, 0)),
            pl.BlockSpec((CHUNK, width), lambda g: (old_at(g) + x_lead, 0)),
            pl.BlockSpec((1, 1, 3 * width), lambda g: (new_at(g) // chunks_per_image, 0, 0)),
            pl.BlockSpec((1, 1, CHUNK + 2 * HALO), lambda g: (attn_at(g), 0, 0)),
            const_spec(bias.shape),
        ]
        + [const_spec(w.shape) for w in consts],
        out_specs=[
            pl.BlockSpec((CHUNK, 3 * width), lambda g: (new_at(g), 0)),
            pl.BlockSpec((CHUNK // QBLOCK, pairs, KWIN, 2 * QBLOCK), lambda g: (g, 0, 0, 0)),
            row,
            row,
            wide,
            wide,
            row,
        ],
        out_shape=[
            jax.ShapeDtypeStruct((chunks * CHUNK, 3 * width), BF16),
            jax.ShapeDtypeStruct((steps * (CHUNK // QBLOCK), pairs, KWIN, 2 * QBLOCK), BF16),
            jax.ShapeDtypeStruct((rows, width), BF16),
            jax.ShapeDtypeStruct((rows, width), F32),
            jax.ShapeDtypeStruct((rows, hidden), BF16),
            jax.ShapeDtypeStruct((rows, hidden), BF16),
            jax.ShapeDtypeStruct((rows, width), out_dtype),
        ],
        scratch_shapes=[
            pltpu.VMEM((CHUNK, width), BF16),
            pltpu.VMEM((HALO + 2 * CHUNK, width), BF16),
            pltpu.VMEM((width, HALO + 2 * CHUNK), BF16),
            pltpu.VMEM((CHUNK, width), BF16),
        ],
        compiler_params=pltpu.CompilerParams(vmem_limit_bytes=VMEM_BYTES),
        name="block_forward",
    )(x, x, tproj, mask, bias, *consts)


def feed_back_kernel(
    gx,
    mid,
    act,
    slope,
    o,
    gain2,
    shift2,
    w1t,
    w2t,
    wot,
    gmid_out,
    go_out,
    gw2t,
    gw1,
    gwo,
    sums,
    gb1,
):
    step = pl.program_id(0)

    @pl.when(step == 0)
    def _():
        for ref in (gw2t, gw1, gwo, sums, gb1):
            ref[...] = jnp.zeros_like(ref)

    grad = gx[...].astype(F32)
    gr = grad.astype(BF16)
    gw2t[...] += dot(gr.T, act[...])
    ge = dot(gr, w2t[...])
    gu = (ge * slope[...].astype(F32)).astype(BF16)
    gb1[...] += row_sums(gu.astype(F32))
    xh, inverse = norm_stats(mid[...])
    c = (xh * gain2[...] + shift2[...]).astype(BF16)
    gw1[...] += dot(c.T, gu)
    gc = dot(gu, w1t[...])
    gmid = grad + norm_back(gc, xh, inverse, gain2[...])
    gmid_out[...] = gmid
    gb = gmid.astype(BF16)
    gwo[...] += dot(o[...].T, gb)
    go_out[...] = dot(gb, wot[...]).astype(BF16)
    sums[0] += row_sums(gr.astype(F32))
    sums[1] += row_sums(gb.astype(F32))
    sums[2] += row_sums(gc * xh)
    sums[3] += row_sums(gc)


def feed_back(gx, gx_lead, chunks, mid, act, slope, o, gain2, shift2, w1t, w2t, wot):
    width = mid.shape[1]
    hidden = act.shape[1]

    def rows(cols, lead):
        return pl.BlockSpec((CHUNK, cols), lambda g: (g + lead, 0))

    def kept(shape):
        zeros = (0,) * len(shape)
        return pl.BlockSpec(shape, lambda g: zeros)

    grads = [(width, hidden), (width, hidden), (width, width), (4, 8, width), (8, hidden)]
    return pl.pallas_call(
        feed_back_kernel,
        grid=(chunks,),
        in_specs=[
            rows(width, gx_lead),
            rows(width, 2),
            rows(hidden, 2),
            rows(hidden, 2),
            rows(width, 1),
        ]
        + [const_spec(w.shape) for w in (gain2, shift2, w1t, w2t, wot)],
        out_specs=[rows(width, 0), rows(width, 0)] + [kept(shape) for shape in grads],
        out_shape=[
            jax.ShapeDtypeStruct((chunks * CHUNK, width), F32),
            jax.ShapeDtypeStruct((chunks * CHUNK, width), BF16),
        ]
        + [jax.ShapeDtypeStruct(shape, F32) for shape in grads],
        compiler_params=pltpu.CompilerParams(vmem_limit_bytes=VMEM_BYTES),
        name="feed_back",
    )(gx, mid, act, slope, o, gain2, shift2, w1t, w2t, wot)


def attend_back_kernel(
    pairs,
    chunks,
    chunks_per_image,
    prev,
    cur,
    nxt,
    p_in,
    go_in,
    o_in,
    gmid,
    x,
    gain1,
    shift1,
    wqkvt,
    gx_out,
    gwqkv,
    gbias,
    gtime,
    sums,
    gq_ring,
    gkv_ring,
):
    step = pl.program_id(0)
    width = x.shape[1]

    @pl.when(step == 0)
    def _():
        for ref in (gwqkv, gbias, gtime, sums, gq_ring, gkv_ring):
            ref[...] = jnp.zeros_like(ref)

    gq_old = gq_ring[...]
    live = (step < chunks).astype(BF16)
    go = go_in[...] * live
    qkv = cur[...]
    queries = qkv[:, :width] * jnp.asarray(0.125, BF16)
    keys = jnp.concatenate(
        [prev[:, width : 2 * width], qkv[:, width : 2 * width], nxt[:, width : 2 * width]], axis=0
    )
    keys_t = keys.T
    values = jnp.concatenate([prev[:, 2 * width :], qkv[:, 2 * width :], nxt[:, 2 * width :]], axis=0)
    dots = (go.astype(F32) * o_in[...].astype(F32)).T
    for blk in range(CHUNK // QBLOCK):
        low = blk * QBLOCK
        for pair in range(pairs):
            feat = slice(pair * 128, (pair + 1) * 128)
            own = dots[feat, low : low + QBLOCK]
            row_dot = jnp.concatenate(
                [
                    jnp.sum(own[:64], axis=0, keepdims=True),
                    jnp.sum(own[64:], axis=0, keepdims=True),
                ],
                axis=1,
            )
            p = p_in[blk, pair]
            split_go = split_heads(go[low : low + QBLOCK, feat])
            split_q = split_heads(queries[low : low + QBLOCK, feat])
            gp = dot_nt(values[low : low + KWIN, feat], split_go)
            gs = p.astype(F32) * (gp - row_dot)
            gbias[pair] += gs
            gs = gs.astype(BF16)
            at = HALO + low
            gkv_ring[at : at + KWIN, feat] += dot(gs, split_q)
            vfeat = slice(width + pair * 128, width + (pair + 1) * 128)
            gkv_ring[at : at + KWIN, vfeat] += dot(p, split_go)
            gq = join_heads(dot(keys_t[feat, low : low + KWIN], gs)) * 0.125
            gq_ring[low : low + QBLOCK, feat] = gq.astype(BF16)

    done = jnp.concatenate([gq_old, gkv_ring[:CHUNK, :].astype(BF16)], axis=1)
    gkv_ring[:CHUNK, :] = gkv_ring[CHUNK : 2 * CHUNK, :]
    gkv_ring[CHUNK : CHUNK + HALO, :] = gkv_ring[2 * CHUNK :, :]
    gkv_ring[CHUNK + HALO :, :] = jnp.zeros((CHUNK, 2 * width), F32)
    xh, inverse = norm_stats(x[...].astype(F32))
    a = (xh * gain1[...] + shift1[...]).astype(BF16)
    gwqkv[...] += dot(a.T, done)
    ga = dot(done, wqkvt[...])
    gx_out[...] = (gmid[...] + norm_back(ga, xh, inverse, gain1[...])).astype(gx_out.dtype)
    sums[0] += row_sums(ga * xh)
    sums[1] += row_sums(ga)
    first = lax.rem(step + chunks_per_image - 1, chunks_per_image) == 0
    before = jnp.where(first, jnp.zeros(gtime.shape[1:], F32), gtime[0])
    summed = row_sums(done.astype(F32))
    gtime[0] = before + jnp.concatenate([summed[:, :width], summed[:, 2 * width :]], axis=1)


def attend_back(
    qkv, p, go, o, gmid, x, x_lead, chunks, chunks_per_image, gain1, shift1, wqkvt, out_dtype
):
    width = x.shape[1]
    pairs = width // 128
    steps = chunks + 1
    halves = CHUNK // HALO

    def now(g):
        return jnp.minimum(g, chunks - 1)

    def late(g):
        return jnp.maximum(g - 1, 0)

    def rows(cols, lead, index):
        return pl.BlockSpec((CHUNK, cols), lambda g: (index(g) + lead, 0))

    def kept(shape):
        zeros = (0,) * len(shape)
        return pl.BlockSpec(shape, lambda g: zeros)

    images = chunks // chunks_per_image
    return pl.pallas_call(
        functools.partial(attend_back_kernel, pairs, chunks, chunks_per_image),
        grid=(steps,),
        in_specs=[
            pl.BlockSpec((HALO, 3 * width), lambda g: (jnp.maximum(halves * now(g) - 1, 0), 0)),
            rows(3 * width, 0, now),
            pl.BlockSpec(
                (HALO, 3 * width),
                lambda g: (jnp.minimum(halves * (now(g) + 1), halves * chunks - 1), 0),
            ),
            pl.BlockSpec(
                (CHUNK // QBLOCK, pairs, KWIN, 2 * QBLOCK), lambda g: (now(g) + 1, 0, 0, 0)
            ),
            rows(width, 0, now),
            rows(width, 1, now),
            rows(width, 0, late),
            rows(width, x_lead, late),
        ]
        + [const_spec(w.shape) for w in (gain1, shift1, wqkvt)],
        out_specs=[
            rows(width, 0, lambda g: g),
            kept((width, 3 * width)),
            kept((pairs, KWIN, 2 * QBLOCK)),
            pl.BlockSpec((1, 8, 2 * width), lambda g: (late(g) // chunks_per_image, 0, 0)),
            kept((2, 8, width)),
        ],
        out_shape=[
            jax.ShapeDtypeStruct((steps * CHUNK, width), out_dtype),
            jax.ShapeDtypeStruct((width, 3 * width), F32),
            jax.ShapeDtypeStruct((pairs, KWIN, 2 * QBLOCK), F32),
            jax.ShapeDtypeStruct((images, 8, 2 * width), F32),
            jax.ShapeDtypeStruct((2, 8, width), F32),
        ],
        scratch_shapes=[
            pltpu.VMEM((CHUNK, width), BF16),
            pltpu.VMEM((2 * CHUNK + HALO, 2 * width), F32),
        ],
        compiler_params=pltpu.CompilerParams(vmem_limit_bytes=VMEM_BYTES),
        name="attend_back",
    )(qkv, qkv, qkv, p, go, o, gmid, x, gain1, shift1, wqkvt)


def time_embedding(timesteps, width):
    half_width = width // 2
    frequency = jnp.exp(
        jnp.arange(half_width, dtype=jnp.int32).astype(F32) * (-math.log(10000.0) / half_width)
    )
    angles = timesteps.astype(F32)[:, None] * frequency[None, :]
    return jnp.concatenate([jnp.sin(angles), jnp.cos(angles)], axis=-1)


def column_table(grid_cols):
    col = jnp.arange(grid_cols, dtype=jnp.int32)
    col_diff = col[None, :] - col[:, None] + grid_cols - 1
    return (
        col_diff[:, :, None] == jnp.arange(2 * grid_cols - 1, dtype=jnp.int32)[None, None, :]
    ).astype(F32)


def bias_tiles(offset_bias, index_table, grid_cols):
    layers, heads, entries = offset_bias.shape
    span = 2 * WIN + 1
    query_rows = QBLOCK // grid_cols
    key_rows = KWIN // grid_cols
    select = (index_table[:, None] == jnp.arange(entries, dtype=jnp.int32)[None, :]).astype(F32)
    table = offset_bias.reshape(layers * heads, entries)
    per_offset = jnp.dot(table, select.T, precision=EXACT)
    per_offset = per_offset.reshape(layers * heads, span, 2 * grid_cols - 1)
    mixed = jnp.einsum("hab,ctb->hatc", per_offset, column_table(grid_cols), precision=EXACT)
    placed = [
        jnp.pad(
            mixed,
            ((0, 0), (row, key_rows - row - span), (0, 0), (0, 0)),
            constant_values=NEG_FILL,
        )
        for row in range(query_rows)
    ]
    tile = jnp.stack(placed, axis=3).reshape(layers, heads // 2, 2, KWIN, QBLOCK)
    return tile.transpose(0, 1, 3, 2, 4).reshape(layers, heads // 2, KWIN, 2 * QBLOCK)


def bias_pull(grad, index_table, grid_cols):
    pairs = grad.shape[0]
    entries = index_table.shape[0]
    span = 2 * WIN + 1
    query_rows = QBLOCK // grid_cols
    key_rows = KWIN // grid_cols
    parts = grad.reshape(pairs, key_rows, grid_cols, 2, query_rows, grid_cols)
    mixed = sum(parts[:, row : row + span, :, :, row, :] for row in range(query_rows))
    per_offset = jnp.einsum("pathc,ctb->phab", mixed, column_table(grid_cols), precision=EXACT)
    per_offset = per_offset.reshape(2 * pairs, entries)
    select = (index_table[:, None] == jnp.arange(entries, dtype=jnp.int32)[None, :]).astype(F32)
    return jnp.dot(per_offset, select, precision=EXACT)


def body(
    tokens,
    cotangent,
    valid_mask,
    timesteps,
    index_table,
    first_gain,
    first_shift,
    attend_weight,
    time_weight,
    offset_bias,
    output_weight,
    output_bias,
    second_gain,
    second_shift,
    expand_weight,
    expand_bias,
    reduce_weight,
    reduce_bias,
):
    images, band_rows, grid_cols, width = tokens.shape
    layers = attend_weight.shape[0]
    bands = lax.axis_size("band")
    me = lax.axis_index("band")
    own = images // bands
    part = band_rows * grid_cols
    patches = bands * part
    per_image = patches // CHUNK
    chunks = own * per_image

    def to_images(shard):
        shard = shard.reshape(bands, own, part, width)
        whole = jnp.zeros((own, bands, part, width), shard.dtype)
        for by in range(bands):
            piece = lax.dynamic_index_in_dim(shard, (me + by) % bands, 0, keepdims=False)
            if by:
                pairs = [(i, (i + by) % bands) for i in range(bands)]
                piece = lax.ppermute(piece, "band", pairs)
            whole = lax.dynamic_update_index_in_dim(whole, piece, (me - by) % bands, 1)
        return whole.reshape(own * patches, width)

    def to_bands(whole):
        whole = whole.reshape(own, bands, part, width)
        shard = jnp.zeros((bands, own, part, width), whole.dtype)
        for by in range(bands):
            piece = lax.dynamic_index_in_dim(whole, (me + by) % bands, 1, keepdims=False)
            if by:
                pairs = [(i, (i + by) % bands) for i in range(bands)]
                piece = lax.ppermute(piece, "band", pairs)
            shard = lax.dynamic_update_index_in_dim(shard, piece, (me - by) % bands, 0)
        return shard.reshape(images, band_rows, grid_cols, width)

    x0 = to_images(tokens)
    cot = to_images(cotangent)

    mine = lax.dynamic_slice_in_dim(valid_mask, me * own, own, 0).reshape(own, patches)
    fill = jnp.where(mine == 1, 0.0, NEG_FILL).astype(F32)
    fill = jnp.pad(fill, ((0, 0), (HALO, HALO)), constant_values=NEG_FILL)
    mask = jnp.stack(
        [fill[:, c * CHUNK : (c + 1) * CHUNK + 2 * HALO] for c in range(per_image)], axis=1
    ).reshape(chunks, 1, CHUNK + 2 * HALO)

    time_low = time_embedding(
        lax.dynamic_slice_in_dim(timesteps, me * own, own, 0), width
    ).astype(BF16)
    biases = bias_tiles(offset_bias, index_table, grid_cols)

    def row(v):
        return v.reshape(1, -1)

    x, x_lead = x0, 0
    kept = []
    for layer in range(layers):
        tp = jnp.dot(time_low, time_weight[layer], preferred_element_type=F32)
        tproj = jnp.concatenate([tp[:, :width], jnp.zeros_like(tp[:, :width]), tp[:, width:]], axis=1)
        weights = (
            row(first_gain[layer]),
            row(first_shift[layer]),
            attend_weight[layer],
            output_weight[layer],
            row(output_bias[layer]),
            row(second_gain[layer]),
            row(second_shift[layer]),
            expand_weight[layer],
            row(expand_bias[layer]),
            reduce_weight[layer],
            row(reduce_bias[layer]),
        )
        qkv, p, o, mid, act, slope, nxt = forward_layer(
            x,
            x_lead,
            chunks,
            per_image,
            tproj[:, None, :],
            mask,
            biases[layer],
            weights,
            F32 if layer < layers - 1 else BF16,
        )
        kept.append((x, x_lead, qkv, p, o, mid, act, slope))
        x, x_lead = nxt, 2
    output = to_bands(x[x_lead * CHUNK :])

    gx, gx_lead = cot, 0
    grads = [None] * layers
    for layer in reversed(range(layers)):
        x, x_lead, qkv, p, o, mid, act, slope = kept[layer]
        gmid, go, gw2t, gw1, gwo, sums2, gb1 = feed_back(
            gx,
            gx_lead,
            chunks,
            mid,
            act,
            slope,
            o,
            row(second_gain[layer]),
            row(second_shift[layer]),
            expand_weight[layer].T,
            reduce_weight[layer].T,
            output_weight[layer].T,
        )
        gx, gwqkv, gbias, gtime, sums1 = attend_back(
            qkv,
            p,
            go,
            o,
            gmid,
            x,
            x_lead,
            chunks,
            per_image,
            row(first_gain[layer]),
            row(first_shift[layer]),
            attend_weight[layer].T,
            F32 if layer else BF16,
        )
        gx_lead = 1
        sums1 = jnp.sum(sums1, axis=1)
        sums2 = jnp.sum(sums2, axis=1)
        gtime = jnp.sum(gtime, axis=1)
        gtw = jnp.sum(time_low.astype(F32)[:, :, None] * gtime[:, None, :], axis=0)
        grads[layer] = (
            sums1[0],
            sums1[1],
            gwqkv,
            gtw,
            bias_pull(gbias, index_table, grid_cols),
            gwo,
            sums2[1],
            sums2[2],
            sums2[3],
            gw1,
            jnp.sum(gb1, axis=0),
            gw2t.T,
            sums2[0],
        )
    input_grad = to_bands(gx[gx_lead * CHUNK :])
    stacked = tuple(jnp.stack([g[member] for g in grads]) for member in range(13))
    return (output, input_grad) + tuple(lax.psum(stacked, ("img", "band")))


def solution(mesh):
    split = P("img", "band", None, None)
    placed = (split, split, P("img", None, None), P("img")) + (P(),) * 14
    return jax.shard_map(
        body,
        mesh=mesh,
        in_specs=placed,
        out_specs=(split, split) + (P(),) * 13,
        check_vma=False,
    )
```

time: 1720 us -> 827 us (0.48)
  matrix products: 654 us -> 11.2 us
  local copies, waits for them, and re-layouts: 578 us -> 169 us
  Pallas kernels: 0 us -> 373 us
  other arithmetic: 217 us -> 22.8 us
  blocking collectives: 42.4 us -> 123 us
  waiting for transfers between devices: 161 us -> 102 us
  starting transfers between devices: 32.2 us -> 5.06 us
    dot_general x46 -> x8, matrix products: 572 us -> 11.2 us  [the longest x2 3.8 us: body(): tp = jnp.dot(time_low, time_weight[layer], preferred_element_type=F32)]
    pallas_call x0 -> x6, Pallas kernels: none -> 373 us  [the longest x2 189 us: forward_layer(): pl.pallas_call(functools.partial(forward_kernel, pairs), grid=(steps,), i...]
    reshape x20 -> x8, local copies, waits for them, and re-layouts: 242 us -> 15.7 us  [the longest x2 7.03 us: bias_pull(): parts = grad.reshape(pairs, key_rows, grid_cols, 2, query_rows, grid_cols)]
    reduce_sum x14 -> x9, other arithmetic: 165 us -> 2.97 us  [the longest x2 1.23 us: body(): sums2 = jnp.sum(sums2, axis=1)]
    sub x2 -> x0, matrix products: 82.9 us -> none  [forward_layer(): exp_terms = jnp.exp(scores - row_max)]
    psum x1, blocking collectives: 42.4 us -> 123 us  [body(): return (output, input_grad) + tuple(lax.psum(stacked, ('img', 'band')))]
    add x4 -> x0, local copies, waits for them, and re-layouts: 79.3 us -> none  [forward_layer(): jnp.einsum('bnhe,bkhe->bhnk', query_heads, key_heads, preferred_element_t...]
    psum x1, waiting for transfers between devices: 142 us -> 102 us  [body(): return (output, input_grad) + tuple(lax.psum(stacked, ('img', 'band')))]
  transfers between devices with their start and end apart: 9 -> 5, of which waited for: 3 -> 1; matrix products, arithmetic and copies ran while one was open for 20% -> 19% of each run, Pallas kernels for 0% -> 0%
where the time goes in v1:
time: 827 us; the launch traced here: 822 us
  Pallas kernels  373 us (45%)
  local copies, waits for them, and re-layouts  169 us (20%)
  blocking collectives  123 us (15%)
  waiting for transfers between devices  102 us (12%)
  other arithmetic  22.8 us (3%)
  between operations  15 us (2%)
  matrix products  11.2 us (1%)
    pallas_call x2, Pallas kernels, forward_layer(): pl.pallas_call(functools.partial(forward_kernel, pairs), grid=(steps,), i...  189 us
    psum x1, blocking collectives, body(): return (output, input_grad) + tuple(lax.psum(stacked, ('img', 'band')))  123 us
    psum x1, waiting for transfers between devices, body(): return (output, input_grad) + tuple(lax.psum(stacked, ('img', 'band')))  102 us
    pallas_call x2, Pallas kernels, attend_back(): pl.pallas_call(functools.partial(attend_back_kernel, pairs, chunks, chunk...  102 us
    pallas_call x2, Pallas kernels, feed_back(): pl.pallas_call(feed_back_kernel, grid=(chunks,), in_specs=[rows(width, gx...  82 us
    unnamed x157, local copies, waits for them, and re-layouts  62.8 us
    another operation x2, local copies, waits for them, and re-layouts, bias_tiles(): jnp.stack(placed, axis=3).reshape(layers, heads // 2, 2, KWIN, QBLOCK)  20.9 us
  transfers between devices with their start and end apart: 5, of which 1 were waited for; matrix products, arithmetic and copies ran while one was open for 19% of the time, Pallas kernels for 0%

profile of v1, /device:TPU:0, one launch (start us, length us, event | category | flops | bytes accessed | tf_op | source)
XLA Modules:
  0.0 822.2 jit_solution(4956239527080284529)
XLA Ops:
  7.3 2.9 dynamic-slice_bitcast_fusion.3
  10.1 3.0 collective-permute-start
  22.0 2.7 convolution_bitcast_fusion
  24.7 7.1 pad_bitcast_fusion.3
  31.8 6.7 pad_maximum_fusion
  38.4 13.9 %copy.104 = f32[12,12,32,4,32]{4,3,2,1,0:T(4,128)} copy(f32[12,12,32,4,32]{2,0,1,4,3:T(8,128)} %pad_maximum_fusion) | data formatting | bytes 4718592 | tf_op jit(solution)/shard_map/stack | solution.py:489
  52.3 7.0 reshape.165
  73.7 3.2 copy.105
  76.9 3.1 squeeze.72.bias
  81.3 3.2 copy.115
  84.5 3.1 squeeze.78.bias
  87.6 2.4 copy.144
  108.4 2.5 bitcast_dynamic-update-slice_fusion.2
  114.3 94.8 %block_forward.2 = (bf16[4096,1152]{1,0:T(8,128)(2,1)}, bf16[36,3,384,256]{3,2,1,0:T(8,128)(2,1)}, bf16[4608,384]{1,0:T(8,128)(2,1)}, f32[4608,384]{1,0:T(8,128)...) custom-call(bf16[4096,384]{1,0:T(8,128)(2,1)} %bitcast.154, ...), custom_call_target="tpu_custom_call" | custom-call | tf_op jit(solution)/shard_map/block_forward/pallas_call | solution.py:184
  209.1 94.5 %block_forward.3 = (bf16[4096,1152]{1,0:T(8,128)(2,1)}, bf16[36,3,384,256]{3,2,1,0:T(8,128)(2,1)}, bf16[4608,384]{1,0:T(8,128)(2,1)}, f32[4608,384]{1,0:T(8,128)...) custom-call(f32[4608,384]{1,0:T(8,128)} %get-tuple-element.53.x_new.x_old.x, ...), custom_call_target="tpu_custom_call" | custom-call | tf_op jit(solution)/shard_map/block_forward/pallas_call | solution.py:184
  303.6 41.2 %feed_back.2 = (f32[4096,384]{1,0:T(8,128)}, bf16[4096,384]{1,0:T(8,128)(2,1)}, f32[384,1536]{1,0:T(8,128)}, f32[384,1536]{1,0:T(8,128)}, f32[384,384]{1,0:T(8,1...) custom-call(bf16[4096,384]{1,0:T(8,128)(2,1)} %bitcast.157, f32[4608,384]{1,0:T(8,128)} %get-tuple-element.59.mid, ...), custom_call_target="tpu_custom_call" | custom-call | tf_op jit(solution)/shard_map/feed_back/pallas_call | solution.py:283
  344.8 50.5 %attend_back.2 = (f32[4352,384]{1,0:T(8,128)}, f32[384,1152]{1,0:T(8,128)}, f32[3,384,256]{2,1,0:T(8,128)}, f32[4,8,768]{2,1,0:T(8,128)}, f32[2,8,384]{2,1,0:T(8,128)}) custom-call(bf16[4096,1152]{1,0:T(8,128)(2,1)} %get-tuple-element.57.prev.cur.nxt, bf16[4096,1152]{1,0:T(8,128)(2,1)} %get-tuple-element.57.prev.cur.nxt, ...), custom_call_target="tpu_custom_call" | custom-call | tf_op jit(solution)/shard_map/attend_back/pallas_call | solution.py:412
  395.3 40.8 %feed_back.3 = (f32[4096,384]{1,0:T(8,128)}, bf16[4096,384]{1,0:T(8,128)(2,1)}, f32[384,1536]{1,0:T(8,128)}, f32[384,1536]{1,0:T(8,128)}, f32[384,384]{1,0:T(8,1...) custom-call(f32[4352,384]{1,0:T(8,128)} %get-tuple-element.65.gx, f32[4608,384]{1,0:T(8,128)} %get-tuple-element.66.mid, ...), custom_call_target="tpu_custom_call" | custom-call | tf_op jit(solution)/shard_map/feed_back/pallas_call | solution.py:283
  436.2 51.4 %attend_back.3 = (bf16[4352,384]{1,0:T(8,128)(2,1)}, f32[384,1152]{1,0:T(8,128)}, f32[3,384,256]{2,1,0:T(8,128)}, f32[4,8,768]{2,1,0:T(8,128)}, f32[2,8,384]{2,1,0:T(8,128)}) custom-call(bf16[4096,1152]{1,0:T(8,128)(2,1)} %get-tuple-element.55.prev.cur.nxt, bf16[4096,1152]{1,0:T(8,128)(2,1)} %get-tuple-element.55.prev.cur.nxt, ...), custom_call_target="tpu_custom_call" | custom-call | tf_op jit(solution)/shard_map/attend_back/pallas_call | solution.py:412
  488.6 4.3 pad_maximum_fusion.2
  492.9 2.5 pad_maximum_fusion.1
  504.2 3.5 reshape.172
  507.7 8.2 fusion.46
  524.4 3.5 reshape.174
  527.9 7.8 fusion.47
  542.0 2.3 copy.153
  544.4 2.5 slice.223
  560.8 123.4 %all-reduce.5 = (f32[2,384]{1,0:T(2,128)}, f32[2,384]{1,0:T(2,128)}, f32[2,6,567]{2,1,0:T(8,128)S(1)}, f32[2,384]{1,0:T(2,128)}, f32[2,384]{1,0:T(2,128)}, /*ind...) all-reduce(f32[2,384]{1,0:T(2,128)S(1)} %pad_maximum_fusion.11, ...), channel_id=1, replica_groups=mesh['img'=16,'band'=2] {'img','band'}, use_global_device_ids=true, to_apply=%region_2.3 | all-reduce | flops 14484 | bytes 115872 | tf_op jit(solution)/shard_map/psum | solution.py:665
  692.5 2.7 bitcast_dynamic-update-slice_fusion
  695.3 2.7 bitcast_dynamic-update-slice_fusion.4
  698.0 102.2 %all-reduce.9.cloned.1.call-done = (f32[2,384,1152]{2,1,0:T(8,128)}, f32[2,384,768]{2,1,0:T(8,128)}, f32[2,384,384]{2,1,0:T(8,128)}, f32[2,384,1536]{2,1,0:T(8,128)}, f32[2,1536,384]{1,2,0:T(8,128)}) async-done(((f32[2,384,1152]{2,1,0:T(8,128)}, f32[2,384,768]{2,1,0:T(8,128)}, f32[2,384,384]{2,1,0:T(8,128)}, f32[2,384,1536]{2,1,0:T(8,128)}, f32[2,1536,384]{1,2,0:T(8,128)}), (f32[2,384,1152]{2,1,0:T(8,128)}, ...) | async-done | bytes 16515088 | tf_op jit(solution)/shard_map/psum | solution.py:665
  800.2 6.2 copy.133
  (242 shorter events, 101.5 us)
Async XLA Ops:
  7.2 5.9 copy-start.14
  7.2 793.0 %all-reduce.9.cloned.1.call-start = ((), (), s32[]{:S(2)}) async-start(), calls=%async_computation | async-start | bytes 33030144 | tf_op jit(solution)/shard_map/psum | solution.py:665
  10.1 4.3 copy-start.64
  10.1 8.4 %copy-start.45 = (s32[8,32,32]{2,1,0:T(8,128)S(1)}, s32[8,32,32]{2,1,0:T(8,128)}, u32[]{:S(2)}) copy-start(s32[8,32,32]{2,1,0:T(8,128)} %param.20) | copy-start | bytes 98308
  10.1 98.3 %collective-permute-start = (bf16[4,512,384]{2,1,0:T(8,128)(2,1)}, bf16[4,512,384]{2,1,0:T(8,128)(2,1)}, u32[]{:S(2)}, u32[]{:S(2)}) collective-permute-start(bf16[4,512,384]{2,1,0:T(8,128)(2,1)} %dynamic-slice_bitcast_fusion.3), channel_id=1, source_target_pairs={{0,1},{1,0},{2,3},{3,2},{4,5},{5,4},{6,7},{7,6},{8,9},{9,8},{10,11... | collective-permute-start | bytes 4718600 | tf_op jit(solution)/shard_map/ppermute | solution.py:544
  13.1 8.0 copy-start.50
  13.1 8.0 copy-start.62
  14.4 94.1 %collective-permute-start.2 = (bf16[4,512,384]{2,1,0:T(8,128)(2,1)}, bf16[4,512,384]{2,1,0:T(8,128)(2,1)}, u32[]{:S(2)}, u32[]{:S(2)}) collective-permute-start(bf16[4,512,384]{2,1,0:T(8,128)(2,1)} %dynamic-slice_bitcast_fusion.1), channel_id=1, source_target_pairs={{0,1},{1,0},{2,3},{3,2},{4,5},{5,4},{6,7},{7,6},{8,9},{9,8},{10,11... | collective-permute-start | bytes 4718600 | tf_op jit(solution)/shard_map/ppermute | solution.py:544
  14.6 3.8 copy-start.41
  14.7 3.8 copy-start.43
  66.5 3.8 copy-start.46
  66.5 3.8 copy-start.47
  66.5 3.8 copy-start.48
  95.6 3.8 copy-start.13
  97.0 4.3 copy-start.42
  97.0 4.3 copy-start.44
  436.2 52.3 %copy-start.34 = (f32[4,8,768]{2,1,0:T(8,128)S(1)}, f32[4,8,768]{2,1,0:T(8,128)}, u32[]{:S(2)}) copy-start(f32[4,8,768]{2,1,0:T(8,128)} %get-tuple-element.78) | copy-start | bytes 294916
  436.2 52.4 %copy-start.22 = (f32[384,1536]{1,0:T(8,128)S(1)}, f32[384,1536]{1,0:T(8,128)}, u32[]{:S(2)}) copy-start(f32[384,1536]{1,0:T(8,128)} %get-tuple-element.90) | copy-start | bytes 7077892
  488.6 4.3 copy-start.21
  488.6 4.3 copy-start.23
  520.1 4.2 copy-start.29
  539.9 4.4 copy-start.52
  544.4 5.8 copy-start.17
  548.2 144.3 %collective-permute-start.3 = (bf16[4,512,384]{2,1,0:T(8,128)(2,1)}, bf16[4,512,384]{2,1,0:T(8,128)(2,1)}, u32[]{:S(2)}, u32[]{:S(2)}) collective-permute-start(bf16[4,512,384]{2,1,0:T(8,128)(2,1)} %dynamic-slice_bitcast_fusion), channel_id=1, source_target_pairs={{0,1},{1,0},{2,3},{3,2},{4,5},{5,4},{6,7},{7,6},{8,9},{9,8},{10,11... | collective-permute-start | bytes 4718600 | tf_op jit(solution)/shard_map/ppermute | solution.py:555
  550.2 3.8 copy-start.7
  550.5 5.8 copy-start.2
  550.6 3.9 copy-start.4
  550.6 4.4 copy-start.5
  551.9 143.4 %collective-permute-start.1 = (bf16[4,512,384]{2,1,0:T(8,128)(2,1)}, bf16[4,512,384]{2,1,0:T(8,128)(2,1)}, u32[]{:S(2)}, u32[]{:S(2)}) collective-permute-start(bf16[4,512,384]{2,1,0:T(8,128)(2,1)} %dynamic-slice_bitcast_fusion.2), channel_id=1, source_target_pairs={{0,1},{1,0},{2,3},{3,2},{4,5},{5,4},{6,7},{7,6},{8,9},{9,8},{10,11... | collective-permute-start | bytes 4718600 | tf_op jit(solution)/shard_map/ppermute | solution.py:555
  800.2 6.2 copy-start.12
  806.4 6.5 slice-start
  806.4 6.5 slice-start.1
  (40 other events, 82.5 us)
Sparse Core Ops, SparseCore 0:
  502.3 297.8 all-reduce.8

commit v2 on v1

v2 whole, which is shorter than its diff:
```python
import functools
import math

import jax
import jax.numpy as jnp
from jax import lax
from jax.experimental import pallas as pl
from jax.experimental.pallas import tpu as pltpu
from jax.sharding import PartitionSpec as P

WIN = 4
CHUNK = 256
QBLOCK = 128
KWIN = 384
HALO = 128
FEED = 512

EXACT = lax.Precision.HIGHEST
NEG_FILL = -1000000000.0
EPSILON = 1e-06
GELU_A = math.sqrt(2.0 / math.pi)
GELU_B = 0.044715 * GELU_A
VMEM_BYTES = 58 * 1024 * 1024

F32 = jnp.float32
BF16 = jnp.bfloat16


def dot(a, b):
    return jnp.dot(a, b, preferred_element_type=F32)


def dot_nt(a, b):
    return lax.dot_general(a, b, (((1,), (1,)), ((), ())), preferred_element_type=F32)


def norm_stats(v):
    mean = jnp.mean(v, axis=-1, keepdims=True)
    centered = v - mean
    inverse = lax.rsqrt(jnp.mean(centered * centered, axis=-1, keepdims=True) + EPSILON)
    return centered * inverse, inverse


def norm_back(gy, xh, inverse, gain):
    gs = gy * gain
    return inverse * (
        gs - jnp.mean(gs, axis=-1, keepdims=True) - xh * jnp.mean(gs * xh, axis=-1, keepdims=True)
    )


def row_sums(v):
    rows, cols = v.shape
    return jnp.sum(v.reshape(rows // 8, 8, cols), axis=0)


def split_heads(block):
    lane = lax.broadcasted_iota(jnp.int32, block.shape, 1)
    zero = jnp.zeros_like(block)
    first = lane < block.shape[1] // 2
    return jnp.concatenate(
        [jnp.where(first, block, zero), jnp.where(first, zero, block)], axis=0
    )


def join_heads(product):
    half = product.shape[0] // 2
    width = product.shape[1] // 2
    return jnp.concatenate([product[:half, :width], product[half:, width:]], axis=0).T


def fold(v, op):
    return op(v.reshape(v.shape[0] // 8, 8, v.shape[1]), axis=0)


def unroll_bias(rows, bias):
    pairs, keys, lanes = bias.shape
    grid_cols = QBLOCK // 4
    key_rows = keys // grid_cols
    lane = lax.broadcasted_iota(jnp.int32, (grid_cols, QBLOCK), 1)
    even = lax.rem(lane // grid_cols, 2) == 0
    for pair in range(pairs):
        for head in range(2):
            for key_row in range(key_rows):
                turned = [
                    pltpu.roll(
                        jnp.broadcast_to(
                            rows[pl.ds(((pair * 2 + head) * 2 + odd) * key_rows + key_row, 1), :],
                            (grid_cols, QBLOCK),
                        ),
                        0,
                        1,
                        stride=1,
                        stride_axis=0,
                    )
                    for odd in range(2)
                ]
                bias[
                    pair,
                    key_row * grid_cols : (key_row + 1) * grid_cols,
                    head * QBLOCK : (head + 1) * QBLOCK,
                ] = jnp.where(even, turned[0], turned[1])


def gather_bias(grads):
    pairs, keys, lanes = grads.shape
    grid_cols = QBLOCK // 4
    lane = lax.broadcasted_iota(jnp.int32, (keys, QBLOCK), 1)
    column = lax.rem(lax.broadcasted_iota(jnp.int32, (keys, QBLOCK), 0), grid_cols)
    parity = lax.rem(lane // grid_cols, 2)
    sums = []
    for pair in range(pairs):
        for head in range(2):
            for odd in range(2):
                v = grads[pair, :, head * QBLOCK : (head + 1) * QBLOCK]
                v = jnp.where(parity == odd, v, 0.0)
                for bit in (1, 2, 4, 8, 16):
                    turned = pltpu.roll(v, QBLOCK - bit, 1)
                    v = jnp.where(lax.rem(column // bit, 2) == 1, turned, v)
                sums.append(jnp.sum(v.reshape(keys // grid_cols, grid_cols, QBLOCK), axis=1))
    return jnp.concatenate(sums, axis=0)


def forward_kernel(
    pairs,
    x_new,
    x_old,
    tproj,
    mask,
    bias_rows,
    gain1,
    shift1,
    wqkv,
    wo,
    bo,
    gain2,
    shift2,
    w1,
    b1,
    w2,
    b2,
    qkv_out,
    p_out,
    o_out,
    mid_out,
    act_out,
    slope_out,
    x_out,
    bias,
    q_ring,
    k_ring,
    vt_ring,
    o_ring,
    s_scr,
):
    step = pl.program_id(0)
    width = x_new.shape[1]

    @pl.when(step == 0)
    def _():
        unroll_bias(bias_rows, bias)
        q_ring[...] = jnp.zeros_like(q_ring)
        k_ring[...] = jnp.zeros_like(k_ring)
        vt_ring[...] = jnp.zeros_like(vt_ring)
        o_ring[...] = jnp.zeros_like(o_ring)

    attended = o_ring[...]
    mid = x_old[...].astype(F32) + (dot(attended, wo[...]) + bo[...])
    mid_out[...] = mid
    xh2, _ = norm_stats(mid)
    c = (xh2 * gain2[...] + shift2[...]).astype(BF16)
    parts = 2 * pairs
    tile = w1.shape[1] // parts

    def feed(part):
        cols = slice(part * tile, (part + 1) * tile)
        whole = dot(c, w1[:, cols])
        for low in range(0, CHUNK, 64):
            u = whole[low : low + 64] + b1[:, cols]
            u2 = u * u
            t = jnp.tanh(u * (GELU_A + GELU_B * u2))
            h = 0.5 + 0.5 * t
            e = u * h
            act_out[low : low + 64, cols] = e.astype(BF16)
            slope_out[low : low + 64, cols] = (
                h + (e * (1.0 - t)) * (GELU_A + (3.0 * GELU_B) * u2)
            ).astype(BF16)

    queries = q_ring[...]
    xh1, _ = norm_stats(x_new[...].astype(F32))
    a = (xh1 * gain1[...] + shift1[...]).astype(BF16)
    qkv = (dot(a, wqkv[...]) + tproj[0]).astype(BF16)
    qkv_out[...] = qkv
    q_ring[...] = qkv[:, :width] * jnp.asarray(0.125, BF16)
    k_ring[:HALO, :] = k_ring[CHUNK : CHUNK + HALO, :]
    k_ring[HALO : HALO + CHUNK, :] = k_ring[HALO + CHUNK :, :]
    k_ring[HALO + CHUNK :, :] = qkv[:, width : 2 * width]
    vt_ring[:, :HALO] = vt_ring[:, CHUNK : CHUNK + HALO]
    vt_ring[:, HALO : HALO + CHUNK] = vt_ring[:, HALO + CHUNK :]
    vt_ring[:, HALO + CHUNK :] = qkv[:, 2 * width :].T

    key_index = lax.broadcasted_iota(jnp.int32, (KWIN, QBLOCK), 0)
    query_index = lax.broadcasted_iota(jnp.int32, (KWIN, QBLOCK), 1)
    diagonal = key_index == query_index + HALO
    extras = []
    for blk in range(CHUNK // QBLOCK):
        line = mask[0, :, blk * QBLOCK : blk * QBLOCK + KWIN]
        column = jnp.broadcast_to(line, (QBLOCK, KWIN)).T
        extras.append(jnp.where(diagonal, 0.0, column))
    todo = [(blk, pair) for blk in range(CHUNK // QBLOCK) for pair in range(pairs)]
    cells = [(k * 128, h * 128) for k in range(KWIN // 128) for h in range(2)]
    tops = {}

    def score(blk, pair):
        low = blk * QBLOCK
        feat = slice(pair * 128, (pair + 1) * 128)
        split_q = split_heads(queries[low : low + QBLOCK, feat])
        best = [None, None]
        for k in range(0, KWIN, 128):
            s = dot_nt(k_ring[low + k : low + k + 128, feat], split_q)
            for h in range(2):
                lane = slice(h * 128, h * 128 + 128)
                v = s[:, lane] + bias[pair, k : k + 128, lane] + extras[blk][k : k + 128]
                s_scr[blk, pair, k : k + 128, lane] = v
                top = fold(v, jnp.max)
                best[h] = top if best[h] is None else jnp.maximum(best[h], top)
        tops[blk, pair] = [jnp.max(v, axis=0, keepdims=True) for v in best]

    def soften(blk, pair):
        sums = [None, None]
        for k, lane in cells:
            at = (blk, pair, slice(k, k + 128), slice(lane, lane + 128))
            h = lane // 128
            ex = jnp.exp(s_scr[at] - tops[blk, pair][h])
            total = fold(ex, jnp.sum)
            sums[h] = total if sums[h] is None else sums[h] + total
            s_scr[at] = ex
        inverse = [1.0 / jnp.sum(v, axis=0, keepdims=True) for v in sums]
        for k, lane in cells:
            at = (blk, pair, slice(k, k + 128), slice(lane, lane + 128))
            p_out[at] = (s_scr[at] * inverse[lane // 128]).astype(BF16)

    def attend(blk, pair):
        low = blk * QBLOCK
        feat = slice(pair * 128, (pair + 1) * 128)
        o = join_heads(dot(vt_ring[feat, low : low + KWIN], p_out[blk, pair])).astype(BF16)
        o_ring[low : low + QBLOCK, feat] = o
        o_out[low : low + QBLOCK, feat] = o

    for i in range(len(todo) + 2):
        if i < len(todo):
            score(*todo[i])
            feed(i)
        if 1 <= i <= len(todo):
            soften(*todo[i - 1])
        if i >= 2:
            attend(*todo[i - 2])
    x_out[...] = (mid_out[...] + (dot(act_out[...], w2[...]) + b2[...])).astype(x_out.dtype)


def const_spec(shape):
    zeros = (0,) * len(shape)
    return pl.BlockSpec(shape, lambda g: zeros, pipeline_mode=pl.Buffered(1))


def forward_layer(x, x_lead, chunks, chunks_per_image, tproj, mask, bias_rows, weights, out_dtype):
    width = x.shape[1]
    hidden = weights[7].shape[1]
    pairs = width // 128
    steps = chunks + 2

    def at(lead, least=0):
        def index(g):
            return jnp.clip(g - lead, least, chunks - 1)

        return index

    new_at, attn_at, old_at = at(0), at(1), at(2)
    row = pl.BlockSpec((CHUNK, width), lambda g: (g, 0))
    wide = pl.BlockSpec((CHUNK, hidden), lambda g: (g, 0))
    rows = steps * CHUNK
    gain1, shift1, wqkv, wo, bo, gain2, shift2, w1, b1, w2, b2 = weights
    consts = [gain1, shift1, wqkv, wo, bo, gain2, shift2, w1, b1, w2, b2]
    return pl.pallas_call(
        functools.partial(forward_kernel, pairs),
        grid=(steps,),
        in_specs=[
            pl.BlockSpec((CHUNK, width), lambda g: (new_at(g) + x_lead, 0)),
            pl.BlockSpec((CHUNK, width), lambda g: (old_at(g) + x_lead, 0)),
            pl.BlockSpec((1, 1, 3 * width), lambda g: (new_at(g) // chunks_per_image, 0, 0)),
            pl.BlockSpec((1, 1, CHUNK + 2 * HALO), lambda g: (attn_at(g), 0, 0)),
            const_spec(bias_rows.shape),
        ]
        + [const_spec(w.shape) for w in consts],
        out_specs=[
            pl.BlockSpec((CHUNK, 3 * width), lambda g: (new_at(g), 0)),
            pl.BlockSpec((CHUNK // QBLOCK, pairs, KWIN, 2 * QBLOCK), lambda g: (g, 0, 0, 0)),
            pl.BlockSpec((CHUNK, width), lambda g: (g + 1, 0)),
            row,
            wide,
            wide,
            row,
        ],
        out_shape=[
            jax.ShapeDtypeStruct((chunks * CHUNK, 3 * width), BF16),
            jax.ShapeDtypeStruct((steps * (CHUNK // QBLOCK), pairs, KWIN, 2 * QBLOCK), BF16),
            jax.ShapeDtypeStruct((rows + CHUNK, width), BF16),
            jax.ShapeDtypeStruct((rows, width), F32),
            jax.ShapeDtypeStruct((rows, hidden), BF16),
            jax.ShapeDtypeStruct((rows, hidden), BF16),
            jax.ShapeDtypeStruct((rows, width), out_dtype),
        ],
        scratch_shapes=[
            pltpu.VMEM((pairs, KWIN, 2 * QBLOCK), F32),
            pltpu.VMEM((CHUNK, width), BF16),
            pltpu.VMEM((HALO + 2 * CHUNK, width), BF16),
            pltpu.VMEM((width, HALO + 2 * CHUNK), BF16),
            pltpu.VMEM((CHUNK, width), BF16),
            pltpu.VMEM((CHUNK // QBLOCK, pairs, KWIN, 2 * QBLOCK), F32),
        ],
        compiler_params=pltpu.CompilerParams(vmem_limit_bytes=VMEM_BYTES),
        name="block_forward",
    )(x, x, tproj, mask, bias_rows, *consts)


def put_tiles(out, first, acc):
    width = acc.shape[0]
    for j in range(acc.shape[1] // 128):
        at = (first + j) * width
        out[at : at + width, :] = acc[:, j * 128 : (j + 1) * 128].astype(out.dtype)


def put_rows(out, at, vectors):
    lines = [v[:, j : j + 128] for v in vectors for j in range(0, v.shape[1], 128)]
    lines += [jnp.zeros((1, 128), F32)] * (-len(lines) % 16)
    out[at : at + len(lines), :] = jnp.concatenate(lines, axis=0).astype(out.dtype)


def feed_back_kernel(
    gx,
    mid,
    act,
    slope,
    o,
    gain2,
    shift2,
    w1,
    w2,
    wo,
    gmid_out,
    go_out,
    grads_out,
    gw2t,
    gw1,
    gwo,
    sums,
    gb1,
    gu_scr,
):
    step = pl.program_id(0)

    @pl.when(step == 0)
    def _():
        for ref in (gw2t, gw1, gwo, sums, gb1):
            ref[...] = jnp.zeros_like(ref)

    grad = gx[...].astype(F32)
    gr = grad.astype(BF16)
    gr_t = gr.T
    xh, inverse = norm_stats(mid[...])
    c_t = (xh * gain2[...] + shift2[...]).astype(BF16).T
    hidden = act.shape[1]
    tile = 256
    for low in range(0, hidden, tile):
        cols = slice(low, low + tile)
        ge = dot_nt(gr, w2[cols, :])
        gu = (ge * slope[:, cols].astype(F32)).astype(BF16)
        gu_scr[:, cols] = gu
        gb1[:, cols] += row_sums(gu.astype(F32))
        gw2t[:, cols] += dot(gr_t, act[:, cols])
        gw1[:, cols] += dot(c_t, gu)
    gc = dot_nt(gu_scr[...], w1[...])
    gmid = grad + norm_back(gc, xh, inverse, gain2[...])
    gmid_out[...] = gmid
    gb = gmid.astype(BF16)
    gwo[...] += dot(o[...].T, gb)
    go_out[...] = dot_nt(gb, wo[...]).astype(BF16)
    sums[0] += row_sums(gr.astype(F32))
    sums[1] += row_sums(gb.astype(F32))
    sums[2] += row_sums(gc * xh)
    sums[3] += row_sums(gc)

    @pl.when(step == pl.num_programs(0) - 1)
    def _():
        tiles = hidden // 128
        put_tiles(grads_out, 0, gw2t)
        put_tiles(grads_out, tiles, gw1)
        put_tiles(grads_out, 2 * tiles, gwo)
        whole = [jnp.sum(sums[i], axis=0, keepdims=True) for i in range(4)]
        whole.append(jnp.sum(gb1[...], axis=0, keepdims=True))
        at = (2 * tiles + gwo.shape[1] // 128) * gwo.shape[0]
        put_rows(grads_out, at, whole)


def feed_rows(width, hidden):
    tiles = (2 * hidden + width) // 128
    return tiles * width, -(-(4 * width + hidden) // 128 // 16) * 16


def feed_back(gx, gx_lead, patches, mid, act, slope, o, gain2, shift2, w1, w2, wo):
    width = mid.shape[1]
    hidden = act.shape[1]

    def rows(cols, lead):
        return pl.BlockSpec((FEED, cols), lambda g: (g + lead, 0))

    grad_rows = sum(feed_rows(width, hidden))
    return pl.pallas_call(
        feed_back_kernel,
        grid=(patches // FEED,),
        in_specs=[
            rows(width, gx_lead),
            rows(width, 1),
            rows(hidden, 1),
            rows(hidden, 1),
            rows(width, 1),
        ]
        + [const_spec(w.shape) for w in (gain2, shift2, w1, w2, wo)],
        out_specs=[rows(width, 0), rows(width, 0), const_spec((grad_rows, 128))],
        out_shape=[
            jax.ShapeDtypeStruct((patches, width), F32),
            jax.ShapeDtypeStruct((patches, width), BF16),
            jax.ShapeDtypeStruct((grad_rows, 128), BF16),
        ],
        scratch_shapes=[
            pltpu.VMEM((width, hidden), F32),
            pltpu.VMEM((width, hidden), F32),
            pltpu.VMEM((width, width), F32),
            pltpu.VMEM((4, 8, width), F32),
            pltpu.VMEM((8, hidden), F32),
            pltpu.VMEM((FEED, hidden), BF16),
        ],
        compiler_params=pltpu.CompilerParams(vmem_limit_bytes=VMEM_BYTES),
        name="feed_back",
    )(gx, mid, act, slope, o, gain2, shift2, w1, w2, wo)


def attend_back_kernel(
    pairs,
    chunks,
    chunks_per_image,
    prev,
    cur,
    nxt,
    p_in,
    go_in,
    o_in,
    gmid,
    x,
    gain1,
    shift1,
    wqkv,
    gx_out,
    gtime,
    grads_out,
    gwqkv,
    gbias,
    sums,
    gq_ring,
    gkv_ring,
    gs_scr,
):
    step = pl.program_id(0)
    width = x.shape[1]

    @pl.when(step == 0)
    def _():
        for ref in (gwqkv, gbias, gtime, sums, gq_ring, gkv_ring):
            ref[...] = jnp.zeros_like(ref)

    gq_old = gq_ring[...]
    live = (step < chunks).astype(BF16)
    go = go_in[...] * live
    qkv = cur[...]
    queries = qkv[:, :width] * jnp.asarray(0.125, BF16)
    keys = jnp.concatenate(
        [prev[:, width : 2 * width], qkv[:, width : 2 * width], nxt[:, width : 2 * width]], axis=0
    )
    keys_t = keys.T
    values = jnp.concatenate([prev[:, 2 * width :], qkv[:, 2 * width :], nxt[:, 2 * width :]], axis=0)
    dots = (go.astype(F32) * o_in[...].astype(F32)).T
    blocks = CHUNK // QBLOCK
    todo = [(blk, pair) for pair in range(pairs) for blk in range(blocks)]

    def spread(blk, pair):
        low = blk * QBLOCK
        feat = slice(pair * 128, (pair + 1) * 128)
        split_go = split_heads(go[low : low + QBLOCK, feat])
        own = dots[feat, low : low + QBLOCK]
        row_dot = [jnp.sum(own[h * 64 : h * 64 + 64], axis=0, keepdims=True) for h in range(2)]
        for k in range(0, KWIN, 128):
            gp = dot_nt(values[low + k : low + k + 128, feat], split_go)
            for h in range(2):
                lane = slice(h * 128, h * 128 + 128)
                gs = p_in[blk, pair, k : k + 128, lane].astype(F32) * (gp[:, lane] - row_dot[h])
                gbias[pair, k : k + 128, lane] += gs
                gs_scr[blk, pair, k : k + 128, lane] = gs.astype(BF16)

    def pull(blk, pair):
        low = blk * QBLOCK
        feat = slice(pair * 128, (pair + 1) * 128)
        vfeat = slice(width + pair * 128, width + (pair + 1) * 128)
        gs = gs_scr[blk, pair]
        at = HALO + low
        gkv_ring[at : at + KWIN, feat] += dot(gs, split_heads(queries[low : low + QBLOCK, feat]))
        gkv_ring[at : at + KWIN, vfeat] += dot(
            p_in[blk, pair], split_heads(go[low : low + QBLOCK, feat])
        )
        gq = join_heads(dot(keys_t[feat, low : low + KWIN], gs)) * 0.125
        gq_ring[low : low + QBLOCK, feat] = gq.astype(BF16)

    for i in range(len(todo) + 1):
        if i < len(todo):
            spread(*todo[i])
        if i >= 1:
            pull(*todo[i - 1])

    done = jnp.concatenate([gq_old, gkv_ring[:CHUNK, :].astype(BF16)], axis=1)
    gkv_ring[:CHUNK, :] = gkv_ring[CHUNK : 2 * CHUNK, :]
    gkv_ring[CHUNK : CHUNK + HALO, :] = gkv_ring[2 * CHUNK :, :]
    gkv_ring[CHUNK + HALO :, :] = jnp.zeros((CHUNK, 2 * width), F32)
    xh, inverse = norm_stats(x[...].astype(F32))
    a = (xh * gain1[...] + shift1[...]).astype(BF16)
    gwqkv[...] += dot(a.T, done)
    ga = dot_nt(done, wqkv[...])
    gx_out[...] = (gmid[...] + norm_back(ga, xh, inverse, gain1[...])).astype(gx_out.dtype)
    sums[0] += row_sums(ga * xh)
    sums[1] += row_sums(ga)
    first = lax.rem(step + chunks_per_image - 1, chunks_per_image) == 0
    before = jnp.where(first, jnp.zeros(gtime.shape[1:], F32), gtime[0])
    summed = row_sums(done.astype(F32))
    gtime[0] = before + jnp.concatenate([summed[:, :width], summed[:, 2 * width :]], axis=1)

    @pl.when(step == chunks)
    def _():
        put_tiles(grads_out, 0, gwqkv)
        tiles = gwqkv.shape[1] // 128
        lines = attend_rows(width)[2]
        grads_out[tiles * width : tiles * width + lines, :] = gather_bias(gbias).astype(BF16)
        put_rows(
            grads_out,
            tiles * width + lines,
            [jnp.sum(sums[i], axis=0, keepdims=True) for i in range(2)],
        )


def attend_rows(width):
    lines = 2 * (width // 128) * (KWIN * 4 // QBLOCK) * 2
    small = -(-2 * width // 128 // 16) * 16
    return 3 * width // 128 * width, 3 * width // 128 * width + lines + small, lines


def attend_back(
    qkv, p, go, o, gmid, x, x_lead, chunks, chunks_per_image, gain1, shift1, wqkv, out_dtype
):
    width = x.shape[1]
    pairs = width // 128
    steps = chunks + 1
    halves = CHUNK // HALO

    def now(g):
        return jnp.minimum(g, chunks - 1)

    def late(g):
        return jnp.maximum(g - 1, 0)

    def rows(cols, lead, index):
        return pl.BlockSpec((CHUNK, cols), lambda g: (index(g) + lead, 0))

    images = chunks // chunks_per_image
    grad_rows = attend_rows(width)[1]
    return pl.pallas_call(
        functools.partial(attend_back_kernel, pairs, chunks, chunks_per_image),
        grid=(steps,),
        in_specs=[
            pl.BlockSpec((HALO, 3 * width), lambda g: (jnp.maximum(halves * now(g) - 1, 0), 0)),
            rows(3 * width, 0, now),
            pl.BlockSpec(
                (HALO, 3 * width),
                lambda g: (jnp.minimum(halves * (now(g) + 1), halves * chunks - 1), 0),
            ),
            pl.BlockSpec(
                (CHUNK // QBLOCK, pairs, KWIN, 2 * QBLOCK), lambda g: (now(g) + 1, 0, 0, 0)
            ),
            rows(width, 0, now),
            rows(width, 2, now),
            rows(width, 0, late),
            rows(width, x_lead, late),
        ]
        + [const_spec(w.shape) for w in (gain1, shift1, wqkv)],
        out_specs=[
            rows(width, 1, lambda g: g),
            pl.BlockSpec((1, 8, 2 * width), lambda g: (late(g) // chunks_per_image, 0, 0)),
            const_spec((grad_rows, 128)),
        ],
        out_shape=[
            jax.ShapeDtypeStruct(((steps + 1) * CHUNK, width), out_dtype),
            jax.ShapeDtypeStruct((images, 8, 2 * width), F32),
            jax.ShapeDtypeStruct((grad_rows, 128), BF16),
        ],
        scratch_shapes=[
            pltpu.VMEM((width, 3 * width), F32),
            pltpu.VMEM((pairs, KWIN, 2 * QBLOCK), F32),
            pltpu.VMEM((2, 8, width), F32),
            pltpu.VMEM((CHUNK, width), BF16),
            pltpu.VMEM((2 * CHUNK + HALO, 2 * width), F32),
            pltpu.VMEM((CHUNK // QBLOCK, pairs, KWIN, 2 * QBLOCK), BF16),
        ],
        compiler_params=pltpu.CompilerParams(vmem_limit_bytes=VMEM_BYTES),
        name="attend_back",
    )(qkv, qkv, qkv, p, go, o, gmid, x, gain1, shift1, wqkv)


def share_rows(rows):
    return max(n for n in range(16, 257, 16) if rows % n == 0)


def add_rows(total, at, others, rows):
    share = share_rows(rows)

    def one(i, carry):
        low = pl.multiple_of(i * share, 16)
        here = pl.ds(pl.multiple_of(at + low, 16), share)
        v = total[here, :].astype(F32)
        for ref, row in others:
            v = v + ref[pl.ds(pl.multiple_of(row + low, 16), share), :].astype(F32)
        total[here, :] = v.astype(total.dtype)
        return carry

    lax.fori_loop(0, rows // share, one, 0)


def cut(ref, at, rows):
    return ref.at[pl.ds(pl.multiple_of(at, 16), rows), :]


class Places:
    def __init__(self, plan):
        self.xs, self.bs, self.zs = plan
        self.img = lax.axis_index("img")
        self.b = lax.axis_index("band")
        self.c = lax.rem(self.img, 2)
        self.x = lax.rem(self.img // 2, self.xs)
        self.z = self.img // (2 * self.xs)

    def core(self, by):
        return (self.img + 1 - 2 * self.c, self.b)

    def along_x(self, by):
        return ((self.z * self.xs + lax.rem(self.x + by, self.xs)) * 2 + self.c, self.b)

    def along_b(self, by):
        return (self.img, lax.rem(self.b + by, self.bs))

    def along_z(self, by):
        return ((lax.rem(self.z + by, self.zs) * self.xs + self.x) * 2 + self.c, self.b)

    def greet(self):
        barrier = pltpu.get_barrier_semaphore()
        peers = [self.core(1)]
        peers += [self.along_x(by) for by in range(1, self.xs)]
        peers += [self.along_b(by) for by in range(1, self.bs)]
        peers += [self.along_z(by) for by in range(1, self.zs)]
        for peer in peers:
            pl.semaphore_signal(barrier, inc=1, device_id=peer, device_id_type=pl.DeviceIdType.MESH)
        pl.semaphore_wait(barrier, len(peers))


class Lane:
    def __init__(self, plan, sems):
        self.plan, self.sems, self.steps = plan, sems, []

    def add(self, copies, then=None):
        count = [0, 0]
        here = Places(self.plan)
        for src, dst, peer in copies(here):
            count[peer is None] += 1
        base = (self.sems.sent, self.sems.kept)
        self.sems.sent += count[0]
        self.sems.kept += count[1]
        self.steps.append((copies, then, base))

    def described(self, step):
        copies, _, (sent, kept) = self.steps[step]
        made = []
        for src, dst, peer in copies(Places(self.plan)):
            if peer is None:
                made.append(pltpu.make_async_copy(src, dst, self.sems.own.at[kept]))
                kept += 1
            else:
                made.append(
                    pltpu.make_async_remote_copy(
                        src_ref=src,
                        dst_ref=dst,
                        send_sem=self.sems.send.at[sent],
                        recv_sem=self.sems.recv.at[sent],
                        device_id=peer,
                        device_id_type=pl.DeviceIdType.MESH,
                    )
                )
                sent += 1
        return made

    def part(self, i):
        if i > 0:
            for copy in self.described(i - 1):
                copy.wait()
            if self.steps[i - 1][1] is not None:
                self.steps[i - 1][1](Places(self.plan))
        if i < len(self.steps):
            for copy in self.described(i):
                copy.start()


class Sems:
    def __init__(self, send, recv, own):
        self.send, self.recv, self.own = send, recv, own
        self.sent = self.kept = 0


def scatter_lane(lane, grad, held, chunk=None):
    acc, r1, r2a, r2b, r3a, r3b, r4 = held
    xs, bs, zs = lane.plan
    half = grad.shape[0] // 2
    quarter = half // 2
    nx, nb, n2 = quarter // xs, quarter // bs, quarter // (xs * bs)
    n = n2 // zs

    def core_copies(at):
        return [
            (cut(grad, at.c * half, half), acc, None),
            (cut(grad, half - at.c * half, half), r1, at.core(1)),
        ]

    lane.add(core_copies, lambda at: add_rows(acc, 0, [(r1, 0)], half))

    def wide_copies(at):
        made = []
        for by in range(1, xs):
            there = lax.rem(at.x + by, xs)
            made.append((cut(acc, there * nx, nx), cut(r2a, (by - 1) * nx, nx), at.along_x(by)))
        for by in range(1, bs):
            there = quarter + lax.rem(at.b + by, bs) * nb
            made.append((cut(acc, there, nb), cut(r2b, (by - 1) * nb, nb), at.along_b(by)))
        return made

    def wide_add(at):
        add_rows(acc, at.x * nx, [(r2a, k * nx) for k in range(xs - 1)], nx)
        add_rows(acc, quarter + at.b * nb, [(r2b, k * nb) for k in range(bs - 1)], nb)

    lane.add(wide_copies, wide_add)

    def cross_copies(at):
        made = []
        for by in range(1, bs):
            there = at.x * nx + lax.rem(at.b + by, bs) * n2
            made.append((cut(acc, there, n2), cut(r3a, (by - 1) * n2, n2), at.along_b(by)))
        for by in range(1, xs):
            there = quarter + at.b * nb + lax.rem(at.x + by, xs) * n2
            made.append((cut(acc, there, n2), cut(r3b, (by - 1) * n2, n2), at.along_x(by)))
        return made

    def plane(at):
        return at.x * nx + at.b * n2, quarter + at.b * nb + at.x * n2

    def cross_add(at):
        first, second = plane(at)
        add_rows(acc, first, [(r3a, k * n2) for k in range(bs - 1)], n2)
        add_rows(acc, second, [(r3b, k * n2) for k in range(xs - 1)], n2)

    lane.add(cross_copies, cross_add)

    def deep_copies(at):
        made = []
        for by in range(1, zs):
            there = lax.rem(at.z + by, zs) * n
            for k, low in enumerate(plane(at)):
                slot = (2 * (by - 1) + k) * n
                made.append((cut(acc, low + there, n), cut(r4, slot, n), at.along_z(by)))
        return made

    def deep_add(at):
        for k, low in enumerate(plane(at)):
            add_rows(acc, low + at.z * n, [(r4, (2 * i + k) * n) for i in range(zs - 1)], n)

    lane.add(deep_copies, deep_add)

    def ends(at):
        return [cut(acc, low + at.z * n, n) for low in plane(at)]

    if chunk is None:
        return ends
    lane.add(lambda at: [(ref, cut(chunk, k * n, n), None) for k, ref in enumerate(ends(at))])


def collect_lane(lane, ends, out):
    xs, bs, zs = lane.plan
    half = out.shape[0] // 2
    quarter = half // 2
    nx, nb, n2 = quarter // xs, quarter // bs, quarter // (xs * bs)
    n = n2 // zs

    def plane(at):
        base = at.c * half
        return base + at.x * nx + at.b * n2, base + quarter + at.b * nb + at.x * n2

    def deep(at):
        made = []
        for ref, low in zip(ends(at), plane(at)):
            there = cut(out, low + at.z * n, n)
            made.append((ref, there, None))
            made += [(ref, there, at.along_z(by)) for by in range(1, zs)]
        return made

    def cross(at):
        first, second = plane(at)
        a, b = cut(out, first, n2), cut(out, second, n2)
        made = [(a, a, at.along_b(by)) for by in range(1, bs)]
        return made + [(b, b, at.along_x(by)) for by in range(1, xs)]

    def wide(at):
        a = cut(out, at.c * half + at.x * nx, nx)
        b = cut(out, at.c * half + quarter + at.b * nb, nb)
        made = [(a, a, at.along_x(by)) for by in range(1, xs)]
        return made + [(b, b, at.along_b(by)) for by in range(1, bs)]

    def core(at):
        whole = cut(out, at.c * half, half)
        return [(whole, whole, at.core(1))]

    for copies in (deep, cross, wide, core):
        lane.add(copies)


def extra_lane(lane, extra, out):
    xs, bs, zs = lane.plan
    rows = extra.shape[0]

    def deep(at):
        there = cut(out, (((at.c * xs + at.x) * bs + at.b) * zs + at.z) * rows, rows)
        return [(extra, there, None)] + [(extra, there, at.along_z(by)) for by in range(1, zs)]

    def cross(at):
        there = cut(out, ((at.c * xs + at.x) * bs + at.b) * zs * rows, zs * rows)
        return [(there, there, at.along_b(by)) for by in range(1, bs)]

    def wide(at):
        there = cut(out, (at.c * xs + at.x) * bs * zs * rows, bs * zs * rows)
        return [(there, there, at.along_x(by)) for by in range(1, xs)]

    def core(at):
        there = cut(out, at.c * xs * bs * zs * rows, xs * bs * zs * rows)
        return [(there, there, at.core(1))]

    for copies in (deep, cross, wide, core):
        lane.add(copies)


def bands_lane(lane, whole, lead, out):
    bs = lane.plan[1]
    rows, width = out.shape[2:]
    own = out.shape[1]

    def copies(at):
        made = []
        for by in range(bs):
            there = lax.rem(at.b + by, bs)
            for i in range(own):
                src = cut(whole, lead + (i * bs + there) * rows, rows)
                made.append((src, out.at[at.b, i], at.along_b(by) if by else None))
        return made

    lane.add(copies)


def link_plan():
    pairs = lax.axis_size("img") // 2
    xs = 2 if pairs % 2 == 0 else 1
    return xs, lax.axis_size("band"), pairs // xs


def held_shapes(plan, rows):
    xs, bs, zs = plan
    quarter = rows // 4
    sizes = [
        rows // 2,
        rows // 2,
        (xs - 1) * quarter // xs,
        (bs - 1) * quarter // bs,
        (bs - 1) * quarter // (xs * bs),
        (xs - 1) * quarter // (xs * bs),
        (zs - 1) * 2 * quarter // (xs * bs * zs),
    ]
    return [pltpu.VMEM((max(n, 16), 128), BF16) for n in sizes]


def sems_shapes(plan, lanes, moved=0):
    xs, bs, zs = plan
    count = lanes * (1 + 2 * (xs - 1 + bs - 1) + 2 * (zs - 1)) + moved
    return [
        pltpu.SemaphoreType.DMA((count,)),
        pltpu.SemaphoreType.DMA((count,)),
        pltpu.SemaphoreType.DMA((2 * lanes + moved + 1,)),
    ]


def final_kernel(plan, count, lead, *refs):
    grads, extra, whole = refs[:count], refs[count], refs[count + 1]
    outs, extra_out, bands_out = refs[count + 2 : 2 * count + 2], refs[2 * count + 2], refs[2 * count + 3]
    scratch = refs[2 * count + 4 :]
    sems = Sems(*scratch[-3:])
    each = 7
    Places(plan).greet()
    lanes = []
    for i in range(count):
        lane = Lane(plan, sems)
        ends = scatter_lane(lane, grads[i], scratch[i * each : (i + 1) * each])
        collect_lane(lane, ends, outs[i])
        lanes.append(lane)
    lane = Lane(plan, sems)
    extra_lane(lane, extra, extra_out)
    lanes.append(lane)
    late = Lane(plan, sems)
    bands_lane(late, whole, lead, bands_out)
    late.part(0)
    for i in range(max(len(lane.steps) for lane in lanes) + 1):
        for lane in lanes:
            if i <= len(lane.steps):
                lane.part(i)
    late.part(1)


def final_exchange(grads, extra, whole, lead, own, part):
    plan = link_plan()
    xs, bs, zs = plan
    count = len(grads)
    held = []
    for grad in grads:
        held += held_shapes(plan, grad.shape[0])
    anywhere = pl.BlockSpec(memory_space=pl.ANY)
    out = pl.pallas_call(
        functools.partial(final_kernel, plan, count, lead),
        in_specs=[anywhere] * (count + 2),
        out_specs=[anywhere] * (count + 2),
        out_shape=[jax.ShapeDtypeStruct(grad.shape, BF16) for grad in grads]
        + [
            jax.ShapeDtypeStruct((2 * xs * bs * zs * extra.shape[0], 128), BF16),
            jax.ShapeDtypeStruct((bs, own, part, whole.shape[1]), BF16),
        ],
        scratch_shapes=held + sems_shapes(plan, 2 * count + 1, bs * own),
        compiler_params=pltpu.CompilerParams(
            vmem_limit_bytes=VMEM_BYTES, collective_id=0, has_side_effects=True
        ),
        name="final_exchange",
    )(*grads, extra, whole)
    return out[:count], out[count], out[count + 1]


def unpack_kernel(layers, *refs):
    ins = [refs[4 * i : 4 * i + 4] for i in range(layers)]
    w2_out, w1_out, attend_out, wo_out = refs[4 * layers :]
    width = w1_out.shape[1]
    for layer, (w2t, w1, attend, wo) in enumerate(ins):
        for j in range(w1.shape[0] // width):
            rows = slice(j * width, (j + 1) * width)
            cols = slice(j * 128, (j + 1) * 128)
            w2_out[layer, cols, :] = w2t[rows, :].astype(F32).T
            w1_out[layer, :, cols] = w1[rows, :].astype(F32)
            attend_out[layer, :, cols] = attend[rows, :].astype(F32)
            wo_out[layer, :, cols] = wo[rows, :].astype(F32)


def unpack(fulls, width, hidden):
    layers = len(fulls)
    wide = width // 128
    steps = hidden // width
    rows = wide * width
    last = 3 * width // width - 1
    block = (rows, 128)

    def spec(first, top):
        return pl.BlockSpec(block, lambda g: (first + jnp.minimum(g, top), 0))

    ins = [
        spec(0, steps),
        spec(steps, steps),
        spec(2 * steps + 1, last),
        spec(2 * steps, 0),
    ]
    return pl.pallas_call(
        functools.partial(unpack_kernel, layers),
        grid=(steps,),
        in_specs=ins * layers,
        out_specs=[
            pl.BlockSpec((layers, width, width), lambda g: (0, g, 0)),
            pl.BlockSpec((layers, width, width), lambda g: (0, 0, g)),
            pl.BlockSpec((layers, width, width), lambda g: (0, 0, jnp.minimum(g, last))),
            pl.BlockSpec((layers, width, width), lambda g: (0, 0, 0)),
        ],
        out_shape=[
            jax.ShapeDtypeStruct((layers, hidden, width), F32),
            jax.ShapeDtypeStruct((layers, width, hidden), F32),
            jax.ShapeDtypeStruct((layers, width, 3 * width), F32),
            jax.ShapeDtypeStruct((layers, width, width), F32),
        ],
        compiler_params=pltpu.CompilerParams(vmem_limit_bytes=VMEM_BYTES),
        name="unpack",
    )(*[full for full in fulls for _ in range(4)])


def time_embedding(timesteps, width):
    half_width = width // 2
    frequency = jnp.exp(
        jnp.arange(half_width, dtype=jnp.int32).astype(F32) * (-math.log(10000.0) / half_width)
    )
    angles = timesteps.astype(F32)[:, None] * frequency[None, :]
    return jnp.concatenate([jnp.sin(angles), jnp.cos(angles)], axis=-1)


def bias_rows(table, index_table, grid_cols):
    heads, entries = table.shape
    span = 2 * WIN + 1
    offsets = 2 * grid_cols - 1
    turned = index_table.reshape(span, offsets)[:, ::-1].reshape(entries)
    select = (turned[None, :] == jnp.arange(entries, dtype=jnp.int32)[:, None]).astype(F32)
    rows = jnp.dot(table, select, precision=EXACT).reshape(heads, span, offsets)
    key_rows = KWIN // grid_cols
    a0, a1, a2, a3 = [
        jnp.pad(
            rows, ((0, 0), (q, key_rows - span - q), (0, 0)), constant_values=NEG_FILL
        )
        for q in range(QBLOCK // grid_cols)
    ]
    gap = jnp.full((heads, key_rows, 1), NEG_FILL, F32)
    even = jnp.concatenate(
        [a0[..., grid_cols - 1 :], gap, a2, gap, a0[..., : grid_cols - 1]], axis=-1
    )
    odd = jnp.concatenate([gap, a1, gap, a3], axis=-1)
    return jnp.stack([even, odd], axis=1)


def body(
    tokens,
    cotangent,
    valid_mask,
    timesteps,
    index_table,
    first_gain,
    first_shift,
    attend_weight,
    time_weight,
    offset_bias,
    output_weight,
    output_bias,
    second_gain,
    second_shift,
    expand_weight,
    expand_bias,
    reduce_weight,
    reduce_bias,
):
    images, band_rows, grid_cols, width = tokens.shape
    layers = attend_weight.shape[0]
    bands = lax.axis_size("band")
    me = lax.axis_index("band")
    own = images // bands
    part = band_rows * grid_cols
    patches = bands * part
    per_image = patches // CHUNK
    chunks = own * per_image

    def to_images(shard):
        shard = shard.reshape(bands, own, part, width)
        whole = jnp.zeros((own, bands, part, width), shard.dtype)
        for by in range(bands):
            piece = lax.dynamic_index_in_dim(shard, (me + by) % bands, 0, keepdims=False)
            if by:
                pairs = [(i, (i + by) % bands) for i in range(bands)]
                piece = lax.ppermute(piece, "band", pairs)
            whole = lax.dynamic_update_index_in_dim(whole, piece, (me - by) % bands, 1)
        return whole.reshape(own * patches, width)

    def to_bands(whole):
        whole = whole.reshape(own, bands, part, width)
        shard = jnp.zeros((bands, own, part, width), whole.dtype)
        for by in range(bands):
            piece = lax.dynamic_index_in_dim(whole, (me + by) % bands, 1, keepdims=False)
            if by:
                pairs = [(i, (i + by) % bands) for i in range(bands)]
                piece = lax.ppermute(piece, "band", pairs)
            shard = lax.dynamic_update_index_in_dim(shard, piece, (me - by) % bands, 0)
        return shard.reshape(images, band_rows, grid_cols, width)

    x0 = to_images(tokens)
    x0, late = lax.optimization_barrier((x0, cotangent))
    cot = to_images(late)

    mine = lax.dynamic_slice_in_dim(valid_mask, me * own, own, 0).reshape(own, patches)
    fill = jnp.where(mine == 1, 0.0, NEG_FILL).astype(F32)
    fill = jnp.pad(fill, ((0, 0), (HALO, HALO)), constant_values=NEG_FILL)
    mask = jnp.stack(
        [fill[:, c * CHUNK : (c + 1) * CHUNK + 2 * HALO] for c in range(per_image)], axis=1
    ).reshape(chunks, 1, CHUNK + 2 * HALO)

    time_low = time_embedding(
        lax.dynamic_slice_in_dim(timesteps, me * own, own, 0), width
    ).astype(BF16)
    heads, entries = offset_bias.shape[1:]

    def make_rows(table):
        return bias_rows(table, index_table, grid_cols)

    biases, bias_pull = jax.vjp(make_rows, offset_bias.reshape(layers * heads, entries))
    biases = biases.reshape(layers, -1, QBLOCK)

    def row(v):
        return v.reshape(1, -1)

    x, x_lead = x0, 0
    kept = []
    for layer in range(layers):
        tp = jnp.dot(time_low, time_weight[layer], preferred_element_type=F32)
        tproj = jnp.concatenate([tp[:, :width], jnp.zeros_like(tp[:, :width]), tp[:, width:]], axis=1)
        weights = (
            row(first_gain[layer]),
            row(first_shift[layer]),
            attend_weight[layer],
            output_weight[layer],
            row(output_bias[layer]),
            row(second_gain[layer]),
            row(second_shift[layer]),
            expand_weight[layer],
            row(expand_bias[layer]),
            reduce_weight[layer],
            row(reduce_bias[layer]),
        )
        qkv, p, o, mid, act, slope, nxt = forward_layer(
            x,
            x_lead,
            chunks,
            per_image,
            tproj[:, None, :],
            mask,
            biases[layer],
            weights,
            F32 if layer < layers - 1 else BF16,
        )
        kept.append((x, x_lead, qkv, p, o, mid, act, slope))
        x, x_lead = nxt, 2
    output = to_bands(x[x_lead * CHUNK :])

    gx, gx_lead = cot, 0
    devices = bands * lax.axis_size("img")
    big, feed_small = feed_rows(width, expand_weight.shape[2])
    attend_big, attend_all, lines = attend_rows(width)
    used = big + feed_small + attend_all
    buckets = [None] * layers
    extra = [time_low]
    for layer in reversed(range(layers)):
        x, x_lead, qkv, p, o, mid, act, slope = kept[layer]
        gmid, go, feed_grads = feed_back(
            gx,
            gx_lead,
            own * patches,
            mid,
            act,
            slope,
            o,
            row(second_gain[layer]),
            row(second_shift[layer]),
            expand_weight[layer],
            reduce_weight[layer],
            output_weight[layer],
        )
        if layer == layers - 1:
            gmid, output = lax.optimization_barrier((gmid, output))
        gx, gtime, attend_grads = attend_back(
            qkv,
            p,
            go,
            o,
            gmid,
            x,
            x_lead,
            chunks,
            per_image,
            row(first_gain[layer]),
            row(first_shift[layer]),
            attend_weight[layer],
            F32 if layer else BF16,
        )
        gx_lead = 1
        spare = jnp.zeros((-used % (devices * 32), 128), BF16)
        buckets[layer] = jnp.concatenate(
            [feed_grads[:big], attend_grads[:attend_big], feed_grads[big:], attend_grads[attend_big:], spare]
        )
        extra.append(jnp.sum(gtime, axis=1).astype(BF16))
    extra = jnp.concatenate(extra, axis=1).reshape(-1, 128)
    lead = extra.shape[0]
    extra = jnp.pad(extra, ((0, -lead % 16), (0, 0)))
    fulls, gathered, input_grad = final_exchange(buckets, extra, gx, 2 * CHUNK, own, part)
    input_grad = input_grad.reshape(tokens.shape)
    gathered = gathered.reshape(devices, -1, 128)[:, :lead].reshape(devices * own, -1)
    grad_time = jnp.stack(
        [
            lax.dot_general(
                gathered[:, :width],
                gathered[:, width * (1 + 2 * turn) : width * (3 + 2 * turn)],
                (((0,), (0,)), ((), ())),
                preferred_element_type=F32,
            )
            for turn in reversed(range(layers))
        ]
    )
    grad_reduce, grad_expand, grad_attend, grad_output = unpack(fulls, width, expand_weight.shape[2])
    small = jnp.stack([full[big + attend_big : used] for full in fulls]).astype(F32)
    each = width // 128

    def vector(at, count):
        return small[:, at : at + count].reshape(layers, count * 128)

    grad_rows = small[:, feed_small : feed_small + lines]
    (grad_offset,) = bias_pull(grad_rows.reshape(layers * heads, 2, -1, QBLOCK))
    tail = feed_small + lines
    return (
        output,
        input_grad,
        vector(tail, each),
        vector(tail + each, each),
        grad_attend,
        grad_time,
        grad_offset.reshape(layers, heads, entries),
        grad_output,
        vector(each, each),
        vector(2 * each, each),
        vector(3 * each, each),
        grad_expand,
        vector(4 * each, expand_weight.shape[2] // 128),
        grad_reduce,
        vector(0, each),
    )


def solution(mesh):
    split = P("img", "band", None, None)
    placed = (split, split, P("img", None, None), P("img")) + (P(),) * 14
    return jax.shard_map(
        body,
        mesh=mesh,
        in_specs=placed,
        out_specs=(split, split) + (P(),) * 13,
        check_vma=False,
    )
```

time: 827 us -> 533 us (0.64)
  blocking collectives: 123 us -> 0 us
  local copies, waits for them, and re-layouts: 169 us -> 53.2 us
  waiting for transfers between devices: 102 us -> 13.5 us
  Pallas kernels: 373 us -> 447 us
  other arithmetic: 22.8 us -> 4.6 us
  between operations: 15 us -> 1.75 us
    pallas_call x2 -> x4, Pallas kernels: 82 us -> 223 us  [the longest x1 135 us: final_exchange(): pl.pallas_call(functools.partial(final_kernel, plan, count, lead), in_spe...]
    psum x1 -> x0, blocking collectives: 123 us -> none  [body(): return (output, input_grad) + tuple(lax.psum(stacked, ('img', 'band')))]
    psum x1 -> x0, waiting for transfers between devices: 102 us -> none  [body(): return (output, input_grad) + tuple(lax.psum(stacked, ('img', 'band')))]
    pallas_call x2, Pallas kernels: 189 us -> 127 us  [forward_layer(): pl.pallas_call(functools.partial(forward_kernel, pairs), grid=(steps,), i...]
    unnamed x157 -> x76, local copies, waits for them, and re-layouts: 62.8 us -> 17.8 us
    slice x11 -> x3, local copies, waits for them, and re-layouts: 25.3 us -> 0.11 us  [the longest x1 0.09 us: bias_rows(): a0[..., grid_cols - 1:]]
    another operation x9 -> x6, local copies, waits for them, and re-layouts: 25.4 us -> 2.17 us  [the longest x2 1.61 us: body(): jnp.stack([full[big + attend_big:used] for full in fulls]).astype(F32)]
    another operation x15 -> x4, other arithmetic: 18.4 us -> 1.84 us  [the longest x1 1.56 us: body(): jnp.stack([lax.dot_general(gathered[:, :width], gathered[:, width * (1 +...]
  transfers between devices with their start and end apart: 5 -> 3, of which waited for: 1 -> 1; matrix products, arithmetic and copies ran while one was open for 19% -> 5% of each run, Pallas kernels for 0% -> 31%
where the time goes in v2:
time: 533 us; the launch traced here: 529 us
  Pallas kernels  447 us (84%)
  local copies, waits for them, and re-layouts  53.2 us (10%)
  waiting for transfers between devices  13.5 us (3%)
    pallas_call x1, Pallas kernels, final_exchange(): pl.pallas_call(functools.partial(final_kernel, plan, count, lead), in_spe...  135 us
    pallas_call x2, Pallas kernels, forward_layer(): pl.pallas_call(functools.partial(forward_kernel, pairs), grid=(steps,), i...  127 us
    pallas_call x2, Pallas kernels, attend_back(): pl.pallas_call(functools.partial(attend_back_kernel, pairs, chunks, chunk...  97.9 us
    pallas_call x2, Pallas kernels, feed_back(): pl.pallas_call(feed_back_kernel, grid=(patches // FEED,), in_specs=[rows(...  79.2 us
    unnamed x76, local copies, waits for them, and re-layouts  17.8 us
    ppermute x2, waiting for transfers between devices, to_images(): piece = lax.ppermute(piece, 'band', pairs)  13.5 us
  transfers between devices with their start and end apart: 3, of which 1 were waited for; matrix products, arithmetic and copies ran while one was open for 5% of the time, Pallas kernels for 31%

profile of v2, /device:TPU:0, one launch (start us, length us, event | category | flops | bytes accessed | tf_op | source)
XLA Modules:
  0.0 528.7 jit_solution(12474359562768923637)
XLA Ops:
  0.7 2.8 dynamic-slice_bitcast_fusion.2
  3.5 3.0 collective-permute-start
  15.4 1.7 slice_bitcast_fusion
  17.0 0.9 slice_bitcast_fusion.6
  19.5 1.7 bitcast_dynamic-update-slice_fusion.5
  23.1 3.2 slice_bitcast_fusion.1
  26.3 1.4 slice_bitcast_fusion.4
  27.6 13.5 %collective-permute-done = bf16[4,512,384]{2,1,0:T(8,128)(2,1)} collective-permute-done((bf16[4,512,384]{2,1,0:T(8,128)(2,1)}, bf16[4,512,384]{2,1,0:T(8,128)(2,1)}, u32[]{:S(2)}, u32[]{:S(2)}) %collective-permute-start) | collective-permute-done | bytes 1572896 | tf_op jit(solution)/shard_map/ppermute | solution.py:1088
  41.2 1.7 bitcast_dynamic-update-slice_fusion.4
  42.9 1.5 dynamic-slice_bitcast_fusion.1
  44.4 1.7 collective-permute-start.1
  46.8 63.4 %block_forward.2 = (bf16[4096,1152]{1,0:T(8,128)(2,1)}, bf16[36,3,384,256]{3,2,1,0:T(8,128)(2,1)}, bf16[4864,384]{1,0:T(8,128)(2,1)}, f32[4608,384]{1,0:T(8,128)...) custom-call(bf16[4096,384]{1,0:T(8,128)(2,1)} %bitcast.117, ...), custom_call_target="tpu_custom_call" | custom-call | tf_op jit(solution)/shard_map/block_forward/pallas_call | solution.py:283
  110.2 63.4 %block_forward.3 = (bf16[4096,1152]{1,0:T(8,128)(2,1)}, bf16[36,3,384,256]{3,2,1,0:T(8,128)(2,1)}, bf16[4864,384]{1,0:T(8,128)(2,1)}, f32[4608,384]{1,0:T(8,128)...) custom-call(f32[4608,384]{1,0:T(8,128)} %get-tuple-element.55.x_new.x_old.x, ...), custom_call_target="tpu_custom_call" | custom-call | tf_op jit(solution)/shard_map/block_forward/pallas_call | solution.py:283
  173.6 2.2 slice.235
  175.8 1.3 dynamic-slice_bitcast_fusion
  178.3 2.4 copy-done.6
  181.0 1.7 bitcast_dynamic-update-slice_fusion.2
  182.8 1.7 copy-done.1
  184.4 39.6 %feed_back.2 = (f32[4096,384]{1,0:T(8,128)}, bf16[4096,384]{1,0:T(8,128)(2,1)}, bf16[10400,128]{1,0:T(8,128)(2,1)}) custom-call(bf16[4096,384]{1,0:T(8,128)(2,1)} %bitcast.120, f32[4608,384]{1,0:T(8,128)} %get-tuple-element.56.mid, bf16[4608,1536]{1,0:T(8,128)(2,1)} %get-tuple-element.57.act, bf16[4608,1536]{1,0:T(8,128)(2,1)} %get-tuple-element.58.slope, ...), custom_call_target="tpu_custom_call" | custom-call | tf_op jit(solution)/shard_map/feed_back/pallas_call | solution.py:417
  224.0 1.3 bitcast_dynamic-update-slice_fusion
  225.3 49.0 %attend_back.2 = (f32[4608,384]{1,0:T(8,128)}, f32[4,8,768]{2,1,0:T(8,128)}, bf16[3616,128]{1,0:T(8,128)(2,1)}) custom-call(bf16[4096,1152]{1,0:T(8,128)(2,1)} %get-tuple-element.63.prev.cur.nxt, bf16[4096,1152]{1,0:T(8,128)(2,1)} %get-tuple-element.63.prev.cur.nxt, bf16[4096,1152]{1,0:T(8,128)(2,1)} %get-tuple-element.63.prev.cur.nxt, ...), custom_call_target="tpu_custom_call" | custom-call | tf_op jit(solution)/shard_map/attend_back/pallas_call | solution.py:581
  274.3 39.6 %feed_back.3 = (f32[4096,384]{1,0:T(8,128)}, bf16[4096,384]{1,0:T(8,128)(2,1)}, bf16[10400,128]{1,0:T(8,128)(2,1)}) custom-call(f32[4608,384]{1,0:T(8,128)} %get-tuple-element.67.gx, f32[4608,384]{1,0:T(8,128)} %get-tuple-element.68.mid, bf16[4608,1536]{1,0:T(8,128)(2,1)} %get-tuple-element.69.act, bf16[4608,1536]{1,0:T(8,128)(2,1)} %get-tuple-element.70.slope, ...), custom_call_target="tpu_custom_call" | custom-call | tf_op jit(solution)/shard_map/feed_back/pallas_call | solution.py:417
  314.0 48.9 %attend_back.3 = (bf16[4608,384]{1,0:T(8,128)(2,1)}, f32[4,8,768]{2,1,0:T(8,128)}, bf16[3616,128]{1,0:T(8,128)(2,1)}) custom-call(bf16[4096,1152]{1,0:T(8,128)(2,1)} %get-tuple-element.73.prev.cur.nxt, bf16[4096,1152]{1,0:T(8,128)(2,1)} %get-tuple-element.73.prev.cur.nxt, bf16[4096,1152]{1,0:T(8,128)(2,1)} %get-tuple-element.73.prev.cur.nxt, ...), custom_call_target="tpu_custom_call" | custom-call | tf_op jit(solution)/shard_map/attend_back/pallas_call | solution.py:581
  362.9 0.9 reduce_sum.19
  364.2 0.9 copy-done.12
  366.0 2.0 slice_dynamic-update-slice_fusion.1
  368.0 1.0 slice_dynamic-update-slice_fusion.3
  371.5 134.9 %final_exchange.1 = (bf16[14336,128]{1,0:T(8,128)(2,1)}, bf16[14336,128]{1,0:T(8,128)(2,1)}, bf16[2048,128]{1,0:T(8,128)(2,1)}, bf16[2,4,512,384]{3,2,1,0:T(8,128)(2,1)}) custom-call(bf16[14336,128]{1,0:T(8,128)(2,1)} %broadcast_dynamic-update-slice_fusion.1.refs_0_, bf16[14336,128]{1,0:T(8,128)(2,1)} %copy-done.2, bf16[64,128]{1,0:T(8,128)(2,1)} %pad.52.refs_2_, ...), custom_call_target="tpu_custom_call" | custom-call | tf_op jit(solution)/shard_map/final_exchange/pallas_call | solution.py:950
  508.0 1.6 reshape.138
  510.3 8.7 %unpack.1 = (f32[2,1536,384]{2,1,0:T(8,128)}, f32[2,384,1536]{2,1,0:T(8,128)}, f32[2,384,1152]{2,1,0:T(8,128)}, f32[2,384,384]{2,1,0:T(8,128)}) custom-call(bf16[14336,128]{1,0:T(8,128)(2,1)} %get-tuple-element.84.refs_0_.refs_1_.refs_2_.refs_3_, bf16[14336,128]{1,0:T(8,128)(2,1)} %get-tuple-element.84.refs_0_.refs_1_.refs_2_.refs_3_, ...), custom_call_target="tpu_custom_call" | custom-call | tf_op jit(solution)/shard_map/unpack/pallas_call | solution.py:999
  525.0 1.6 pad_maximum_fusion
  526.5 1.7 copy.87
  (139 shorter events, 26.2 us)
Async XLA Ops:
  0.6 5.8 %copy-start.28 = (s32[8]{0:T(128)S(1)}, s32[8]{0:T(128)}, u32[]{:S(2)}) copy-start(s32[8]{0:T(128)} %param.21) | copy-start | bytes 100
  0.7 6.0 %copy-start.11 = (bf16[2,384,768]{2,1,0:T(8,128)(2,1)S(1)}, bf16[2,384,768]{2,1,0:T(8,128)(2,1)}, u32[]{:S(2)}) copy-start(bf16[2,384,768]{2,1,0:T(8,128)(2,1)} %param.26) | copy-start | bytes 3538948
  3.5 11.9 %copy-start.9 = (bf16[2,1536,384]{2,1,0:T(8,128)(2,1)S(1)}, bf16[2,1536,384]{2,1,0:T(8,128)(2,1)}, u32[]{:S(2)}) copy-start(bf16[2,1536,384]{2,1,0:T(8,128)(2,1)} %param.34) | copy-start | bytes 7077892
  3.5 37.7 %collective-permute-start = (bf16[4,512,384]{2,1,0:T(8,128)(2,1)}, bf16[4,512,384]{2,1,0:T(8,128)(2,1)}, u32[]{:S(2)}, u32[]{:S(2)}) collective-permute-start(bf16[4,512,384]{2,1,0:T(8,128)(2,1)} %dynamic-slice_bitcast_fusion.2), channel_id=1, source_target_pairs={{0,1},{1,0},{2,3},{3,2},{4,5},{5,4},{6,7},{7,6},{8,9},{9,8},{10,11... | collective-permute-start | bytes 4718600 | tf_op jit(solution)/shard_map/ppermute | solution.py:1088
  6.7 0.6 copy-start.17
  9.0 0.8 copy-start.20
  14.3 2.7 copy-start.14
  14.7 3.2 copy-start.16
  19.2 2.0 copy-start.22
  19.2 2.1 copy-start.23
  19.2 2.7 copy-start.24
  19.2 2.7 copy-start.25
  19.2 3.3 copy-start.19
  21.3 5.0 copy-start.10
  26.3 16.6 %copy-start.5 = (bf16[8,16,32,384]{3,2,1,0:T(8,128)(2,1)S(1)}, bf16[8,16,32,384]{3,2,1,0:T(8,128)(2,1)}, u32[]{:S(2)}) copy-start(bf16[8,16,32,384]{3,2,1,0:T(8,128)(2,1)} %param.19) | copy-start | bytes 9437188
  27.6 18.5 %copy-start.26 = (f32[2,384]{1,0:T(2,128)S(1)}, f32[2,384]{1,0:T(2,128)}, u32[]{:S(2)}) copy-start(f32[2,384]{1,0:T(2,128)} %param.35) | copy-start | bytes 9220
  27.6 18.5 %copy-start.27 = (f32[2,384]{1,0:T(2,128)S(1)}, f32[2,384]{1,0:T(2,128)}, u32[]{:S(2)}) copy-start(f32[2,384]{1,0:T(2,128)} %param.29) | copy-start | bytes 9220
  42.9 3.9 copy-start
  44.4 136.6 %collective-permute-start.1 = (bf16[4,512,384]{2,1,0:T(8,128)(2,1)}, bf16[4,512,384]{2,1,0:T(8,128)(2,1)}, u32[]{:S(2)}, u32[]{:S(2)}) collective-permute-start(bf16[4,512,384]{2,1,0:T(8,128)(2,1)} %dynamic-slice_bitcast_fusion.1), channel_id=1, source_target_pairs={{0,1},{1,0},{2,3},{3,2},{4,5},{5,4},{6,7},{7,6},{8,9},{9,8},{10,11... | collective-permute-start | bytes 4718600 | tf_op jit(solution)/shard_map/ppermute | solution.py:1088
  177.1 46.9 %collective-permute-start.2 = (bf16[4,512,384]{2,1,0:T(8,128)(2,1)}, bf16[4,512,384]{2,1,0:T(8,128)(2,1)S(1)}, u32[]{:S(2)}, u32[]{:S(2)}) collective-permute-start(bf16[4,512,384]{2,1,0:T(8,128)(2,1)} %dynamic-slice_bitcast_fusion), channel_id=1, source_target_pairs={{0,1},{1,0},{2,3},{3,2},{4,5},{5,4},{6,7},{7,6},{8,9},{9,8},{10,11... | collective-permute-start | bytes 4718600 | tf_op jit(solution)/shard_map/ppermute | solution.py:1099
  177.7 3.0 copy-start.6
  178.0 3.0 copy-start.4
  182.8 1.7 copy-start.1
  313.9 49.9 %copy-start.15 = (f32[4,8,768]{2,1,0:T(8,128)S(1)}, f32[4,8,768]{2,1,0:T(8,128)}, u32[]{:S(2)}) copy-start(f32[4,8,768]{2,1,0:T(8,128)} %get-tuple-element.80) | copy-start | bytes 294916
  313.9 49.9 %copy-start.18 = (bf16[4,192]{1,0:T(4,128)(2,1)S(1)}, bf16[4,192]{1,0:T(4,128)(2,1)}, u32[]{:S(2)}) copy-start(bf16[4,192]{1,0:T(4,128)(2,1)} %copy-done.17) | copy-start | bytes 4612
  314.0 50.0 %copy-start.7 = (bf16[10400,128]{1,0:T(8,128)(2,1)S(1)}, bf16[10400,128]{1,0:T(8,128)(2,1)}, u32[]{:S(2)}) copy-start(bf16[10400,128]{1,0:T(8,128)(2,1)} %get-tuple-element.78) | copy-start | bytes 7987204
  364.0 1.2 copy-start.12
  364.0 2.0 copy-start.8
  365.3 2.7 copy-start.13
  365.3 3.7 copy-start.2
  510.3 9.8 %copy-start.21 = (s32[567]{0:T(1024)S(1)}, s32[567]{0:T(1024)}, u32[]{:S(2)}) copy-start(s32[567]{0:T(1024)} %copy-done.20) | copy-start | bytes 6808
  520.0 6.5 %copy-start.3 = (bf16[2,4,512,384]{3,2,1,0:T(8,128)(2,1)S(1)}, bf16[2,4,512,384]{3,2,1,0:T(8,128)(2,1)}, u32[]{:S(2)}) copy-start(bf16[2,4,512,384]{3,2,1,0:T(8,128)(2,1)} %get-tuple-element.83) | copy-start | bytes 9437188

commit v3 on v2

--- a/solution.py
+++ b/solution.py
@@ -66,6 +66,371 @@
     half = product.shape[0] // 2
     width = product.shape[1] // 2
     return jnp.concatenate([product[:half, :width], product[half:, width:]], axis=0).T
+
+
+def share_rows(rows):
+    return max(n for n in range(16, 257, 16) if rows % n == 0)
+
+
+def add_rows(total, at, others, rows):
+    share = share_rows(rows)
+
+    def one(i, carry):
+        low = pl.multiple_of(i * share, 16)
+        here = pl.ds(pl.multiple_of(at + low, 16), share)
+        v = total[here, :].astype(F32)
+        for ref, row in others:
+            v = v + ref[pl.ds(pl.multiple_of(row + low, 16), share), :].astype(F32)
+        total[here, :] = v.astype(total.dtype)
+        return carry
+
+    lax.fori_loop(0, rows // share, one, 0)
+
+
+def cut(ref, at, rows):
+    return ref.at[pl.ds(pl.multiple_of(at, 16), rows), :]
+
+
+class Places:
+    def __init__(self, plan):
+        self.xs, self.bs, self.zs = plan
+        self.img = lax.axis_index("img")
+        self.b = lax.axis_index("band")
+        self.c = lax.rem(self.img, 2)
+        self.x = lax.rem(self.img // 2, self.xs)
+        self.z = self.img // (2 * self.xs)
+
+    def core(self, by):
+        return (self.img + 1 - 2 * self.c, self.b)
+
+    def along_x(self, by):
+        return ((self.z * self.xs + lax.rem(self.x + by, self.xs)) * 2 + self.c, self.b)
+
+    def along_b(self, by):
+        return (self.img, lax.rem(self.b + by, self.bs))
+
+    def along_z(self, by):
+        return ((lax.rem(self.z + by, self.zs) * self.xs + self.x) * 2 + self.c, self.b)
+
+    def greet(self):
+        barrier = pltpu.get_barrier_semaphore()
+        peers = [self.core(1)]
+        peers += [self.along_x(by) for by in range(1, self.xs)]
+        peers += [self.along_b(by) for by in range(1, self.bs)]
+        peers += [self.along_z(by) for by in range(1, self.zs)]
+        for peer in peers:
+            pl.semaphore_signal(barrier, inc=1, device_id=peer, device_id_type=pl.DeviceIdType.MESH)
+        pl.semaphore_wait(barrier, len(peers))
+
+
+class Lane:
+    def __init__(self, plan, sems):
+        self.plan, self.sems, self.steps = plan, sems, []
+
+    def add(self, copies, then=None):
+        count = [0, 0]
+        here = Places(self.plan)
+        for src, dst, peer in copies(here):
+            count[peer is None] += 1
+        base = (self.sems.sent, self.sems.kept)
+        self.sems.sent += count[0]
+        self.sems.kept += count[1]
+        self.steps.append((copies, then, base))
+
+    def described(self, step):
+        copies, _, (sent, kept) = self.steps[step]
+        made = []
+        for src, dst, peer in copies(Places(self.plan)):
+            if peer is None:
+                made.append(pltpu.make_async_copy(src, dst, self.sems.own.at[kept]))
+                kept += 1
+            else:
+                made.append(
+                    pltpu.make_async_remote_copy(
+                        src_ref=src,
+                        dst_ref=dst,
+                        send_sem=self.sems.send.at[sent],
+                        recv_sem=self.sems.recv.at[sent],
+                        device_id=peer,
+                        device_id_type=pl.DeviceIdType.MESH,
+                    )
+                )
+                sent += 1
+        return made
+
+    def part(self, i):
+        if i > 0:
+            for copy in self.described(i - 1):
+                copy.wait()
+            if self.steps[i - 1][1] is not None:
+                self.steps[i - 1][1](Places(self.plan))
+        if i < len(self.steps):
+            for copy in self.described(i):
+                copy.start()
+
+
+class Sems:
+    def __init__(self, send, recv, own):
+        self.send, self.recv, self.own = send, recv, own
+        self.sent = self.kept = 0
+
+
+def scatter_lane(lane, grad, held, chunk=None):
+    acc, r1, r2a, r2b, r3a, r3b, r4 = held
+    xs, bs, zs = lane.plan
+    half = grad.shape[0] // 2
+    quarter = half // 2
+    nx, nb, n2 = quarter // xs, quarter // bs, quarter // (xs * bs)
+    n = n2 // zs
+
+    def core_copies(at):
+        return [
+            (cut(grad, at.c * half, half), acc, None),
+            (cut(grad, half - at.c * half, half), r1, at.core(1)),
+        ]
+
+    lane.add(core_copies, lambda at: add_rows(acc, 0, [(r1, 0)], half))
+
+    def wide_copies(at):
+        made = []
+        for by in range(1, xs):
+            there = lax.rem(at.x + by, xs)
+            made.append((cut(acc, there * nx, nx), cut(r2a, (by - 1) * nx, nx), at.along_x(by)))
+        for by in range(1, bs):
+            there = quarter + lax.rem(at.b + by, bs) * nb
+            made.append((cut(acc, there, nb), cut(r2b, (by - 1) * nb, nb), at.along_b(by)))
+        return made
+
+    def wide_add(at):
+        add_rows(acc, at.x * nx, [(r2a, k * nx) for k in range(xs - 1)], nx)
+        add_rows(acc, quarter + at.b * nb, [(r2b, k * nb) for k in range(bs - 1)], nb)
+
+    lane.add(wide_copies, wide_add)
+
+    def cross_copies(at):
+        made = []
+        for by in range(1, bs):
+            there = at.x * nx + lax.rem(at.b + by, bs) * n2
+            made.append((cut(acc, there, n2), cut(r3a, (by - 1) * n2, n2), at.along_b(by)))
+        for by in range(1, xs):
+            there = quarter + at.b * nb + lax.rem(at.x + by, xs) * n2
+            made.append((cut(acc, there, n2), cut(r3b, (by - 1) * n2, n2), at.along_x(by)))
+        return made
+
+    def plane(at):
+        return at.x * nx + at.b * n2, quarter + at.b * nb + at.x * n2
+
+    def cross_add(at):
+        first, second = plane(at)
+        add_rows(acc, first, [(r3a, k * n2) for k in range(bs - 1)], n2)
+        add_rows(acc, second, [(r3b, k * n2) for k in range(xs - 1)], n2)
+
+    lane.add(cross_copies, cross_add)
+
+    def deep_copies(at):
+        made = []
+        for by in range(1, zs):
+            there = lax.rem(at.z + by, zs) * n
+            for k, low in enumerate(plane(at)):
+                slot = (2 * (by - 1) + k) * n
+                made.append((cut(acc, low + there, n), cut(r4, slot, n), at.along_z(by)))
+        return made
+
+    def deep_add(at):
+        for k, low in enumerate(plane(at)):
+            add_rows(acc, low + at.z * n, [(r4, (2 * i + k) * n) for i in range(zs - 1)], n)
+
+    lane.add(deep_copies, deep_add)
+
+    def ends(at):
+        return [cut(acc, low + at.z * n, n) for low in plane(at)]
+
+    if chunk is None:
+        return ends
+    lane.add(lambda at: [(ref, cut(chunk, k * n, n), None) for k, ref in enumerate(ends(at))])
+
+
+def collect_lane(lane, ends, out):
+    xs, bs, zs = lane.plan
+    half = out.shape[0] // 2
+    quarter = half // 2
+    nx, nb, n2 = quarter // xs, quarter // bs, quarter // (xs * bs)
+    n = n2 // zs
+
+    def plane(at):
+        base = at.c * half
+        return base + at.x * nx + at.b * n2, base + quarter + at.b * nb + at.x * n2
+
+    def deep(at):
+        made = []
+        for ref, low in zip(ends(at), plane(at)):
+            there = cut(out, low + at.z * n, n)
+            made.append((ref, there, None))
+            made += [(ref, there, at.along_z(by)) for by in range(1, zs)]
+        return made
+
+    def cross(at):
+        first, second = plane(at)
+        a, b = cut(out, first, n2), cut(out, second, n2)
+        made = [(a, a, at.along_b(by)) for by in range(1, bs)]
+        return made + [(b, b, at.along_x(by)) for by in range(1, xs)]
+
+    def wide(at):
+        a = cut(out, at.c * half + at.x * nx, nx)
+        b = cut(out, at.c * half + quarter + at.b * nb, nb)
+        made = [(a, a, at.along_x(by)) for by in range(1, xs)]
+        return made + [(b, b, at.along_b(by)) for by in range(1, bs)]
+
+    def core(at):
+        whole = cut(out, at.c * half, half)
+        return [(whole, whole, at.core(1))]
+
+    for copies in (deep, cross, wide, core):
+        lane.add(copies)
+
+
+def extra_lane(lane, extra, out):
+    xs, bs, zs = lane.plan
+    rows = extra.shape[0]
+
+    def deep(at):
+        there = cut(out, (((at.c * xs + at.x) * bs + at.b) * zs + at.z) * rows, rows)
+        return [(extra, there, None)] + [(extra, there, at.along_z(by)) for by in range(1, zs)]
+
+    def cross(at):
+        there = cut(out, ((at.c * xs + at.x) * bs + at.b) * zs * rows, zs * rows)
+        return [(there, there, at.along_b(by)) for by in range(1, bs)]
+
+    def wide(at):
+        there = cut(out, (at.c * xs + at.x) * bs * zs * rows, bs * zs * rows)
+        return [(there, there, at.along_x(by)) for by in range(1, xs)]
+
+    def core(at):
+        there = cut(out, at.c * xs * bs * zs * rows, xs * bs * zs * rows)
+        return [(there, there, at.core(1))]
+
+    for copies in (deep, cross, wide, core):
+        lane.add(copies)
+
+
+def bands_lane(lane, whole, lead, out):
+    bs = lane.plan[1]
+    rows, width = out.shape[2:]
+    own = out.shape[1]
+
+    def copies(at):
+        made = []
+        for by in range(bs):
+            there = lax.rem(at.b + by, bs)
+            for i in range(own):
+                src = cut(whole, lead + (i * bs + there) * rows, rows)
+                made.append((src, out.at[at.b, i], at.along_b(by) if by else None))
+        return made
+
+    lane.add(copies)
+
+
+def link_plan():
+    pairs = lax.axis_size("img") // 2
+    xs = 2 if pairs % 2 == 0 else 1
+    return xs, lax.axis_size("band"), pairs // xs
+
+
+def padded_rows(rows):
+    xs, bs, zs = link_plan()
+    return -(-rows // (64 * xs * bs * zs)) * (64 * xs * bs * zs)
+
+
+def held_shapes(plan, rows):
+    xs, bs, zs = plan
+    quarter = rows // 4
+    sizes = [
+        rows // 2,
+        rows // 2,
+        (xs - 1) * quarter // xs,
+        (bs - 1) * quarter // bs,
+        (bs - 1) * quarter // (xs * bs),
+        (xs - 1) * quarter // (xs * bs),
+        (zs - 1) * 2 * quarter // (xs * bs * zs),
+    ]
+    return [pltpu.VMEM((max(n, 16), 128), BF16) for n in sizes]
+
+
+def sems_shapes(plan, lanes, moved=0):
+    xs, bs, zs = plan
+    count = lanes * (1 + 2 * (xs - 1 + bs - 1) + 2 * (zs - 1)) + moved
+    return [
+        pltpu.SemaphoreType.DMA((count,)),
+        pltpu.SemaphoreType.DMA((count,)),
+        pltpu.SemaphoreType.DMA((2 * lanes + moved + 1,)),
+    ]
+
+
+class Links:
+    def __init__(self, jobs):
+        self.jobs = jobs
+        self.plan = link_plan()
+        xs, bs, zs = self.plan
+        self.devices = 2 * xs * bs * zs
+        self.arrays = [job[1] for job in jobs]
+        self.shapes, self.scratch = [], []
+        for job in jobs:
+            if job[0] == "scatter":
+                rows = job[1].shape[0] // self.devices
+                self.scratch += held_shapes(self.plan, job[1].shape[0])
+            else:
+                rows = job[2]
+            self.shapes.append(jax.ShapeDtypeStruct((rows, 128), BF16))
+        if jobs:
+            self.scratch += sems_shapes(self.plan, len(jobs))
+        self.specs = [pl.BlockSpec(memory_space=pl.ANY)] * len(jobs)
+
+    def host(self, kernel, ins, outs, scratch):
+        if not self.jobs:
+            return kernel
+
+        def run(*refs):
+            count = len(self.jobs)
+            a, b, c = ins, ins + count, ins + count + outs
+            d, e = c + count, c + count + scratch
+            step = pl.program_id(0)
+            self.carry(step, refs[a:b], refs[c:d], refs[e:])
+            kernel(*refs[:a], *refs[b:c], *refs[d:e])
+
+        return run
+
+    def carry(self, step, given, made, scratch):
+        sems = Sems(*scratch[-3:])
+        held = list(scratch[:-3])
+        parts = {}
+        for job, ref, out in zip(self.jobs, given, made):
+            lane = Lane(self.plan, sems)
+            if job[0] == "scatter":
+                scatter_lane(lane, ref, held[:7], out)
+                held = held[7:]
+            else:
+                rows = ref.shape[0] // 2
+                collect_lane(
+                    lane, lambda at, ref=ref, rows=rows: [cut(ref, k * rows, rows) for k in range(2)], out
+                )
+            assert len(job[-1]) == len(lane.steps) + 1
+            for part, when in enumerate(job[-1]):
+                parts.setdefault(when, []).append((lane, part))
+        for when in sorted(parts):
+
+            @pl.when(step == when)
+            def _(when=when):
+                if when == 0:
+                    Places(self.plan).greet()
+                for lane, part in parts[when]:
+                    lane.part(part)
+
+    def params(self, number):
+        if not self.jobs:
+            return pltpu.CompilerParams(vmem_limit_bytes=VMEM_BYTES)
+        return pltpu.CompilerParams(
+            vmem_limit_bytes=VMEM_BYTES, collective_id=number, has_side_effects=True
+        )
 
 
 def fold(v, op):
@@ -399,6 +764,10 @@
         whole.append(jnp.sum(gb1[...], axis=0, keepdims=True))
         at = (2 * tiles + gwo.shape[1] // 128) * gwo.shape[0]
         put_rows(grads_out, at, whole)
+        used = sum(feed_rows(gwo.shape[0], hidden))
+        spare = grads_out.shape[0] - used
+        if spare:
+            grads_out[used:, :] = jnp.zeros((spare, 128), grads_out.dtype)
 
 
 def feed_rows(width, hidden):
@@ -406,16 +775,16 @@
     return tiles * width, -(-(4 * width + hidden) // 128 // 16) * 16
 
 
-def feed_back(gx, gx_lead, patches, mid, act, slope, o, gain2, shift2, w1, w2, wo):
+def feed_back(gx, gx_lead, patches, mid, act, slope, o, gain2, shift2, w1, w2, wo, links, number):
     width = mid.shape[1]
     hidden = act.shape[1]
 
     def rows(cols, lead):
         return pl.BlockSpec((FEED, cols), lambda g: (g + lead, 0))
 
-    grad_rows = sum(feed_rows(width, hidden))
+    grad_rows = padded_rows(sum(feed_rows(width, hidden)))
     return pl.pallas_call(
-        feed_back_kernel,
+        links.host(feed_back_kernel, 10, 3, 6),
         grid=(patches // FEED,),
         in_specs=[
             rows(width, gx_lead),
@@ -424,13 +793,15 @@
             rows(hidden, 1),
             rows(width, 1),
         ]
-        + [const_spec(w.shape) for w in (gain2, shift2, w1, w2, wo)],
-        out_specs=[rows(width, 0), rows(width, 0), const_spec((grad_rows, 128))],
+        + [const_spec(w.shape) for w in (gain2, shift2, w1, w2, wo)]
+        + links.specs,
+        out_specs=[rows(width, 0), rows(width, 0), const_spec((grad_rows, 128))] + links.specs,
         out_shape=[
             jax.ShapeDtypeStruct((patches, width), F32),
             jax.ShapeDtypeStruct((patches, width), BF16),
             jax.ShapeDtypeStruct((grad_rows, 128), BF16),
-        ],
+        ]
+        + links.shapes,
         scratch_shapes=[
             pltpu.VMEM((width, hidden), F32),
             pltpu.VMEM((width, hidden), F32),
@@ -438,10 +809,11 @@
             pltpu.VMEM((4, 8, width), F32),
             pltpu.VMEM((8, hidden), F32),
             pltpu.VMEM((FEED, hidden), BF16),
-        ],
-        compiler_params=pltpu.CompilerParams(vmem_limit_bytes=VMEM_BYTES),
+        ]
+        + links.scratch,
+        compiler_params=links.params(number),
         name="feed_back",
-    )(gx, mid, act, slope, o, gain2, shift2, w1, w2, wo)
+    )(gx, mid, act, slope, o, gain2, shift2, w1, w2, wo, *links.arrays)
 
 
 def attend_back_kernel(
@@ -551,6 +923,10 @@
             tiles * width + lines,
             [jnp.sum(sums[i], axis=0, keepdims=True) for i in range(2)],
         )
+        used = attend_rows(width)[1]
+        spare = grads_out.shape[0] - used
+        if spare:
+            grads_out[used:, :] = jnp.zeros((spare, 128), grads_out.dtype)
 
 
 def attend_rows(width):
@@ -560,7 +936,21 @@
 
 
 def attend_back(
-    qkv, p, go, o, gmid, x, x_lead, chunks, chunks_per_image, gain1, shift1, wqkv, out_dtype
+    qkv,
+    p,
+    go,
+    o,
+    gmid,
+    x,
+    x_lead,
+    chunks,
+    chunks_per_image,
+    gain1,
+    shift1,
+    wqkv,
+    out_dtype,
+    links,
+    number,
 ):
     width = x.shape[1]
     pairs = width // 128
@@ -577,9 +967,10 @@
         return pl.BlockSpec((CHUNK, cols), lambda g: (index(g) + lead, 0))
 
     images = chunks // chunks_per_image
-    grad_rows = attend_rows(width)[1]
+    grad_rows = padded_rows(attend_rows(width)[1])
+    kernel = functools.partial(attend_back_kernel, pairs, chunks, chunks_per_image)
     return pl.pallas_call(
-        functools.partial(attend_back_kernel, pairs, chunks, chunks_per_image),
+        links.host(kernel, 11, 3, 6),
         grid=(steps,),
         in_specs=[
             pl.BlockSpec((HALO, 3 * width), lambda g: (jnp.maximum(halves * now(g) - 1, 0), 0)),
@@ -596,17 +987,20 @@
             rows(width, 0, late),
             rows(width, x_lead, late),
         ]
-        + [const_spec(w.shape) for w in (gain1, shift1, wqkv)],
+        + [const_spec(w.shape) for w in (gain1, shift1, wqkv)]
+        + links.specs,
         out_specs=[
             rows(width, 1, lambda g: g),
             pl.BlockSpec((1, 8, 2 * width), lambda g: (late(g) // chunks_per_image, 0, 0)),
             const_spec((grad_rows, 128)),
-        ],
+        ]
+        + links.specs,
         out_shape=[
             jax.ShapeDtypeStruct(((steps + 1) * CHUNK, width), out_dtype),
             jax.ShapeDtypeStruct((images, 8, 2 * width), F32),
             jax.ShapeDtypeStruct((grad_rows, 128), BF16),
-        ],
+        ]
+        + links.shapes,
         scratch_shapes=[
             pltpu.VMEM((width, 3 * width), F32),
             pltpu.VMEM((pairs, KWIN, 2 * QBLOCK), F32),
@@ -614,321 +1008,25 @@
             pltpu.VMEM((CHUNK, width), BF16),
             pltpu.VMEM((2 * CHUNK + HALO, 2 * width), F32),
             pltpu.VMEM((CHUNK // QBLOCK, pairs, KWIN, 2 * QBLOCK), BF16),
-        ],
-        compiler_params=pltpu.CompilerParams(vmem_limit_bytes=VMEM_BYTES),
+        ]
+        + links.scratch,
+        compiler_params=links.params(number),
         name="attend_back",
-    )(qkv, qkv, qkv, p, go, o, gmid, x, gain1, shift1, wqkv)
-
-
-def share_rows(rows):
-    return max(n for n in range(16, 257, 16) if rows % n == 0)
-
-
-def add_rows(total, at, others, rows):
-    share = share_rows(rows)
-
-    def one(i, carry):
-        low = pl.multiple_of(i * share, 16)
-        here = pl.ds(pl.multiple_of(at + low, 16), share)
-        v = total[here, :].astype(F32)
-        for ref, row in others:
-            v = v + ref[pl.ds(pl.multiple_of(row + low, 16), share), :].astype(F32)
-        total[here, :] = v.astype(total.dtype)
-        return carry
-
-    lax.fori_loop(0, rows // share, one, 0)
-
-
-def cut(ref, at, rows):
-    return ref.at[pl.ds(pl.multiple_of(at, 16), rows), :]
-
-
-class Places:
-    def __init__(self, plan):
-        self.xs, self.bs, self.zs = plan
-        self.img = lax.axis_index("img")
-        self.b = lax.axis_index("band")
-        self.c = lax.rem(self.img, 2)
-        self.x = lax.rem(self.img // 2, self.xs)
-        self.z = self.img // (2 * self.xs)
-
-    def core(self, by):
-        return (self.img + 1 - 2 * self.c, self.b)
-
-    def along_x(self, by):
-        return ((self.z * self.xs + lax.rem(self.x + by, self.xs)) * 2 + self.c, self.b)
-
-    def along_b(self, by):
-        return (self.img, lax.rem(self.b + by, self.bs))
-
-    def along_z(self, by):
-        return ((lax.rem(self.z + by, self.zs) * self.xs + self.x) * 2 + self.c, self.b)
-
-    def greet(self):
-        barrier = pltpu.get_barrier_semaphore()
-        peers = [self.core(1)]
-        peers += [self.along_x(by) for by in range(1, self.xs)]
-        peers += [self.along_b(by) for by in range(1, self.bs)]
-        peers += [self.along_z(by) for by in range(1, self.zs)]
-        for peer in peers:
-            pl.semaphore_signal(barrier, inc=1, device_id=peer, device_id_type=pl.DeviceIdType.MESH)
-        pl.semaphore_wait(barrier, len(peers))
-
-
-class Lane:
-    def __init__(self, plan, sems):
-        self.plan, self.sems, self.steps = plan, sems, []
-
-    def add(self, copies, then=None):
-        count = [0, 0]
-        here = Places(self.plan)
-        for src, dst, peer in copies(here):
-            count[peer is None] += 1
-        base = (self.sems.sent, self.sems.kept)
-        self.sems.sent += count[0]
-        self.sems.kept += count[1]
-        self.steps.append((copies, then, base))
-
-    def described(self, step):
-        copies, _, (sent, kept) = self.steps[step]
-        made = []
-        for src, dst, peer in copies(Places(self.plan)):
-            if peer is None:
-                made.append(pltpu.make_async_copy(src, dst, self.sems.own.at[kept]))
-                kept += 1
-            else:
-                made.append(
-                    pltpu.make_async_remote_copy(
-                        src_ref=src,
-                        dst_ref=dst,
-                        send_sem=self.sems.send.at[sent],
-                        recv_sem=self.sems.recv.at[sent],
-                        device_id=peer,
-                        device_id_type=pl.DeviceIdType.MESH,
-                    )
-                )
-                sent += 1
-        return made
-
-    def part(self, i):
-        if i > 0:
-            for copy in self.described(i - 1):
-                copy.wait()
-            if self.steps[i - 1][1] is not None:
-                self.steps[i - 1][1](Places(self.plan))
-        if i < len(self.steps):
-            for copy in self.described(i):
-                copy.start()
-
-
-class Sems:
-    def __init__(self, send, recv, own):
-        self.send, self.recv, self.own = send, recv, own
-        self.sent = self.kept = 0
-
-
-def scatter_lane(lane, grad, held, chunk=None):
-    acc, r1, r2a, r2b, r3a, r3b, r4 = held
-    xs, bs, zs = lane.plan
-    half = grad.shape[0] // 2
-    quarter = half // 2
-    nx, nb, n2 = quarter // xs, quarter // bs, quarter // (xs * bs)
-    n = n2 // zs
-
-    def core_copies(at):
-        return [
-            (cut(grad, at.c * half, half), acc, None),
-            (cut(grad, half - at.c * half, half), r1, at.core(1)),
-        ]
-
-    lane.add(core_copies, lambda at: add_rows(acc, 0, [(r1, 0)], half))
-
-    def wide_copies(at):
-        made = []
-        for by in range(1, xs):
-            there = lax.rem(at.x + by, xs)
-            made.append((cut(acc, there * nx, nx), cut(r2a, (by - 1) * nx, nx), at.along_x(by)))
-        for by in range(1, bs):
-            there = quarter + lax.rem(at.b + by, bs) * nb
-            made.append((cut(acc, there, nb), cut(r2b, (by - 1) * nb, nb), at.along_b(by)))
-        return made
-
-    def wide_add(at):
-        add_rows(acc, at.x * nx, [(r2a, k * nx) for k in range(xs - 1)], nx)
-        add_rows(acc, quarter + at.b * nb, [(r2b, k * nb) for k in range(bs - 1)], nb)
-
-    lane.add(wide_copies, wide_add)
-
-    def cross_copies(at):
-        made = []
-        for by in range(1, bs):
-            there = at.x * nx + lax.rem(at.b + by, bs) * n2
-            made.append((cut(acc, there, n2), cut(r3a, (by - 1) * n2, n2), at.along_b(by)))
-        for by in range(1, xs):
-            there = quarter + at.b * nb + lax.rem(at.x + by, xs) * n2
-            made.append((cut(acc, there, n2), cut(r3b, (by - 1) * n2, n2), at.along_x(by)))
-        return made
-
-    def plane(at):
-        return at.x * nx + at.b * n2, quarter + at.b * nb + at.x * n2
-
-    def cross_add(at):
-        first, second = plane(at)
-        add_rows(acc, first, [(r3a, k * n2) for k in range(bs - 1)], n2)
-        add_rows(acc, second, [(r3b, k * n2) for k in range(xs - 1)], n2)
-
-    lane.add(cross_copies, cross_add)
-
-    def deep_copies(at):
-        made = []
-        for by in range(1, zs):
-            there = lax.rem(at.z + by, zs) * n
-            for k, low in enumerate(plane(at)):
-                slot = (2 * (by - 1) + k) * n
-                made.append((cut(acc, low + there, n), cut(r4, slot, n), at.along_z(by)))
-        return made
-
-    def deep_add(at):
-        for k, low in enumerate(plane(at)):
-            add_rows(acc, low + at.z * n, [(r4, (2 * i + k) * n) for i in range(zs - 1)], n)
-
-    lane.add(deep_copies, deep_add)
-
-    def ends(at):
-        return [cut(acc, low + at.z * n, n) for low in plane(at)]
-
-    if chunk is None:
-        return ends
-    lane.add(lambda at: [(ref, cut(chunk, k * n, n), None) for k, ref in enumerate(ends(at))])
-
-
-def collect_lane(lane, ends, out):
-    xs, bs, zs = lane.plan
-    half = out.shape[0] // 2
-    quarter = half // 2
-    nx, nb, n2 = quarter // xs, quarter // bs, quarter // (xs * bs)
-    n = n2 // zs
-
-    def plane(at):
-        base = at.c * half
-        return base + at.x * nx + at.b * n2, base + quarter + at.b * nb + at.x * n2
-
-    def deep(at):
-        made = []
-        for ref, low in zip(ends(at), plane(at)):
-            there = cut(out, low + at.z * n, n)
-            made.append((ref, there, None))
-            made += [(ref, there, at.along_z(by)) for by in range(1, zs)]
-        return made
-
-    def cross(at):
-        first, second = plane(at)
-        a, b = cut(out, first, n2), cut(out, second, n2)
-        made = [(a, a, at.along_b(by)) for by in range(1, bs)]
-        return made + [(b, b, at.along_x(by)) for by in range(1, xs)]
-
-    def wide(at):
-        a = cut(out, at.c * half + at.x * nx, nx)
-        b = cut(out, at.c * half + quarter + at.b * nb, nb)
-        made = [(a, a, at.along_x(by)) for by in range(1, xs)]
-        return made + [(b, b, at.along_b(by)) for by in range(1, bs)]
-
-    def core(at):
-        whole = cut(out, at.c * half, half)
-        return [(whole, whole, at.core(1))]
-
-    for copies in (deep, cross, wide, core):
-        lane.add(copies)
-
-
-def extra_lane(lane, extra, out):
-    xs, bs, zs = lane.plan
-    rows = extra.shape[0]
-
-    def deep(at):
-        there = cut(out, (((at.c * xs + at.x) * bs + at.b) * zs + at.z) * rows, rows)
-        return [(extra, there, None)] + [(extra, there, at.along_z(by)) for by in range(1, zs)]
-
-    def cross(at):
-        there = cut(out, ((at.c * xs + at.x) * bs + at.b) * zs * rows, zs * rows)
-        return [(there, there, at.along_b(by)) for by in range(1, bs)]
-
-    def wide(at):
-        there = cut(out, (at.c * xs + at.x) * bs * zs * rows, bs * zs * rows)
-        return [(there, there, at.along_x(by)) for by in range(1, xs)]
-
-    def core(at):
-        there = cut(out, at.c * xs * bs * zs * rows, xs * bs * zs * rows)
-        return [(there, there, at.core(1))]
-
-    for copies in (deep, cross, wide, core):
-        lane.add(copies)
-
-
-def bands_lane(lane, whole, lead, out):
-    bs = lane.plan[1]
-    rows, width = out.shape[2:]
-    own = out.shape[1]
-
-    def copies(at):
-        made = []
-        for by in range(bs):
-            there = lax.rem(at.b + by, bs)
-            for i in range(own):
-                src = cut(whole, lead + (i * bs + there) * rows, rows)
-                made.append((src, out.at[at.b, i], at.along_b(by) if by else None))
-        return made
-
-    lane.add(copies)
-
-
-def link_plan():
-    pairs = lax.axis_size("img") // 2
-    xs = 2 if pairs % 2 == 0 else 1
-    return xs, lax.axis_size("band"), pairs // xs
-
-
-def held_shapes(plan, rows):
-    xs, bs, zs = plan
-    quarter = rows // 4
-    sizes = [
-        rows // 2,
-        rows // 2,
-        (xs - 1) * quarter // xs,
-        (bs - 1) * quarter // bs,
-        (bs - 1) * quarter // (xs * bs),
-        (xs - 1) * quarter // (xs * bs),
-        (zs - 1) * 2 * quarter // (xs * bs * zs),
-    ]
-    return [pltpu.VMEM((max(n, 16), 128), BF16) for n in sizes]
-
-
-def sems_shapes(plan, lanes, moved=0):
-    xs, bs, zs = plan
-    count = lanes * (1 + 2 * (xs - 1 + bs - 1) + 2 * (zs - 1)) + moved
-    return [
-        pltpu.SemaphoreType.DMA((count,)),
-        pltpu.SemaphoreType.DMA((count,)),
-        pltpu.SemaphoreType.DMA((2 * lanes + moved + 1,)),
-    ]
-
-
-def final_kernel(plan, count, lead, *refs):
-    grads, extra, whole = refs[:count], refs[count], refs[count + 1]
-    outs, extra_out, bands_out = refs[count + 2 : 2 * count + 2], refs[2 * count + 2], refs[2 * count + 3]
-    scratch = refs[2 * count + 4 :]
+    )(qkv, qkv, qkv, p, go, o, gmid, x, gain1, shift1, wqkv, *links.arrays)
+
+
+def final_kernel(plan, lead, *refs):
+    chunk, grad, extra, whole = refs[:4]
+    feed_out, attend_out, extra_out, bands_out = refs[4:8]
+    scratch = refs[8:]
     sems = Sems(*scratch[-3:])
-    each = 7
     Places(plan).greet()
-    lanes = []
-    for i in range(count):
-        lane = Lane(plan, sems)
-        ends = scatter_lane(lane, grads[i], scratch[i * each : (i + 1) * each])
-        collect_lane(lane, ends, outs[i])
-        lanes.append(lane)
-    lane = Lane(plan, sems)
-    extra_lane(lane, extra, extra_out)
-    lanes.append(lane)
+    lanes = [Lane(plan, sems) for _ in range(3)]
+    rows = chunk.shape[0] // 2
+    ends = scatter_lane(lanes[0], grad, scratch[:-3])
+    collect_lane(lanes[0], ends, attend_out)
+    collect_lane(lanes[1], lambda at: [cut(chunk, k * rows, rows) for k in range(2)], feed_out)
+    extra_lane(lanes[2], extra, extra_out)
     late = Lane(plan, sems)
     bands_lane(late, whole, lead, bands_out)
     late.part(0)
@@ -939,30 +1037,26 @@
     late.part(1)
 
 
-def final_exchange(grads, extra, whole, lead, own, part):
+def final_exchange(chunk, feed_rows_all, grad, extra, whole, lead, own, part):
     plan = link_plan()
     xs, bs, zs = plan
-    count = len(grads)
-    held = []
-    for grad in grads:
-        held += held_shapes(plan, grad.shape[0])
     anywhere = pl.BlockSpec(memory_space=pl.ANY)
-    out = pl.pallas_call(
-        functools.partial(final_kernel, plan, count, lead),
-        in_specs=[anywhere] * (count + 2),
-        out_specs=[anywhere] * (count + 2),
-        out_shape=[jax.ShapeDtypeStruct(grad.shape, BF16) for grad in grads]
-        + [
+    return pl.pallas_call(
+        functools.partial(final_kernel, plan, lead),
+        in_specs=[anywhere] * 4,
+        out_specs=[anywhere] * 4,
+        out_shape=[
+            jax.ShapeDtypeStruct((feed_rows_all, 128), BF16),
+            jax.ShapeDtypeStruct(grad.shape, BF16),
             jax.ShapeDtypeStruct((2 * xs * bs * zs * extra.shape[0], 128), BF16),
             jax.ShapeDtypeStruct((bs, own, part, whole.shape[1]), BF16),
         ],
-        scratch_shapes=held + sems_shapes(plan, 2 * count + 1, bs * own),
+        scratch_shapes=held_shapes(plan, grad.shape[0]) + sems_shapes(plan, 4, bs * own),
         compiler_params=pltpu.CompilerParams(
             vmem_limit_bytes=VMEM_BYTES, collective_id=0, has_side_effects=True
         ),
         name="final_exchange",
-    )(*grads, extra, whole)
-    return out[:count], out[count], out[count + 1]
+    )(chunk, grad, extra, whole)
 
 
 def unpack_kernel(layers, *refs):
@@ -993,7 +1087,7 @@
     ins = [
         spec(0, steps),
         spec(steps, steps),
-        spec(2 * steps + 1, last),
+        spec(0, last),
         spec(2 * steps, 0),
     ]
     return pl.pallas_call(
@@ -1014,7 +1108,7 @@
         ],
         compiler_params=pltpu.CompilerParams(vmem_limit_bytes=VMEM_BYTES),
         name="unpack",
-    )(*[full for full in fulls for _ in range(4)])
+    )(*[ref for feed, attend in fulls for ref in (feed, feed, attend, feed)])
 
 
 def time_embedding(timesteps, width):
@@ -1046,6 +1140,10 @@
     )
     odd = jnp.concatenate([gap, a1, gap, a3], axis=-1)
     return jnp.stack([even, odd], axis=1)
+
+
+def spaced(parts, steps):
+    return [i * (steps - 1) // (parts - 1) for i in range(parts)]
 
 
 def body(
@@ -1160,14 +1258,22 @@
 
     gx, gx_lead = cot, 0
     devices = bands * lax.axis_size("img")
-    big, feed_small = feed_rows(width, expand_weight.shape[2])
-    attend_big, attend_all, lines = attend_rows(width)
-    used = big + feed_small + attend_all
-    buckets = [None] * layers
+    feed_big = feed_rows(width, expand_weight.shape[2])[0]
+    attend_big, _, lines = attend_rows(width)
+    fulls = [[None, None] for _ in range(layers)]
     extra = [time_low]
+    feed_part = attend_grads = None
     for layer in reversed(range(layers)):
         x, x_lead, qkv, p, o, mid, act, slope = kept[layer]
-        gmid, go, feed_grads = feed_back(
+        later = layer + 1 < layers
+        jobs = []
+        if later:
+            steps = own * patches // FEED
+            jobs = [
+                ("collect", feed_part, feed_count, spaced(5, steps)),
+                ("scatter", attend_grads, spaced(6, steps)),
+            ]
+        gmid, go, feed_grads, *sent = feed_back(
             gx,
             gx_lead,
             own * patches,
@@ -1180,10 +1286,17 @@
             expand_weight[layer],
             reduce_weight[layer],
             output_weight[layer],
+            Links(jobs),
+            1 + 2 * layer,
         )
+        feed_count = feed_grads.shape[0]
+        jobs = [("scatter", feed_grads, spaced(6, chunks + 1))]
+        if later:
+            fulls[layer + 1][0], attend_part = sent
+            jobs.append(("collect", attend_part, attend_grads.shape[0], spaced(5, chunks + 1)))
         if layer == layers - 1:
             gmid, output = lax.optimization_barrier((gmid, output))
-        gx, gtime, attend_grads = attend_back(
+        gx, gtime, attend_grads, feed_part, *sent = attend_back(
             qkv,
             p,
             go,
@@ -1197,17 +1310,20 @@
             row(first_shift[layer]),
             attend_weight[layer],
             F32 if layer else BF16,
+            Links(jobs),
+            2 + 2 * layer,
         )
+        if later:
+            fulls[layer + 1][1] = sent[0]
         gx_lead = 1
-        spare = jnp.zeros((-used % (devices * 32), 128), BF16)
-        buckets[layer] = jnp.concatenate(
-            [feed_grads[:big], attend_grads[:attend_big], feed_grads[big:], attend_grads[attend_big:], spare]
-        )
         extra.append(jnp.sum(gtime, axis=1).astype(BF16))
+
     extra = jnp.concatenate(extra, axis=1).reshape(-1, 128)
     lead = extra.shape[0]
     extra = jnp.pad(extra, ((0, -lead % 16), (0, 0)))
-    fulls, gathered, input_grad = final_exchange(buckets, extra, gx, 2 * CHUNK, own, part)
+    fulls[0][0], fulls[0][1], gathered, input_grad = final_exchange(
+        feed_part, feed_count, attend_grads, extra, gx, 2 * CHUNK, own, part
+    )
     input_grad = input_grad.reshape(tokens.shape)
     gathered = gathered.reshape(devices, -1, 128)[:, :lead].reshape(devices * own, -1)
     grad_time = jnp.stack(
@@ -1222,31 +1338,31 @@
         ]
     )
     grad_reduce, grad_expand, grad_attend, grad_output = unpack(fulls, width, expand_weight.shape[2])
-    small = jnp.stack([full[big + attend_big : used] for full in fulls]).astype(F32)
+    feed_small = jnp.stack([full[0][feed_big : feed_big + 32] for full in fulls]).astype(F32)
+    attend_small = jnp.stack([full[1][attend_big : attend_big + lines + 16] for full in fulls])
+    attend_small = attend_small.astype(F32)
     each = width // 128
 
-    def vector(at, count):
+    def vector(small, at, count):
         return small[:, at : at + count].reshape(layers, count * 128)
 
-    grad_rows = small[:, feed_small : feed_small + lines]
-    (grad_offset,) = bias_pull(grad_rows.reshape(layers * heads, 2, -1, QBLOCK))
-    tail = feed_small + lines
+    (grad_offset,) = bias_pull(attend_small[:, :lines].reshape(layers * heads, 2, -1, QBLOCK))
     return (
         output,
         input_grad,
-        vector(tail, each),
-        vector(tail + each, each),
+        vector(attend_small, lines, each),
+        vector(attend_small, lines + each, each),
         grad_attend,
         grad_time,
         grad_offset.reshape(layers, heads, entries),
         grad_output,
-        vector(each, each),
-        vector(2 * each, each),
-        vector(3 * each, each),
+        vector(feed_small, each, each),
+        vector(feed_small, 2 * each, each),
+        vector(feed_small, 3 * each, each),
         grad_expand,
-        vector(4 * each, expand_weight.shape[2] // 128),
+        vector(feed_small, 4 * each, expand_weight.shape[2] // 128),
         grad_reduce,
-        vector(0, each),
+        vector(feed_small, 0, each),
     )
 
 

time: 533 us -> 505 us (0.947)
  Pallas kernels: 447 us -> 425 us
  local copies, waits for them, and re-layouts: 53.2 us -> 47.8 us
    pallas_call x5, Pallas kernels: 312 us -> 289 us  [the longest x2 112 us: attend_back(): pl.pallas_call(links.host(kernel, 11, 3, 6), grid=(steps,), in_specs=[pl....]
    unnamed x76 -> x59, local copies, waits for them, and re-layouts: 17.8 us -> 11.6 us
  transfers between devices with their start and end apart: 3 -> 3, of which waited for: 1 -> 1; matrix products, arithmetic and copies ran while one was open for 5% -> 6% of each run, Pallas kernels for 31% -> 33%
where the time goes in v3:
time: 505 us; the launch traced here: 500 us
  Pallas kernels  425 us (84%)
  local copies, waits for them, and re-layouts  47.8 us (9%)
  waiting for transfers between devices  13.5 us (3%)
    pallas_call x2, Pallas kernels, forward_layer(): pl.pallas_call(functools.partial(forward_kernel, pairs), grid=(steps,), i...  127 us
    pallas_call x2, Pallas kernels, attend_back(): pl.pallas_call(links.host(kernel, 11, 3, 6), grid=(steps,), in_specs=[pl....  112 us
    pallas_call x2, Pallas kernels, feed_back(): pl.pallas_call(links.host(feed_back_kernel, 10, 3, 6), grid=(patches // F...  90.6 us
    pallas_call x1, Pallas kernels, final_exchange(): pl.pallas_call(functools.partial(final_kernel, plan, lead), in_specs=[any...  86.4 us
    ppermute x2, waiting for transfers between devices, to_images(): piece = lax.ppermute(piece, 'band', pairs)  13.5 us
    unnamed x59, local copies, waits for them, and re-layouts  11.6 us
  transfers between devices with their start and end apart: 3, of which 1 were waited for; matrix products, arithmetic and copies ran while one was open for 6% of the time, Pallas kernels for 33%

profile of v3, /device:TPU:0, one launch (start us, length us, event | category | flops | bytes accessed | tf_op | source)
XLA Modules:
  0.0 499.9 jit_solution(12609136210999058618)
XLA Ops:
  0.7 2.8 dynamic-slice_bitcast_fusion.2
  3.5 3.0 collective-permute-start
  7.2 0.8 fusion.9
  12.6 0.8 fusion.23
  15.4 1.7 slice_bitcast_fusion
  17.1 0.9 slice_bitcast_fusion.6
  19.5 1.7 bitcast_dynamic-update-slice_fusion.5
  23.1 3.2 slice_bitcast_fusion.1
  26.3 1.4 slice_bitcast_fusion.4
  27.7 13.5 %collective-permute-done = bf16[4,512,384]{2,1,0:T(8,128)(2,1)} collective-permute-done((bf16[4,512,384]{2,1,0:T(8,128)(2,1)}, bf16[4,512,384]{2,1,0:T(8,128)(2,1)}, u32[]{:S(2)}, u32[]{:S(2)}) %collective-permute-start) | collective-permute-done | bytes 1572896 | tf_op jit(solution)/shard_map/ppermute | solution.py:1186
  41.2 1.7 bitcast_dynamic-update-slice_fusion.4
  42.9 1.5 dynamic-slice_bitcast_fusion.1
  44.4 1.7 collective-permute-start.1
  46.8 63.4 %block_forward.2 = (bf16[4096,1152]{1,0:T(8,128)(2,1)}, bf16[36,3,384,256]{3,2,1,0:T(8,128)(2,1)}, bf16[4864,384]{1,0:T(8,128)(2,1)}, f32[4608,384]{1,0:T(8,128)...) custom-call(bf16[4096,384]{1,0:T(8,128)(2,1)} %bitcast.121, ...), custom_call_target="tpu_custom_call" | custom-call | tf_op jit(solution)/shard_map/block_forward/pallas_call | solution.py:648
  110.1 63.4 %block_forward.3 = (bf16[4096,1152]{1,0:T(8,128)(2,1)}, bf16[36,3,384,256]{3,2,1,0:T(8,128)(2,1)}, bf16[4864,384]{1,0:T(8,128)(2,1)}, f32[4608,384]{1,0:T(8,128)...) custom-call(f32[4608,384]{1,0:T(8,128)} %get-tuple-element.60.x_new.x_old.refs_7_, ...), custom_call_target="tpu_custom_call" | custom-call | tf_op jit(solution)/shard_map/block_forward/pallas_call | solution.py:648
  173.6 2.2 slice.217
  175.8 1.3 dynamic-slice_bitcast_fusion
  178.3 2.4 copy-done.5
  181.0 1.7 bitcast_dynamic-update-slice_fusion.2
  182.8 1.7 copy-done.1
  184.4 39.6 %feed_back.2 = (f32[4096,384]{1,0:T(8,128)}, bf16[4096,384]{1,0:T(8,128)(2,1)}, bf16[11264,128]{1,0:T(8,128)(2,1)}) custom-call(bf16[4096,384]{1,0:T(8,128)(2,1)} %bitcast.124, f32[4608,384]{1,0:T(8,128)} %get-tuple-element.61.mid, bf16[4608,1536]{1,0:T(8,128)(2,1)} %get-tuple-element.62.act, bf16[4608,1536]{1,0:T(8,128)(2,1)} %get-tuple-element.63.slope, ...), custom_call_target="tpu_custom_call" | custom-call | tf_op jit(solution)/shard_map/feed_back/pallas_call | solution.py:786
  224.1 1.3 bitcast_dynamic-update-slice_fusion
  225.4 55.6 %attend_back.2 = (f32[4608,384]{1,0:T(8,128)}, f32[4,8,768]{2,1,0:T(8,128)}, bf16[4096,128]{1,0:T(8,128)(2,1)}, bf16[352,128]{1,0:T(8,128)(2,1)}) custom-call(bf16[4096,1152]{1,0:T(8,128)(2,1)} %get-tuple-element.70.refs_0_.refs_1_.refs_2_, bf16[4096,1152]{1,0:T(8,128)(2,1)} %get-tuple-element.70.refs_0_.refs_1_.refs_2_, ...), custom_call_target="tpu_custom_call" | custom-call | tf_op jit(solution)/shard_map/attend_back/pallas_call | solution.py:972
  281.0 50.9 %feed_back.3 = (f32[4096,384]{1,0:T(8,128)}, bf16[4096,384]{1,0:T(8,128)(2,1)}, bf16[11264,128]{1,0:T(8,128)(2,1)}, bf16[11264,128]{1,0:T(8,128)(2,1)}, bf16[128,128]{1,0:T(8,128)(2,1)}) custom-call(f32[4608,384]{1,0:T(8,128)} %get-tuple-element.75.refs_0_, f32[4608,384]{1,0:T(8,128)} %get-tuple-element.76.refs_1_, ...), custom_call_target="tpu_custom_call" | custom-call | tf_op jit(solution)/shard_map/feed_back/pallas_call | solution.py:786
  331.9 56.6 %attend_back.3 = (bf16[4608,384]{1,0:T(8,128)(2,1)}, f32[4,8,768]{2,1,0:T(8,128)}, bf16[4096,128]{1,0:T(8,128)(2,1)}, bf16[352,128]{1,0:T(8,128)(2,1)}, bf16[4096,128]{1,0:T(8,128)(2,1)}) custom-call(bf16[4096,1152]{1,0:T(8,128)(2,1)} %get-tuple-element.68.refs_0_.refs_1_.refs_2_, bf16[4096,1152]{1,0:T(8,128)(2,1)} %get-tuple-element.68.refs_0_.refs_1_.refs_2_, ...), custom_call_target="tpu_custom_call" | custom-call | tf_op jit(solution)/shard_map/attend_back/pallas_call | solution.py:972
  388.5 0.9 reduce_sum.19
  390.3 86.4 %final_exchange.1 = (bf16[11264,128]{1,0:T(8,128)(2,1)}, bf16[4096,128]{1,0:T(8,128)(2,1)}, bf16[2048,128]{1,0:T(8,128)(2,1)}, bf16[2,4,512,384]{3,2,1,0:T(8,128)(2,1)}) custom-call(bf16[352,128]{1,0:T(8,128)(2,1)} %get-tuple-element.86.refs_0_, bf16[4096,128]{1,0:T(8,128)(2,1)} %get-tuple-element.87.refs_1_, bf16[64,128]{1,0:T(8,128)(2,1)} %pad.52.refs_2_, ...), custom_call_target="tpu_custom_call" | custom-call | tf_op jit(solution)/shard_map/final_exchange/pallas_call | solution.py:1044
  478.0 1.6 reshape.138
  481.9 8.6 %unpack.1 = (f32[2,1536,384]{2,1,0:T(8,128)}, f32[2,384,1536]{2,1,0:T(8,128)}, f32[2,384,1152]{2,1,0:T(8,128)}, f32[2,384,384]{2,1,0:T(8,128)}) custom-call(bf16[11264,128]{1,0:T(8,128)(2,1)} %get-tuple-element.94.refs_0_.refs_1_.refs_3_, bf16[11264,128]{1,0:T(8,128)(2,1)} %get-tuple-element.94.refs_0_.refs_1_.refs_3_, ...), custom_call_target="tpu_custom_call" | custom-call | tf_op jit(solution)/shard_map/unpack/pallas_call | solution.py:1093
  493.9 0.8 fusion.2
  496.5 1.6 pad_maximum_fusion
  498.1 1.7 copy.79
  (122 shorter events, 22.1 us)
Async XLA Ops:
  0.6 5.8 %copy-start.23 = (s32[8]{0:T(128)S(1)}, s32[8]{0:T(128)}, u32[]{:S(2)}) copy-start(s32[8]{0:T(128)} %param.21) | copy-start | bytes 100
  0.7 6.0 %copy-start.8 = (bf16[2,384,768]{2,1,0:T(8,128)(2,1)S(1)}, bf16[2,384,768]{2,1,0:T(8,128)(2,1)}, u32[]{:S(2)}) copy-start(bf16[2,384,768]{2,1,0:T(8,128)(2,1)} %param.26) | copy-start | bytes 3538948
  3.5 11.9 %copy-start.6 = (bf16[2,1536,384]{2,1,0:T(8,128)(2,1)S(1)}, bf16[2,1536,384]{2,1,0:T(8,128)(2,1)}, u32[]{:S(2)}) copy-start(bf16[2,1536,384]{2,1,0:T(8,128)(2,1)} %param.34) | copy-start | bytes 7077892
  3.5 37.7 %collective-permute-start = (bf16[4,512,384]{2,1,0:T(8,128)(2,1)}, bf16[4,512,384]{2,1,0:T(8,128)(2,1)}, u32[]{:S(2)}, u32[]{:S(2)}) collective-permute-start(bf16[4,512,384]{2,1,0:T(8,128)(2,1)} %dynamic-slice_bitcast_fusion.2), channel_id=1, source_target_pairs={{0,1},{1,0},{2,3},{3,2},{4,5},{5,4},{6,7},{7,6},{8,9},{9,8},{10,11... | collective-permute-start | bytes 4718600 | tf_op jit(solution)/shard_map/ppermute | solution.py:1186
  6.7 0.6 copy-start.12
  9.0 0.8 copy-start.15
  14.3 2.7 copy-start.9
  14.7 3.3 copy-start.11
  19.2 2.0 copy-start.17
  19.2 2.1 copy-start.18
  19.2 2.7 copy-start.19
  19.2 2.7 copy-start.20
  19.2 3.3 copy-start.14
  21.3 5.0 %copy-start.7 = (bf16[2,384,1152]{2,1,0:T(8,128)(2,1)S(1)}, bf16[2,384,1152]{2,1,0:T(8,128)(2,1)}, u32[]{:S(2)}) copy-start(bf16[2,384,1152]{2,1,0:T(8,128)(2,1)} %param.25) | copy-start | bytes 5308420
  26.3 16.6 %copy-start.4 = (bf16[8,16,32,384]{3,2,1,0:T(8,128)(2,1)S(1)}, bf16[8,16,32,384]{3,2,1,0:T(8,128)(2,1)}, u32[]{:S(2)}) copy-start(bf16[8,16,32,384]{3,2,1,0:T(8,128)(2,1)} %param.19) | copy-start | bytes 9437188
  27.7 18.5 %copy-start.21 = (f32[2,384]{1,0:T(2,128)S(1)}, f32[2,384]{1,0:T(2,128)}, u32[]{:S(2)}) copy-start(f32[2,384]{1,0:T(2,128)} %param.35) | copy-start | bytes 9220
  27.7 18.5 %copy-start.22 = (f32[2,384]{1,0:T(2,128)S(1)}, f32[2,384]{1,0:T(2,128)}, u32[]{:S(2)}) copy-start(f32[2,384]{1,0:T(2,128)} %param.29) | copy-start | bytes 9220
  42.9 3.9 copy-start
  44.4 136.6 %collective-permute-start.1 = (bf16[4,512,384]{2,1,0:T(8,128)(2,1)}, bf16[4,512,384]{2,1,0:T(8,128)(2,1)}, u32[]{:S(2)}, u32[]{:S(2)}) collective-permute-start(bf16[4,512,384]{2,1,0:T(8,128)(2,1)} %dynamic-slice_bitcast_fusion.1), channel_id=1, source_target_pairs={{0,1},{1,0},{2,3},{3,2},{4,5},{5,4},{6,7},{7,6},{8,9},{9,8},{10,11... | collective-permute-start | bytes 4718600 | tf_op jit(solution)/shard_map/ppermute | solution.py:1186
  177.1 47.0 %collective-permute-start.2 = (bf16[4,512,384]{2,1,0:T(8,128)(2,1)}, bf16[4,512,384]{2,1,0:T(8,128)(2,1)S(1)}, u32[]{:S(2)}, u32[]{:S(2)}) collective-permute-start(bf16[4,512,384]{2,1,0:T(8,128)(2,1)} %dynamic-slice_bitcast_fusion), channel_id=1, source_target_pairs={{0,1},{1,0},{2,3},{3,2},{4,5},{5,4},{6,7},{7,6},{8,9},{9,8},{10,11... | collective-permute-start | bytes 4718600 | tf_op jit(solution)/shard_map/ppermute | solution.py:1197
  177.7 3.0 copy-start.5
  178.0 3.0 copy-start.3
  182.8 1.7 copy-start.1
  331.9 57.6 %copy-start.10 = (f32[4,8,768]{2,1,0:T(8,128)S(1)}, f32[4,8,768]{2,1,0:T(8,128)}, u32[]{:S(2)}) copy-start(f32[4,8,768]{2,1,0:T(8,128)} %get-tuple-element.88) | copy-start | bytes 294916
  331.9 57.6 %copy-start.13 = (bf16[4,192]{1,0:T(4,128)(2,1)S(1)}, bf16[4,192]{1,0:T(4,128)(2,1)}, u32[]{:S(2)}) copy-start(bf16[4,192]{1,0:T(4,128)(2,1)} %copy-done.12) | copy-start | bytes 4612
  481.9 12.0 %copy-start.16 = (s32[567]{0:T(1024)S(1)}, s32[567]{0:T(1024)}, u32[]{:S(2)}) copy-start(s32[567]{0:T(1024)} %copy-done.15) | copy-start | bytes 6808
  493.9 4.2 copy-start.2

commit v4 on v3

--- a/solution.py
+++ b/solution.py
@@ -91,26 +91,52 @@
     return ref.at[pl.ds(pl.multiple_of(at, 16), rows), :]
 
 
+def both(first, second):
+    first()
+    second()
+
+
+def dispatch(step, acts):
+    whens = sorted(acts)
+    if len(whens) <= 1:
+        for when in whens:
+            pl.when(step == when)(acts[when])
+        return
+    middle = whens[len(whens) // 2]
+    low = {when: acts[when] for when in whens if when < middle}
+    high = {when: acts[when] for when in whens if when >= middle}
+    pl.when(step < middle)(lambda: dispatch(step, low))
+    pl.when(step >= middle)(lambda: dispatch(step, high))
+
+
+def mod(v, n):
+    return jnp.bitwise_and(v, n - 1) if n & (n - 1) == 0 else lax.rem(v, n)
+
+
+def halved(v, n):
+    return jnp.right_shift(v, n.bit_length() - 1) if n & (n - 1) == 0 else v // n
+
+
 class Places:
     def __init__(self, plan):
         self.xs, self.bs, self.zs = plan
         self.img = lax.axis_index("img")
         self.b = lax.axis_index("band")
-        self.c = lax.rem(self.img, 2)
-        self.x = lax.rem(self.img // 2, self.xs)
-        self.z = self.img // (2 * self.xs)
+        self.c = mod(self.img, 2)
+        self.x = mod(halved(self.img, 2), self.xs)
+        self.z = halved(self.img, 2 * self.xs)
 
     def core(self, by):
         return (self.img + 1 - 2 * self.c, self.b)
 
     def along_x(self, by):
-        return ((self.z * self.xs + lax.rem(self.x + by, self.xs)) * 2 + self.c, self.b)
+        return ((self.z * self.xs + mod(self.x + by, self.xs)) * 2 + self.c, self.b)
 
     def along_b(self, by):
-        return (self.img, lax.rem(self.b + by, self.bs))
+        return (self.img, mod(self.b + by, self.bs))
 
     def along_z(self, by):
-        return ((lax.rem(self.z + by, self.zs) * self.xs + self.x) * 2 + self.c, self.b)
+        return ((mod(self.z + by, self.zs) * self.xs + self.x) * 2 + self.c, self.b)
 
     def greet(self):
         barrier = pltpu.get_barrier_semaphore()
@@ -194,10 +220,10 @@
     def wide_copies(at):
         made = []
         for by in range(1, xs):
-            there = lax.rem(at.x + by, xs)
+            there = mod(at.x + by, xs)
             made.append((cut(acc, there * nx, nx), cut(r2a, (by - 1) * nx, nx), at.along_x(by)))
         for by in range(1, bs):
-            there = quarter + lax.rem(at.b + by, bs) * nb
+            there = quarter + mod(at.b + by, bs) * nb
             made.append((cut(acc, there, nb), cut(r2b, (by - 1) * nb, nb), at.along_b(by)))
         return made
 
@@ -210,10 +236,10 @@
     def cross_copies(at):
         made = []
         for by in range(1, bs):
-            there = at.x * nx + lax.rem(at.b + by, bs) * n2
+            there = at.x * nx + mod(at.b + by, bs) * n2
             made.append((cut(acc, there, n2), cut(r3a, (by - 1) * n2, n2), at.along_b(by)))
         for by in range(1, xs):
-            there = quarter + at.b * nb + lax.rem(at.x + by, xs) * n2
+            there = quarter + at.b * nb + mod(at.x + by, xs) * n2
             made.append((cut(acc, there, n2), cut(r3b, (by - 1) * n2, n2), at.along_x(by)))
         return made
 
@@ -230,7 +256,7 @@
     def deep_copies(at):
         made = []
         for by in range(1, zs):
-            there = lax.rem(at.z + by, zs) * n
+            there = mod(at.z + by, zs) * n
             for k, low in enumerate(plane(at)):
                 slot = (2 * (by - 1) + k) * n
                 made.append((cut(acc, low + there, n), cut(r4, slot, n), at.along_z(by)))
@@ -311,23 +337,6 @@
 
     for copies in (deep, cross, wide, core):
         lane.add(copies)
-
-
-def bands_lane(lane, whole, lead, out):
-    bs = lane.plan[1]
-    rows, width = out.shape[2:]
-    own = out.shape[1]
-
-    def copies(at):
-        made = []
-        for by in range(bs):
-            there = lax.rem(at.b + by, bs)
-            for i in range(own):
-                src = cut(whole, lead + (i * bs + there) * rows, rows)
-                made.append((src, out.at[at.b, i], at.along_b(by) if by else None))
-        return made
-
-    lane.add(copies)
 
 
 def link_plan():
@@ -366,64 +375,123 @@
     ]
 
 
+def images_copies(shard, at, own, part, images):
+    made = []
+    for by in range(at.bs):
+        there = mod(at.b + by, at.bs)
+        for i in images:
+            made.append(((there * own + i) * part, (i * at.bs + at.b) * part, by))
+    return made
+
+
 class Links:
     def __init__(self, jobs):
         self.jobs = jobs
         self.plan = link_plan()
         xs, bs, zs = self.plan
-        self.devices = 2 * xs * bs * zs
         self.arrays = [job[1] for job in jobs]
         self.shapes, self.scratch = [], []
+        remote = local = 0
         for job in jobs:
-            if job[0] == "scatter":
-                rows = job[1].shape[0] // self.devices
-                self.scratch += held_shapes(self.plan, job[1].shape[0])
-            else:
-                rows = job[2]
-            self.shapes.append(jax.ShapeDtypeStruct((rows, 128), BF16))
+            if job[0] == "sum":
+                for _, rows in self.runs(job):
+                    self.scratch += held_shapes(self.plan, rows)
+                    remote += 2 * (1 + 2 * (xs - 1 + bs - 1) + 2 * (zs - 1))
+                    local += 3
+                self.shapes.append(jax.ShapeDtypeStruct(job[1].shape, BF16))
+                continue
+            width = job[1].shape[1]
+            own, part = job[2][-2:]
+            shape = (bs, own, part, width) if job[0] == "bands" else (own * bs * part, width)
+            self.shapes.append(jax.ShapeDtypeStruct(shape, BF16))
+            self.scratch.append(pltpu.VMEM((own, part, width), BF16))
+            remote += (bs - 1) * own
+            local += 2 * own
         if jobs:
-            self.scratch += sems_shapes(self.plan, len(jobs))
+            self.scratch += [
+                pltpu.SemaphoreType.DMA((max(remote, 1),)),
+                pltpu.SemaphoreType.DMA((max(remote, 1),)),
+                pltpu.SemaphoreType.DMA((local,)),
+            ]
         self.specs = [pl.BlockSpec(memory_space=pl.ANY)] * len(jobs)
 
+    def runs(self, job):
+        unit = padded_rows(1)
+        units = job[1].shape[0] // unit
+        lanes = min(len(job[-1]), units)
+        ends = [units * i // lanes * unit for i in range(lanes + 1)]
+        return [(low, high - low) for low, high in zip(ends, ends[1:])]
+
     def host(self, kernel, ins, outs, scratch):
-        if not self.jobs:
-            return kernel
-
         def run(*refs):
             count = len(self.jobs)
             a, b, c = ins, ins + count, ins + count + outs
             d, e = c + count, c + count + scratch
             step = pl.program_id(0)
-            self.carry(step, refs[a:b], refs[c:d], refs[e:])
-            kernel(*refs[:a], *refs[b:c], *refs[d:e])
+            acts = kernel(*refs[:a], *refs[b:c], *refs[d:e]) or {}
+            if self.jobs:
+                parts = self.parts(refs[a:b], refs[c:d], refs[e:])
+                parts.setdefault(0, [])
+                for when in sorted(parts):
+
+                    def act(when=when):
+                        if when == 0:
+                            Places(self.plan).greet()
+                        for lane, part in parts[when]:
+                            lane.part(part)
+
+                    at = min(when, pl.num_programs(0) - 1)
+                    before = acts.get(at)
+                    acts[at] = act if before is None else functools.partial(both, before, act)
+            dispatch(step, acts)
 
         return run
 
-    def carry(self, step, given, made, scratch):
+    def parts(self, given, made, scratch):
         sems = Sems(*scratch[-3:])
         held = list(scratch[:-3])
         parts = {}
+        lanes = []
         for job, ref, out in zip(self.jobs, given, made):
+            if job[0] == "sum":
+                for (low, rows), whens in zip(self.runs(job), job[-1]):
+                    lane = Lane(self.plan, sems)
+                    part_in, part_out = ref.at[pl.ds(low, rows), :], out.at[pl.ds(low, rows), :]
+                    collect_lane(lane, scatter_lane(lane, part_in, held[:7]), part_out)
+                    held = held[7:]
+                    lanes.append((lane, whens))
+                continue
+            own, part = job[2][-2:]
+            lead = job[2][0] if job[0] == "bands" else 0
+
+            def copies(at, kind=job[0], ref=ref, out=out, own=own, part=part, lead=lead):
+                made = []
+                for i in range(own):
+                    for by in range(self.plan[1]):
+                        there = mod(at.b + by, self.plan[1])
+                        if kind == "bands":
+                            src = cut(ref, lead + (i * self.plan[1] + there) * part, part)
+                            dst = out.at[at.b, i]
+                        else:
+                            src = cut(ref, (there * own + i) * part, part)
+                            dst = cut(out, (i * self.plan[1] + at.b) * part, part)
+                        made.append((i, src, dst, at.along_b(by) if by else None))
+                return made
+
             lane = Lane(self.plan, sems)
-            if job[0] == "scatter":
-                scatter_lane(lane, ref, held[:7], out)
-                held = held[7:]
-            else:
-                rows = ref.shape[0] // 2
-                collect_lane(
-                    lane, lambda at, ref=ref, rows=rows: [cut(ref, k * rows, rows) for k in range(2)], out
-                )
-            assert len(job[-1]) == len(lane.steps) + 1
-            for part, when in enumerate(job[-1]):
+            lane.add(lambda at, f=copies: [c[1:] for c in f(at) if c[3] is not None])
+            lanes.append((lane, [job[-1][0], job[-1][-1]]))
+            lane = Lane(self.plan, sems)
+            here = held[0]
+            held = held[1:]
+            lane.add(lambda at, f=copies, h=here: [(c[1], h.at[c[0]], None) for c in f(at) if c[3] is None])
+            lane.add(lambda at, f=copies, h=here: [(h.at[c[0]], c[2], None) for c in f(at) if c[3] is None])
+            lanes.append((lane, job[-1]))
+        for lane, whens in lanes:
+            assert len(whens) == len(lane.steps) + 1
+            for part, when in enumerate(whens):
                 parts.setdefault(when, []).append((lane, part))
-        for when in sorted(parts):
-
-            @pl.when(step == when)
-            def _(when=when):
-                if when == 0:
-                    Places(self.plan).greet()
-                for lane, part in parts[when]:
-                    lane.part(part)
+        return parts
 
     def params(self, number):
         if not self.jobs:
@@ -627,11 +695,55 @@
     return pl.BlockSpec(shape, lambda g: zeros, pipeline_mode=pl.Buffered(1))
 
 
-def forward_layer(x, x_lead, chunks, chunks_per_image, tproj, mask, bias_rows, weights, out_dtype):
+def layer_spec(shape, layer):
+    index = (layer,) + (0,) * (len(shape) - 1)
+    return pl.BlockSpec((None,) + shape[1:], lambda g: index, pipeline_mode=pl.Buffered(1))
+
+
+def first_forward_kernel(pairs, plan, chunks, own, part, shard, *refs):
+    ins, outs, scratch = refs[:14], refs[14:22], refs[22:]
+    x_all, send_sems, recv_sems, own_sems = scratch[-4:]
+    step = pl.program_id(0)
+    sems = Sems(send_sems, recv_sems, own_sems)
+    lanes = []
+    for i in range(own):
+        lane = Lane(plan, sems)
+
+        def copies(at, i=i):
+            return [
+                (cut(shard, src, part), cut(x_all, dst, part), at.along_b(by) if by else None)
+                for src, dst, by in images_copies(shard, at, own, part, (i,))
+            ]
+
+        lane.add(copies)
+        lanes.append(lane)
+    for i in range(own):
+
+        @pl.when(step == i * (chunks // own))
+        def _(i=i):
+            if i == 0:
+                Places(plan).greet()
+                for lane in lanes:
+                    lane.part(0)
+            lanes[i].part(1)
+
+    def chunk(lead):
+        at = jnp.clip(step - lead, 0, chunks - 1) * CHUNK
+        return x_all.at[pl.ds(pl.multiple_of(at, CHUNK), CHUNK), :]
+
+    x_copy = outs[-1]
+    x_copy[...] = chunk(0)[...]
+    forward_kernel(pairs, chunk(0), chunk(2), *ins, *outs[:-1], *scratch[:-4])
+
+
+def forward_layer(
+    x, x_lead, chunks, chunks_per_image, tproj, mask, bias_rows, layer, weights, out_dtype, links, own, part, number
+):
     width = x.shape[1]
-    hidden = weights[7].shape[1]
+    hidden = weights[7].shape[2]
     pairs = width // 128
     steps = chunks + 2
+    first = layer == 0
 
     def at(lead, least=0):
         def index(g):
@@ -643,48 +755,76 @@
     row = pl.BlockSpec((CHUNK, width), lambda g: (g, 0))
     wide = pl.BlockSpec((CHUNK, hidden), lambda g: (g, 0))
     rows = steps * CHUNK
-    gain1, shift1, wqkv, wo, bo, gain2, shift2, w1, b1, w2, b2 = weights
-    consts = [gain1, shift1, wqkv, wo, bo, gain2, shift2, w1, b1, w2, b2]
-    return pl.pallas_call(
-        functools.partial(forward_kernel, pairs),
-        grid=(steps,),
-        in_specs=[
+    if first:
+        x_specs, x_args = [pl.BlockSpec(memory_space=pl.ANY)], [x]
+    else:
+        x_specs = [
             pl.BlockSpec((CHUNK, width), lambda g: (new_at(g) + x_lead, 0)),
             pl.BlockSpec((CHUNK, width), lambda g: (old_at(g) + x_lead, 0)),
-            pl.BlockSpec((1, 1, 3 * width), lambda g: (new_at(g) // chunks_per_image, 0, 0)),
-            pl.BlockSpec((1, 1, CHUNK + 2 * HALO), lambda g: (attn_at(g), 0, 0)),
-            const_spec(bias_rows.shape),
         ]
-        + [const_spec(w.shape) for w in consts],
-        out_specs=[
-            pl.BlockSpec((CHUNK, 3 * width), lambda g: (new_at(g), 0)),
-            pl.BlockSpec((CHUNK // QBLOCK, pairs, KWIN, 2 * QBLOCK), lambda g: (g, 0, 0, 0)),
-            pl.BlockSpec((CHUNK, width), lambda g: (g + 1, 0)),
-            row,
-            wide,
-            wide,
-            row,
-        ],
-        out_shape=[
-            jax.ShapeDtypeStruct((chunks * CHUNK, 3 * width), BF16),
-            jax.ShapeDtypeStruct((steps * (CHUNK // QBLOCK), pairs, KWIN, 2 * QBLOCK), BF16),
-            jax.ShapeDtypeStruct((rows + CHUNK, width), BF16),
-            jax.ShapeDtypeStruct((rows, width), F32),
-            jax.ShapeDtypeStruct((rows, hidden), BF16),
-            jax.ShapeDtypeStruct((rows, hidden), BF16),
-            jax.ShapeDtypeStruct((rows, width), out_dtype),
-        ],
-        scratch_shapes=[
-            pltpu.VMEM((pairs, KWIN, 2 * QBLOCK), F32),
-            pltpu.VMEM((CHUNK, width), BF16),
-            pltpu.VMEM((HALO + 2 * CHUNK, width), BF16),
-            pltpu.VMEM((width, HALO + 2 * CHUNK), BF16),
-            pltpu.VMEM((CHUNK, width), BF16),
-            pltpu.VMEM((CHUNK // QBLOCK, pairs, KWIN, 2 * QBLOCK), F32),
-        ],
-        compiler_params=pltpu.CompilerParams(vmem_limit_bytes=VMEM_BYTES),
+        x_args = [x, x]
+    in_specs = x_specs + [
+        pl.BlockSpec((1, 1, 3 * width), lambda g: (new_at(g) // chunks_per_image, 0, 0)),
+        pl.BlockSpec((1, 1, CHUNK + 2 * HALO), lambda g: (attn_at(g), 0, 0)),
+        layer_spec(bias_rows.shape, layer),
+    ]
+    in_specs += [layer_spec(w.shape, layer) for w in weights]
+    out_specs = [
+        pl.BlockSpec((CHUNK, 3 * width), lambda g: (new_at(g), 0)),
+        pl.BlockSpec((CHUNK // QBLOCK, pairs, KWIN, 2 * QBLOCK), lambda g: (g, 0, 0, 0)),
+        pl.BlockSpec((CHUNK, width), lambda g: (g + 1, 0)),
+        row,
+        wide,
+        wide,
+        row,
+    ]
+    out_shape = [
+        jax.ShapeDtypeStruct((chunks * CHUNK, 3 * width), BF16),
+        jax.ShapeDtypeStruct((steps * (CHUNK // QBLOCK), pairs, KWIN, 2 * QBLOCK), BF16),
+        jax.ShapeDtypeStruct((rows + CHUNK, width), BF16),
+        jax.ShapeDtypeStruct((rows, width), F32),
+        jax.ShapeDtypeStruct((rows, hidden), BF16),
+        jax.ShapeDtypeStruct((rows, hidden), BF16),
+        jax.ShapeDtypeStruct((rows, width), out_dtype),
+    ]
+    scratch = [
+        pltpu.VMEM((pairs, KWIN, 2 * QBLOCK), F32),
+        pltpu.VMEM((CHUNK, width), BF16),
+        pltpu.VMEM((HALO + 2 * CHUNK, width), BF16),
+        pltpu.VMEM((width, HALO + 2 * CHUNK), BF16),
+        pltpu.VMEM((CHUNK, width), BF16),
+        pltpu.VMEM((CHUNK // QBLOCK, pairs, KWIN, 2 * QBLOCK), F32),
+    ]
+    params = links.params(number)
+    if first:
+        plan = link_plan()
+        remote = max((plan[1] - 1) * own, 1)
+        kernel = functools.partial(first_forward_kernel, pairs, plan, chunks, own, part)
+        out_specs.append(pl.BlockSpec((CHUNK, width), lambda g: (new_at(g), 0)))
+        out_shape.append(jax.ShapeDtypeStruct((chunks * CHUNK, width), BF16))
+        scratch += [
+            pltpu.VMEM((chunks * CHUNK, width), BF16),
+            pltpu.SemaphoreType.DMA((remote,)),
+            pltpu.SemaphoreType.DMA((remote,)),
+            pltpu.SemaphoreType.DMA((own,)),
+        ]
+        params = pltpu.CompilerParams(
+            vmem_limit_bytes=VMEM_BYTES, collective_id=number, has_side_effects=True
+        )
+    else:
+        kernel = links.host(
+            functools.partial(forward_kernel, pairs), len(in_specs), len(out_specs), len(scratch)
+        )
+    return pl.pallas_call(
+        kernel,
+        grid=(steps,),
+        in_specs=in_specs + links.specs,
+        out_specs=out_specs + links.specs,
+        out_shape=out_shape + links.shapes,
+        scratch_shapes=scratch + links.scratch,
+        compiler_params=params,
         name="block_forward",
-    )(x, x, tproj, mask, bias_rows, *consts)
+    )(*x_args, tproj, mask, bias_rows, *weights, *links.arrays)
 
 
 def put_tiles(out, first, acc):
@@ -775,7 +915,9 @@
     return tiles * width, -(-(4 * width + hidden) // 128 // 16) * 16
 
 
-def feed_back(gx, gx_lead, patches, mid, act, slope, o, gain2, shift2, w1, w2, wo, links, number):
+def feed_back(
+    gx, gx_lead, patches, mid, act, slope, o, layer, gain2, shift2, w1, w2, wo, links, number
+):
     width = mid.shape[1]
     hidden = act.shape[1]
 
@@ -793,7 +935,7 @@
             rows(hidden, 1),
             rows(width, 1),
         ]
-        + [const_spec(w.shape) for w in (gain2, shift2, w1, w2, wo)]
+        + [layer_spec(w.shape, layer) for w in (gain2, shift2, w1, w2, wo)]
         + links.specs,
         out_specs=[rows(width, 0), rows(width, 0), const_spec((grad_rows, 128))] + links.specs,
         out_shape=[
@@ -814,6 +956,91 @@
         compiler_params=links.params(number),
         name="feed_back",
     )(gx, mid, act, slope, o, gain2, shift2, w1, w2, wo, *links.arrays)
+
+
+class Pusher:
+    SLOTS = 8
+
+    def __init__(self, plan, own, part, refs):
+        self.plan, self.own, self.part = plan, own, part
+        self.out, self.slots, self.send, self.recv, self.local = refs
+        self.piece = min(part, CHUNK)
+        self.subs = part // self.piece
+        self.at = Places(plan)
+
+    def each(self, chunk, act):
+        at, bs = self.at, self.plan[1]
+        whole = bs * self.part
+        slot = chunk % self.SLOTS
+        for k in range(CHUNK // self.piece):
+            row = chunk * CHUNK + k * self.piece
+            image, within = divmod(row, whole)
+            target, sub = within // self.part, within % self.part // self.piece
+            src = self.slots.at[slot, pl.ds(k * self.piece, self.piece), :]
+            dst = self.out.at[at.b, image, pl.ds(sub * self.piece, self.piece), :]
+            sem = slot * (CHUNK // self.piece) + k
+
+            @pl.when(at.b == target)
+            def _():
+                act(pltpu.make_async_copy(src, dst, self.local.at[sem]), False)
+
+            @pl.when(at.b != target)
+            def _():
+                by = mod(target - at.b + bs, bs)
+                copy = pltpu.make_async_remote_copy(
+                    src_ref=src,
+                    dst_ref=dst,
+                    send_sem=self.send.at[sem],
+                    recv_sem=self.recv.at[((by - 1) * self.own + image) * self.subs + sub],
+                    device_id=(at.img, target),
+                    device_id_type=pl.DeviceIdType.MESH,
+                )
+                act(copy, True)
+
+    def start(self, chunk):
+        self.each(chunk, lambda copy, remote: copy.start())
+
+    def sent(self, chunk):
+        self.each(chunk, lambda copy, remote: copy.wait_send() if remote else copy.wait())
+
+    def received(self):
+        at, bs = self.at, self.plan[1]
+        for by in range(1, bs):
+            sender = mod(at.b - by + bs, bs)
+            for image in range(self.own):
+                for sub in range(self.subs):
+                    pltpu.make_async_remote_copy(
+                        src_ref=self.slots.at[0, pl.ds(0, self.piece), :],
+                        dst_ref=self.out.at[sender, image, pl.ds(sub * self.piece, self.piece), :],
+                        send_sem=self.send.at[0],
+                        recv_sem=self.recv.at[((by - 1) * self.own + image) * self.subs + sub],
+                        device_id=(at.img, sender),
+                        device_id_type=pl.DeviceIdType.MESH,
+                    ).wait_recv()
+
+
+def last_attend_back_kernel(pairs, chunks, chunks_per_image, plan, own, part, *refs):
+    ins, outs, scratch = refs[:11], refs[11:14], refs[14:]
+    out, slots = outs[0], scratch[6]
+    step = pl.program_id(0)
+    pusher = Pusher(plan, own, part, (out, slots, *scratch[7:]))
+
+    slot = slots.at[mod(step + Pusher.SLOTS - 1, Pusher.SLOTS)]
+    attend_back_kernel(pairs, chunks, chunks_per_image, *ins, slot, *outs[1:], *scratch[:6])
+    acts = {}
+    for chunk in range(chunks):
+
+        def act(chunk=chunk):
+            pusher.start(chunk)
+            if 0 <= chunk + 1 - Pusher.SLOTS and chunk < chunks - 1:
+                pusher.sent(chunk + 1 - Pusher.SLOTS)
+            if chunk == chunks - 1:
+                for old in range(max(chunks - Pusher.SLOTS, 0), chunks):
+                    pusher.sent(old)
+                pusher.received()
+
+        acts[chunk + 1] = act
+    return acts
 
 
 def attend_back_kernel(
@@ -945,10 +1172,12 @@
     x_lead,
     chunks,
     chunks_per_image,
+    layer,
     gain1,
     shift1,
     wqkv,
-    out_dtype,
+    own,
+    part,
     links,
     number,
 ):
@@ -968,102 +1197,109 @@
 
     images = chunks // chunks_per_image
     grad_rows = padded_rows(attend_rows(width)[1])
+    in_specs = [
+        pl.BlockSpec((HALO, 3 * width), lambda g: (jnp.maximum(halves * now(g) - 1, 0), 0)),
+        rows(3 * width, 0, now),
+        pl.BlockSpec(
+            (HALO, 3 * width),
+            lambda g: (jnp.minimum(halves * (now(g) + 1), halves * chunks - 1), 0),
+        ),
+        pl.BlockSpec((CHUNK // QBLOCK, pairs, KWIN, 2 * QBLOCK), lambda g: (now(g) + 1, 0, 0, 0)),
+        rows(width, 0, now),
+        rows(width, 2, now),
+        rows(width, 0, late),
+        rows(width, x_lead, late),
+    ]
+    in_specs += [layer_spec(w.shape, layer) for w in (gain1, shift1, wqkv)]
+    out_specs = [
+        rows(width, 1, lambda g: g),
+        pl.BlockSpec((1, 8, 2 * width), lambda g: (late(g) // chunks_per_image, 0, 0)),
+        const_spec((grad_rows, 128)),
+    ]
+    out_shape = [
+        jax.ShapeDtypeStruct(((steps + 1) * CHUNK, width), F32),
+        jax.ShapeDtypeStruct((images, 8, 2 * width), F32),
+        jax.ShapeDtypeStruct((grad_rows, 128), BF16),
+    ]
+    scratch = [
+        pltpu.VMEM((width, 3 * width), F32),
+        pltpu.VMEM((pairs, KWIN, 2 * QBLOCK), F32),
+        pltpu.VMEM((2, 8, width), F32),
+        pltpu.VMEM((CHUNK, width), BF16),
+        pltpu.VMEM((2 * CHUNK + HALO, 2 * width), F32),
+        pltpu.VMEM((CHUNK // QBLOCK, pairs, KWIN, 2 * QBLOCK), BF16),
+    ]
     kernel = functools.partial(attend_back_kernel, pairs, chunks, chunks_per_image)
+    if layer == 0:
+        plan = link_plan()
+        bs = plan[1]
+        piece = min(part, CHUNK)
+        pieces = CHUNK // piece
+        kernel = functools.partial(
+            last_attend_back_kernel, pairs, chunks, chunks_per_image, plan, own, part
+        )
+        out_specs[0] = pl.BlockSpec(memory_space=pl.ANY)
+        out_shape[0] = jax.ShapeDtypeStruct((bs, own, part, width), BF16)
+        scratch += [
+            pltpu.VMEM((Pusher.SLOTS, CHUNK, width), BF16),
+            pltpu.SemaphoreType.DMA((Pusher.SLOTS * pieces,)),
+            pltpu.SemaphoreType.DMA((max((bs - 1) * own * (part // piece), 1),)),
+            pltpu.SemaphoreType.DMA((Pusher.SLOTS * pieces,)),
+        ]
     return pl.pallas_call(
-        links.host(kernel, 11, 3, 6),
+        links.host(kernel, len(in_specs), len(out_specs), len(scratch)),
         grid=(steps,),
-        in_specs=[
-            pl.BlockSpec((HALO, 3 * width), lambda g: (jnp.maximum(halves * now(g) - 1, 0), 0)),
-            rows(3 * width, 0, now),
-            pl.BlockSpec(
-                (HALO, 3 * width),
-                lambda g: (jnp.minimum(halves * (now(g) + 1), halves * chunks - 1), 0),
-            ),
-            pl.BlockSpec(
-                (CHUNK // QBLOCK, pairs, KWIN, 2 * QBLOCK), lambda g: (now(g) + 1, 0, 0, 0)
-            ),
-            rows(width, 0, now),
-            rows(width, 2, now),
-            rows(width, 0, late),
-            rows(width, x_lead, late),
-        ]
-        + [const_spec(w.shape) for w in (gain1, shift1, wqkv)]
-        + links.specs,
-        out_specs=[
-            rows(width, 1, lambda g: g),
-            pl.BlockSpec((1, 8, 2 * width), lambda g: (late(g) // chunks_per_image, 0, 0)),
-            const_spec((grad_rows, 128)),
-        ]
-        + links.specs,
-        out_shape=[
-            jax.ShapeDtypeStruct(((steps + 1) * CHUNK, width), out_dtype),
-            jax.ShapeDtypeStruct((images, 8, 2 * width), F32),
-            jax.ShapeDtypeStruct((grad_rows, 128), BF16),
-        ]
-        + links.shapes,
-        scratch_shapes=[
-            pltpu.VMEM((width, 3 * width), F32),
-            pltpu.VMEM((pairs, KWIN, 2 * QBLOCK), F32),
-            pltpu.VMEM((2, 8, width), F32),
-            pltpu.VMEM((CHUNK, width), BF16),
-            pltpu.VMEM((2 * CHUNK + HALO, 2 * width), F32),
-            pltpu.VMEM((CHUNK // QBLOCK, pairs, KWIN, 2 * QBLOCK), BF16),
-        ]
-        + links.scratch,
+        in_specs=in_specs + links.specs,
+        out_specs=out_specs + links.specs,
+        out_shape=out_shape + links.shapes,
+        scratch_shapes=scratch + links.scratch,
         compiler_params=links.params(number),
         name="attend_back",
     )(qkv, qkv, qkv, p, go, o, gmid, x, gain1, shift1, wqkv, *links.arrays)
 
 
-def final_kernel(plan, lead, *refs):
-    chunk, grad, extra, whole = refs[:4]
-    feed_out, attend_out, extra_out, bands_out = refs[4:8]
-    scratch = refs[8:]
+def final_kernel(plan, *refs):
+    grad, extra = refs[:2]
+    attend_out, extra_out = refs[2:4]
+    scratch = refs[4:]
     sems = Sems(*scratch[-3:])
     Places(plan).greet()
-    lanes = [Lane(plan, sems) for _ in range(3)]
-    rows = chunk.shape[0] // 2
-    ends = scatter_lane(lanes[0], grad, scratch[:-3])
-    collect_lane(lanes[0], ends, attend_out)
-    collect_lane(lanes[1], lambda at: [cut(chunk, k * rows, rows) for k in range(2)], feed_out)
-    extra_lane(lanes[2], extra, extra_out)
-    late = Lane(plan, sems)
-    bands_lane(late, whole, lead, bands_out)
-    late.part(0)
+    lanes = [Lane(plan, sems) for _ in range(2)]
+    collect_lane(lanes[0], scatter_lane(lanes[0], grad, scratch[:-3]), attend_out)
+    extra_lane(lanes[1], extra, extra_out)
     for i in range(max(len(lane.steps) for lane in lanes) + 1):
         for lane in lanes:
             if i <= len(lane.steps):
                 lane.part(i)
-    late.part(1)
-
-
-def final_exchange(chunk, feed_rows_all, grad, extra, whole, lead, own, part):
+
+
+def final_exchange(grad, extra):
     plan = link_plan()
     xs, bs, zs = plan
     anywhere = pl.BlockSpec(memory_space=pl.ANY)
     return pl.pallas_call(
-        functools.partial(final_kernel, plan, lead),
-        in_specs=[anywhere] * 4,
-        out_specs=[anywhere] * 4,
+        functools.partial(final_kernel, plan),
+        in_specs=[anywhere] * 2,
+        out_specs=[anywhere] * 2,
         out_shape=[
-            jax.ShapeDtypeStruct((feed_rows_all, 128), BF16),
             jax.ShapeDtypeStruct(grad.shape, BF16),
             jax.ShapeDtypeStruct((2 * xs * bs * zs * extra.shape[0], 128), BF16),
-            jax.ShapeDtypeStruct((bs, own, part, whole.shape[1]), BF16),
         ],
-        scratch_shapes=held_shapes(plan, grad.shape[0]) + sems_shapes(plan, 4, bs * own),
+        scratch_shapes=held_shapes(plan, grad.shape[0]) + sems_shapes(plan, 3),
         compiler_params=pltpu.CompilerParams(
             vmem_limit_bytes=VMEM_BYTES, collective_id=0, has_side_effects=True
         ),
         name="final_exchange",
-    )(chunk, grad, extra, whole)
-
-
-def unpack_kernel(layers, *refs):
-    ins = [refs[4 * i : 4 * i + 4] for i in range(layers)]
-    w2_out, w1_out, attend_out, wo_out = refs[4 * layers :]
+    )(grad, extra)
+
+
+def unpack_kernel(layers, lines, *refs):
+    ins = [refs[6 * i : 6 * i + 6] for i in range(layers)]
+    w2_out, w1_out, attend_out, wo_out = refs[6 * layers : 6 * layers + 4]
+    small_outs = refs[6 * layers + 4 : 6 * layers + 11]
+    rows_out = refs[6 * layers + 11]
     width = w1_out.shape[1]
-    for layer, (w2t, w1, attend, wo) in enumerate(ins):
+    for layer, (w2t, w1, attend, wo, feed_small, attend_small) in enumerate(ins):
         for j in range(w1.shape[0] // width):
             rows = slice(j * width, (j + 1) * width)
             cols = slice(j * 128, (j + 1) * 128)
@@ -1071,6 +1307,19 @@
             w1_out[layer, :, cols] = w1[rows, :].astype(F32)
             attend_out[layer, :, cols] = attend[rows, :].astype(F32)
             wo_out[layer, :, cols] = wo[rows, :].astype(F32)
+        feed = feed_small[...].astype(F32)
+        tail = attend_small[...].astype(F32)
+        rows_out[layer] = tail[:lines]
+        at = 0
+        for out in small_outs[:5]:
+            for j in range(out.shape[1] // 128):
+                out[layer : layer + 1, j * 128 : (j + 1) * 128] = feed[at : at + 1]
+                at += 1
+        at = lines
+        for out in small_outs[5:]:
+            for j in range(out.shape[1] // 128):
+                out[layer : layer + 1, j * 128 : (j + 1) * 128] = tail[at : at + 1]
+                at += 1
 
 
 def unpack(fulls, width, hidden):
@@ -1080,6 +1329,9 @@
     rows = wide * width
     last = 3 * width // width - 1
     block = (rows, 128)
+    feed_big, feed_small = feed_rows(width, hidden)
+    attend_big, attend_all, lines = attend_rows(width)
+    attend_small = attend_all - attend_big
 
     def spec(first, top):
         return pl.BlockSpec(block, lambda g: (first + jnp.minimum(g, top), 0))
@@ -1089,9 +1341,12 @@
         spec(steps, steps),
         spec(0, last),
         spec(2 * steps, 0),
+        pl.BlockSpec((feed_small, 128), lambda g: (0, 0)),
+        pl.BlockSpec((attend_small, 128), lambda g: (0, 0)),
     ]
+    vectors = [width] * 4 + [hidden] + [width] * 2
     return pl.pallas_call(
-        functools.partial(unpack_kernel, layers),
+        functools.partial(unpack_kernel, layers, lines),
         grid=(steps,),
         in_specs=ins * layers,
         out_specs=[
@@ -1099,16 +1354,33 @@
             pl.BlockSpec((layers, width, width), lambda g: (0, 0, g)),
             pl.BlockSpec((layers, width, width), lambda g: (0, 0, jnp.minimum(g, last))),
             pl.BlockSpec((layers, width, width), lambda g: (0, 0, 0)),
-        ],
+        ]
+        + [pl.BlockSpec((layers, n), lambda g: (0, 0)) for n in vectors]
+        + [pl.BlockSpec((layers, lines, 128), lambda g: (0, 0, 0))],
         out_shape=[
             jax.ShapeDtypeStruct((layers, hidden, width), F32),
             jax.ShapeDtypeStruct((layers, width, hidden), F32),
             jax.ShapeDtypeStruct((layers, width, 3 * width), F32),
             jax.ShapeDtypeStruct((layers, width, width), F32),
-        ],
+        ]
+        + [jax.ShapeDtypeStruct((layers, n), F32) for n in vectors]
+        + [jax.ShapeDtypeStruct((layers, lines, 128), F32)],
         compiler_params=pltpu.CompilerParams(vmem_limit_bytes=VMEM_BYTES),
         name="unpack",
-    )(*[ref for feed, attend in fulls for ref in (feed, feed, attend, feed)])
+    )(
+        *[
+            ref
+            for feed, attend in fulls
+            for ref in (
+                feed,
+                feed,
+                attend,
+                feed,
+                feed[feed_big : feed_big + feed_small],
+                attend[attend_big:attend_all],
+            )
+        ]
+    )
 
 
 def time_embedding(timesteps, width):
@@ -1176,32 +1448,6 @@
     per_image = patches // CHUNK
     chunks = own * per_image
 
-    def to_images(shard):
-        shard = shard.reshape(bands, own, part, width)
-        whole = jnp.zeros((own, bands, part, width), shard.dtype)
-        for by in range(bands):
-            piece = lax.dynamic_index_in_dim(shard, (me + by) % bands, 0, keepdims=False)
-            if by:
-                pairs = [(i, (i + by) % bands) for i in range(bands)]
-                piece = lax.ppermute(piece, "band", pairs)
-            whole = lax.dynamic_update_index_in_dim(whole, piece, (me - by) % bands, 1)
-        return whole.reshape(own * patches, width)
-
-    def to_bands(whole):
-        whole = whole.reshape(own, bands, part, width)
-        shard = jnp.zeros((bands, own, part, width), whole.dtype)
-        for by in range(bands):
-            piece = lax.dynamic_index_in_dim(whole, (me + by) % bands, 1, keepdims=False)
-            if by:
-                pairs = [(i, (i + by) % bands) for i in range(bands)]
-                piece = lax.ppermute(piece, "band", pairs)
-            shard = lax.dynamic_update_index_in_dim(shard, piece, (me - by) % bands, 0)
-        return shard.reshape(images, band_rows, grid_cols, width)
-
-    x0 = to_images(tokens)
-    x0, late = lax.optimization_barrier((x0, cotangent))
-    cot = to_images(late)
-
     mine = lax.dynamic_slice_in_dim(valid_mask, me * own, own, 0).reshape(own, patches)
     fill = jnp.where(mine == 1, 0.0, NEG_FILL).astype(F32)
     fill = jnp.pad(fill, ((0, 0), (HALO, HALO)), constant_values=NEG_FILL)
@@ -1220,60 +1466,73 @@
     biases, bias_pull = jax.vjp(make_rows, offset_bias.reshape(layers * heads, entries))
     biases = biases.reshape(layers, -1, QBLOCK)
 
-    def row(v):
-        return v.reshape(1, -1)
-
-    x, x_lead = x0, 0
+    def rows_of(v):
+        return v.reshape(layers, 1, -1)
+
+    tp = jnp.einsum("it,ltc->lic", time_low, time_weight, preferred_element_type=F32)
+    tproj = jnp.concatenate([tp[..., :width], jnp.zeros_like(tp[..., :width]), tp[..., width:]], -1)
+    gain1, shift1, gain2, shift2 = map(
+        rows_of, (first_gain, first_shift, second_gain, second_shift)
+    )
+    weights = (
+        gain1,
+        shift1,
+        attend_weight,
+        output_weight,
+        rows_of(output_bias),
+        gain2,
+        shift2,
+        expand_weight,
+        rows_of(expand_bias),
+        reduce_weight,
+        rows_of(reduce_bias),
+    )
+    x, x_lead = tokens.reshape(images * part, width), 0
     kept = []
     for layer in range(layers):
-        tp = jnp.dot(time_low, time_weight[layer], preferred_element_type=F32)
-        tproj = jnp.concatenate([tp[:, :width], jnp.zeros_like(tp[:, :width]), tp[:, width:]], axis=1)
-        weights = (
-            row(first_gain[layer]),
-            row(first_shift[layer]),
-            attend_weight[layer],
-            output_weight[layer],
-            row(output_bias[layer]),
-            row(second_gain[layer]),
-            row(second_shift[layer]),
-            expand_weight[layer],
-            row(expand_bias[layer]),
-            reduce_weight[layer],
-            row(reduce_bias[layer]),
-        )
-        qkv, p, o, mid, act, slope, nxt = forward_layer(
+        last = layer == layers - 1
+        jobs = []
+        if last:
+            shard = cotangent.reshape(images * part, width)
+            jobs = [("images", shard, (own, part), [0, chunks // 2, chunks + 2])]
+        qkv, p, o, mid, act, slope, nxt, *more = forward_layer(
             x,
             x_lead,
             chunks,
             per_image,
-            tproj[:, None, :],
+            tproj[layer][:, None, :],
             mask,
-            biases[layer],
+            biases,
+            layer,
             weights,
-            F32 if layer < layers - 1 else BF16,
+            BF16 if last else F32,
+            Links(jobs),
+            own,
+            part,
+            1 + layer,
         )
+        if layer == 0:
+            x = more[0]
+        if last:
+            gx = more[-1]
         kept.append((x, x_lead, qkv, p, o, mid, act, slope))
         x, x_lead = nxt, 2
-    output = to_bands(x[x_lead * CHUNK :])
-
-    gx, gx_lead = cot, 0
+
+    gx_lead = 0
     devices = bands * lax.axis_size("img")
-    feed_big = feed_rows(width, expand_weight.shape[2])[0]
-    attend_big, _, lines = attend_rows(width)
+    hidden = expand_weight.shape[2]
     fulls = [[None, None] for _ in range(layers)]
     extra = [time_low]
-    feed_part = attend_grads = None
+    attend_grads = None
+    result = x
     for layer in reversed(range(layers)):
         x, x_lead, qkv, p, o, mid, act, slope = kept[layer]
-        later = layer + 1 < layers
-        jobs = []
-        if later:
-            steps = own * patches // FEED
-            jobs = [
-                ("collect", feed_part, feed_count, spaced(5, steps)),
-                ("scatter", attend_grads, spaced(6, steps)),
-            ]
-        gmid, go, feed_grads, *sent = feed_back(
+        steps = own * patches // FEED
+        if layer == layers - 1:
+            jobs = [("bands", result, (2 * CHUNK, own, part), [0, steps // 2, steps])]
+        else:
+            jobs = [("sum", attend_grads, [spaced(9, steps + 1)])]
+        gmid, go, feed_grads, sent = feed_back(
             gx,
             gx_lead,
             own * patches,
@@ -1281,22 +1540,20 @@
             act,
             slope,
             o,
-            row(second_gain[layer]),
-            row(second_shift[layer]),
-            expand_weight[layer],
-            reduce_weight[layer],
-            output_weight[layer],
+            layer,
+            gain2,
+            shift2,
+            expand_weight,
+            reduce_weight,
+            output_weight,
             Links(jobs),
-            1 + 2 * layer,
+            1 + layers + 2 * layer,
         )
-        feed_count = feed_grads.shape[0]
-        jobs = [("scatter", feed_grads, spaced(6, chunks + 1))]
-        if later:
-            fulls[layer + 1][0], attend_part = sent
-            jobs.append(("collect", attend_part, attend_grads.shape[0], spaced(5, chunks + 1)))
         if layer == layers - 1:
-            gmid, output = lax.optimization_barrier((gmid, output))
-        gx, gtime, attend_grads, feed_part, *sent = attend_back(
+            output = sent.reshape(tokens.shape)
+        else:
+            fulls[layer + 1][1] = sent
+        gx, gtime, attend_grads, fulls[layer][0] = attend_back(
             qkv,
             p,
             go,
@@ -1306,25 +1563,23 @@
             x_lead,
             chunks,
             per_image,
-            row(first_gain[layer]),
-            row(first_shift[layer]),
-            attend_weight[layer],
-            F32 if layer else BF16,
-            Links(jobs),
-            2 + 2 * layer,
+            layer,
+            gain1,
+            shift1,
+            attend_weight,
+            own,
+            part,
+            Links([("sum", feed_grads, [spaced(9, chunks + 1), [i + 1 for i in spaced(9, chunks + 1)]])]),
+            2 + layers + 2 * layer,
         )
-        if later:
-            fulls[layer + 1][1] = sent[0]
         gx_lead = 1
         extra.append(jnp.sum(gtime, axis=1).astype(BF16))
+    input_grad = gx.reshape(tokens.shape)
 
     extra = jnp.concatenate(extra, axis=1).reshape(-1, 128)
     lead = extra.shape[0]
     extra = jnp.pad(extra, ((0, -lead % 16), (0, 0)))
-    fulls[0][0], fulls[0][1], gathered, input_grad = final_exchange(
-        feed_part, feed_count, attend_grads, extra, gx, 2 * CHUNK, own, part
-    )
-    input_grad = input_grad.reshape(tokens.shape)
+    fulls[0][1], gathered = final_exchange(attend_grads, extra)
     gathered = gathered.reshape(devices, -1, 128)[:, :lead].reshape(devices * own, -1)
     grad_time = jnp.stack(
         [
@@ -1337,32 +1592,37 @@
             for turn in reversed(range(layers))
         ]
     )
-    grad_reduce, grad_expand, grad_attend, grad_output = unpack(fulls, width, expand_weight.shape[2])
-    feed_small = jnp.stack([full[0][feed_big : feed_big + 32] for full in fulls]).astype(F32)
-    attend_small = jnp.stack([full[1][attend_big : attend_big + lines + 16] for full in fulls])
-    attend_small = attend_small.astype(F32)
-    each = width // 128
-
-    def vector(small, at, count):
-        return small[:, at : at + count].reshape(layers, count * 128)
-
-    (grad_offset,) = bias_pull(attend_small[:, :lines].reshape(layers * heads, 2, -1, QBLOCK))
+    (
+        grad_reduce,
+        grad_expand,
+        grad_attend,
+        grad_output,
+        reduce_bias_grad,
+        output_bias_grad,
+        second_gain_grad,
+        second_shift_grad,
+        expand_bias_grad,
+        first_gain_grad,
+        first_shift_grad,
+        grad_rows,
+    ) = unpack(fulls, width, hidden)
+    (grad_offset,) = bias_pull(grad_rows.reshape(layers * heads, 2, -1, QBLOCK))
     return (
         output,
         input_grad,
-        vector(attend_small, lines, each),
-        vector(attend_small, lines + each, each),
+        first_gain_grad,
+        first_shift_grad,
         grad_attend,
         grad_time,
         grad_offset.reshape(layers, heads, entries),
         grad_output,
-        vector(feed_small, each, each),
-        vector(feed_small, 2 * each, each),
-        vector(feed_small, 3 * each, each),
+        output_bias_grad,
+        second_gain_grad,
+        second_shift_grad,
         grad_expand,
-        vector(feed_small, 4 * each, expand_weight.shape[2] // 128),
+        expand_bias_grad,
         grad_reduce,
-        vector(feed_small, 0, each),
+        reduce_bias_grad,
     )
 
 

time: 505 us -> 476 us (0.943)
  local copies, waits for them, and re-layouts: 47.8 us -> 28.4 us
  waiting for transfers between devices: 13.5 us -> 0 us
  Pallas kernels: 425 us -> 437 us
    squeeze x9 -> x0, local copies, waits for them, and re-layouts: 14 us -> none  [the longest x2 4.31 us: to_images(): lax.dynamic_index_in_dim(shard, (me + by) % bands, 0, keepdims=False)]
    ppermute x3 -> x0, waiting for transfers between devices: 13.5 us -> none  [the longest x2 13.5 us: to_images(): piece = lax.ppermute(piece, 'band', pairs)]
    pallas_call x2, Pallas kernels: 90.6 us -> 103 us  [feed_back(): pl.pallas_call(links.host(feed_back_kernel, 10, 3, 6), grid=(patches // F...]
    reshape x1 -> x9, local copies, waits for them, and re-layouts: 0.01 us -> 10.5 us  [the longest x7 8.91 us: rows_of(): return v.reshape(layers, 1, -1)]
    dynamic_update_slice x6 -> x0, local copies, waits for them, and re-layouts: 7.13 us -> none  [the longest x4 5.5 us: to_images(): whole = lax.dynamic_update_index_in_dim(whole, piece, (me - by) % bands, 1)]
    unnamed x59 -> x12, local copies, waits for them, and re-layouts: 11.6 us -> 7.14 us
  transfers between devices with their start and end apart: 3 -> 0, of which waited for: 1 -> 0; matrix products, arithmetic and copies ran while one was open for 6% -> 0% of each run, Pallas kernels for 33% -> 0%
where the time goes in v4:
time: 476 us; the launch traced here: 474 us
  Pallas kernels  437 us (92%)
  local copies, waits for them, and re-layouts  28.4 us (6%)
    pallas_call x2, Pallas kernels, forward_layer(): pl.pallas_call(kernel, grid=(steps,), in_specs=in_specs + links.specs, ou...  147 us
    pallas_call x2, Pallas kernels, attend_back(): pl.pallas_call(links.host(kernel, len(in_specs), len(out_specs), len(scra...  141 us
    pallas_call x2, Pallas kernels, feed_back(): pl.pallas_call(links.host(feed_back_kernel, 10, 3, 6), grid=(patches // F...  103 us
    pallas_call x1, Pallas kernels, final_exchange(): pl.pallas_call(functools.partial(final_kernel, plan), in_specs=[anywhere]...  36.2 us

profile of v4, /device:TPU:0, one launch (start us, length us, event | category | flops | bytes accessed | tf_op | source)
XLA Modules:
  0.0 473.6 jit_solution(16850248716955254244)
XLA Ops:
  0.7 0.8 dynamic-slice_convert_fusion
  1.6 1.3 reshape.115.refs_3_.refs_5_.refs_8_
  2.9 1.3 reshape.116.refs_4_.refs_6_.refs_9_
  4.2 1.3 reshape.118.refs_8_.refs_10_.refs_5_
  5.4 1.3 reshape.119.refs_9_.refs_11_.refs_6_
  6.7 1.3 reshape.117.refs_7_.refs_9_
  8.0 1.3 reshape.121.refs_13_.refs_15_
  9.2 0.8 reshape.111
  10.1 1.3 reshape.120.refs_11_.refs_13_
  12.5 0.8 copy.44
  13.9 0.9 fusion.15
  15.0 0.7 reshape.110.refs_1_.refs_3_
  16.2 0.7 reshape.114.refs_2_.refs_4_
  16.9 80.7 %block_forward.2 = (bf16[4096,1152]{1,0:T(8,128)(2,1)}, bf16[36,3,384,256]{3,2,1,0:T(8,128)(2,1)}, bf16[4864,384]{1,0:T(8,128)(2,1)}, f32[4608,384]{1,0:T(8,128)...) custom-call(bf16[4096,384]{1,0:T(8,128)(2,1)} %bitcast.47, ...), custom_call_target="tpu_custom_call" | custom-call | tf_op jit(solution)/shard_map/block_forward/pallas_call | solution.py:818
  97.6 66.7 %block_forward.3 = (bf16[4096,1152]{1,0:T(8,128)(2,1)}, bf16[36,3,384,256]{3,2,1,0:T(8,128)(2,1)}, bf16[4864,384]{1,0:T(8,128)(2,1)}, f32[4608,384]{1,0:T(8,128)...) custom-call(f32[4608,384]{1,0:T(8,128)} %get-tuple-element.61.refs_0, ...), custom_call_target="tpu_custom_call" | custom-call | tf_op jit(solution)/shard_map/block_forward/pallas_call | solution.py:818
  164.3 46.0 %feed_back.2 = (f32[4096,384]{1,0:T(8,128)}, bf16[4096,384]{1,0:T(8,128)(2,1)}, bf16[11264,128]{1,0:T(8,128)(2,1)}, bf16[2,4,512,384]{3,2,1,0:T(8,128)(2,1)}) custom-call(bf16[4096,384]{1,0:T(8,128)(2,1)} %get-tuple-element.62.refs_0_, f32[4608,384]{1,0:T(8,128)} %get-tuple-element.63.refs_1_, bf16[4608,1536]{1,0:T(8,128)(2,1)} %get-tuple-element.64.refs_2_, ...), custom_call_target="tpu_custom_call" | custom-call | tf_op jit(solution)/shard_map/feed_back/pallas_call | solution.py:928
  210.4 62.2 %attend_back.2 = (f32[4608,384]{1,0:T(8,128)}, f32[4,8,768]{2,1,0:T(8,128)}, bf16[4096,128]{1,0:T(8,128)(2,1)}, bf16[11264,128]{1,0:T(8,128)(2,1)}) custom-call(bf16[4096,1152]{1,0:T(8,128)(2,1)} %get-tuple-element.71.refs_0_.refs_1_.refs_2_, bf16[4096,1152]{1,0:T(8,128)(2,1)} %get-tuple-element.71.refs_0_.refs_1_.refs_2_, ...), custom_call_target="tpu_custom_call" | custom-call | tf_op jit(solution)/shard_map/attend_back/pallas_call | solution.py:1249
  272.6 57.3 %feed_back.3 = (f32[4096,384]{1,0:T(8,128)}, bf16[4096,384]{1,0:T(8,128)(2,1)}, bf16[11264,128]{1,0:T(8,128)(2,1)}, bf16[4096,128]{1,0:T(8,128)(2,1)}) custom-call(f32[4608,384]{1,0:T(8,128)} %get-tuple-element.76.refs_0_, f32[4608,384]{1,0:T(8,128)} %get-tuple-element.77.refs_1_, bf16[4608,1536]{1,0:T(8,128)(2,1)} %get-tuple-element.78.refs_2_, ...), custom_call_target="tpu_custom_call" | custom-call | tf_op jit(solution)/shard_map/feed_back/pallas_call | solution.py:928
  329.9 79.1 %attend_back.3 = (bf16[2,4,512,384]{3,2,1,0:T(8,128)(2,1)}, f32[4,8,768]{2,1,0:T(8,128)}, bf16[4096,128]{1,0:T(8,128)(2,1)}, bf16[11264,128]{1,0:T(8,128)(2,1)}) custom-call(bf16[4096,1152]{1,0:T(8,128)(2,1)} %get-tuple-element.69.refs_0_.refs_1_.refs_2_, bf16[4096,1152]{1,0:T(8,128)(2,1)} %get-tuple-element.69.refs_0_.refs_1_.refs_2_, ...), custom_call_target="tpu_custom_call" | custom-call | tf_op jit(solution)/shard_map/attend_back/pallas_call | solution.py:1249
  409.0 0.9 reduce_sum.19
  410.7 1.3 slice.68.refs_4_
  412.0 1.3 slice.70.refs_10_
  413.3 1.4 slice.71.refs_11_
  414.7 36.2 %final_exchange.1 = (bf16[4096,128]{1,0:T(8,128)(2,1)}, bf16[2048,128]{1,0:T(8,128)(2,1)}) custom-call(bf16[4096,128]{1,0:T(8,128)(2,1)} %get-tuple-element.88.refs_0_, bf16[64,128]{1,0:T(8,128)(2,1)} %pad.52.refs_1_), custom_call_target="tpu_custom_call" | custom-call | tf_op jit(solution)/shard_map/final_exchange/pallas_call | solution.py:1280
  450.8 1.6 reshape.127
  452.4 1.4 slice.69.refs_5_
  454.5 1.6 pad_maximum_fusion
  456.1 8.8 %unpack.1 = (f32[2,1536,384]{2,1,0:T(8,128)}, f32[2,384,1536]{2,1,0:T(8,128)}, f32[2,384,1152]{2,1,0:T(8,128)}, f32[2,384,384]{2,1,0:T(8,128)}, f32[2,384]{1,0:T...) custom-call(bf16[11264,128]{1,0:T(8,128)(2,1)} %get-tuple-element.87, ...), custom_call_target="tpu_custom_call" | custom-call | tf_op jit(solution)/shard_map/unpack/pallas_call | solution.py:1348
  464.9 0.9 reshape.128
  466.3 0.8 fusion.2
  467.7 4.1 copy.53
  471.8 1.7 copy.54
  (48 shorter events, 5.1 us)
Async XLA Ops:
  0.6 10.8 %copy-start = (bf16[2,384,768]{2,1,0:T(8,128)(2,1)S(1)}, bf16[2,384,768]{2,1,0:T(8,128)(2,1)}, u32[]{:S(2)}) copy-start(bf16[2,384,768]{2,1,0:T(8,128)(2,1)} %param.26) | copy-start | bytes 3538948
  329.9 80.0 %copy-start.3 = (f32[4,8,768]{2,1,0:T(8,128)S(1)}, f32[4,8,768]{2,1,0:T(8,128)}, u32[]{:S(2)}) copy-start(f32[4,8,768]{2,1,0:T(8,128)} %get-tuple-element.89) | copy-start | bytes 294916
  467.7 4.1 copy-start.2
  467.7 5.7 %copy-start.1 = (bf16[2,384,768]{2,1,0:T(8,128)(2,1)S(1)}, bf16[2,384,768]{2,1,0:T(8,128)(2,1)}, u32[]{:S(2)}) copy-start(bf16[2,384,768]{2,1,0:T(8,128)(2,1)} %param.26) | copy-start | bytes 3538948
